TPU v7x, 32 devices: a whole 2x2x4 slice. The times are simulated.
32 devices in a mesh: dp: 4 (over z), ctx: 8 (over y, x, core).
Axes of the slice: x: 2, y: 2, z: 4, core: 2. Of those that a mesh axis runs over, the one named last changes fastest.
Arguments:
- tokens: bfloat16 [16, 2048, 1024], P('dp', 'ctx'), may hold values from -6 to 6
- segments: int32 [16, 2048], P('dp', 'ctx'), may hold values from -1 to 31, as said below
- cotangent: bfloat16 [16, 2048, 1024], P('dp', 'ctx'), may hold values from -6 to 6
- w_query: float32 [1024, 1024], P(('dp', 'ctx')), may hold values from -0.1875 to 0.1875
- w_key: float32 [1024, 1024], P(('dp', 'ctx')), may hold values from -0.1875 to 0.1875
- w_value: float32 [1024, 1024], P(('dp', 'ctx')), may hold values from -0.1875 to 0.1875
- w_out: float32 [1024, 1024], P(('dp', 'ctx')), may hold values from -0.75 to 0.75
- w_up: float32 [1024, 4096], P(('dp', 'ctx')), may hold values from -0.1875 to 0.1875
- w_down: float32 [4096, 1024], P(('dp', 'ctx')), may hold values from -0.09375 to 0.09375
- b_query: float32 [1024], P(('dp', 'ctx')), may hold values from -3 to 3
- b_value: float32 [1024], P(('dp', 'ctx')), may hold values from -3 to 3
- b_out: float32 [1024], P(('dp', 'ctx')), may hold values from -3 to 3
- b_up: float32 [4096], P(('dp', 'ctx')), may hold values from -3 to 3
- b_down: float32 [1024], P(('dp', 'ctx')), may hold values from -3 to 3
- gain_attn: float32 [1024], P(('dp', 'ctx')), may hold values from 0.5 to 1.5
- shift_attn: float32 [1024], P(('dp', 'ctx')), may hold values from -3 to 3
- gain_mlp: float32 [1024], P(('dp', 'ctx')), may hold values from 0.5 to 1.5
- shift_mlp: float32 [1024], P(('dp', 'ctx')), may hold values from -3 to 3
Outputs:
- output: bfloat16 [16, 2048, 1024], P('dp', 'ctx')
- grad_tokens: bfloat16 [16, 2048, 1024], P('dp', 'ctx')
- grad_w_query: float32 [1024, 1024], P(('dp', 'ctx'))
- grad_w_key: float32 [1024, 1024], P(('dp', 'ctx'))
- grad_w_value: float32 [1024, 1024], P(('dp', 'ctx'))
- grad_w_out: float32 [1024, 1024], P(('dp', 'ctx'))
- grad_w_up: float32 [1024, 4096], P(('dp', 'ctx'))
- grad_w_down: float32 [4096, 1024], P(('dp', 'ctx'))
- grad_b_query: float32 [1024], P(('dp', 'ctx'))
- grad_b_value: float32 [1024], P(('dp', 'ctx'))
- grad_b_out: float32 [1024], P(('dp', 'ctx'))
- grad_b_up: float32 [4096], P(('dp', 'ctx'))
- grad_b_down: float32 [1024], P(('dp', 'ctx'))
- grad_gain_attn: float32 [1024], P(('dp', 'ctx'))
- grad_shift_attn: float32 [1024], P(('dp', 'ctx'))
- grad_gain_mlp: float32 [1024], P(('dp', 'ctx'))
- grad_shift_mlp: float32 [1024], P(('dp', 'ctx'))
Inputs may be any that keep to these rules, and one draw needn't show every extreme that they name: `segments`: within a sequence, document numbers start at 0 and never fall; pad slots, numbered -1, form a tail of at most 512 slots. Among the 4 sequences of each index of dp, one is a single document without pad slots. Number 31 and pad slots both occur in every draw.
All inputs are finite; a program needn't handle non-finite values.
Results may differ from a plain program's by a relative error of at most 0.019.
Values may be sent and summed in bfloat16 or wider, within the bound.
No kernel may reach another device: no remote copies, remote signals or barrier semaphores. Data moves between devices by JAX's collectives and lax.ppermute only.
A program may use at most 256 MiB of HBM per device.

v0:
```python
from functools import partial

import jax
import jax.numpy as jnp
from jax import lax
from jax.sharding import PartitionSpec as P

HD = 64


MASKED = -1e30
EPSILON = 1e-05
QSCALE = 0.125


def passed_along(value, axis, steps):
    count = lax.axis_size(axis)
    pairs = [(source, (source + steps) % count) for source in range(count)]
    return lax.ppermute(value, axis, pairs)


def split_heads(array):
    return array.reshape(array.shape[0], array.shape[1], array.shape[2] // HD, HD)


def merge_heads(array):
    return array.reshape(array.shape[0], array.shape[1], array.shape[2] * array.shape[3])


def to_blocks(array, block_rows):
    shaped = array.reshape(
        (array.shape[0], array.shape[1] // block_rows, block_rows) + array.shape[2:]
    )
    return jnp.moveaxis(shaped, 1, 0)


def empty_state(seq_count, block_rows, model_width):
    head_count = model_width // HD
    return (
        jnp.full((seq_count, head_count, block_rows), MASKED, jnp.float32),
        jnp.zeros((seq_count, head_count, block_rows), jnp.float32),
        jnp.zeros((seq_count, block_rows, head_count, HD), jnp.float32),
    )


def attend_block(carried, queries, seg_query, key_rows, values, seg_key):
    running_max, running_sum, weighted = carried
    scores = jnp.einsum(
        "bqhd,bkhd->bhqk",
        split_heads(queries),
        split_heads(key_rows),
        preferred_element_type=jnp.float32,
    )
    allowed = seg_query[:, None, :, None] == seg_key[:, None, None, :]
    scores = jnp.where(allowed, scores, MASKED)
    new_max = jnp.maximum(running_max, jnp.max(scores, axis=-1))
    factor = jnp.exp(running_max - new_max)
    weights = jnp.exp(scores - new_max[..., None])
    running_sum = running_sum * factor + jnp.sum(weights, axis=-1)
    mixed_part = jnp.einsum(
        "bhqk,bkhd->bqhd",
        weights.astype(jnp.bfloat16),
        split_heads(values),
        preferred_element_type=jnp.float32,
    )
    weighted = weighted * jnp.transpose(factor, (0, 2, 1))[..., None] + mixed_part
    return (new_max, running_sum, weighted)


def finish_state(carried):
    running_max, running_sum, weighted = carried
    outputs = weighted / jnp.transpose(running_sum, (0, 2, 1))[..., None]
    return (merge_heads(outputs).astype(jnp.bfloat16), running_max + jnp.log(running_sum))


def grad_block(queries, seg_query, grad_attn, log_sums, deltas, key_rows, values, seg_key):
    query_heads = split_heads(queries)
    key_heads = split_heads(key_rows)
    value_heads = split_heads(values)
    out_grad_heads = split_heads(grad_attn)
    scores = jnp.einsum(
        "bqhd,bkhd->bhqk", query_heads, key_heads, preferred_element_type=jnp.float32
    )
    allowed = seg_query[:, None, :, None] == seg_key[:, None, None, :]
    scores = jnp.where(allowed, scores, MASKED)
    soft_probs = jnp.exp(scores - log_sums[..., None])
    grad_prob = jnp.einsum(
        "bqhd,bkhd->bhqk", out_grad_heads, value_heads, preferred_element_type=jnp.float32
    )
    grad_score = (soft_probs * (grad_prob - deltas[..., None])).astype(jnp.bfloat16)
    grad_query = jnp.einsum(
        "bhqk,bkhd->bqhd", grad_score, key_heads, preferred_element_type=jnp.float32
    )
    grad_key = jnp.einsum(
        "bhqk,bqhd->bkhd", grad_score, query_heads, preferred_element_type=jnp.float32
    )
    grad_value = jnp.einsum(
        "bhqk,bqhd->bkhd",
        soft_probs.astype(jnp.bfloat16),
        out_grad_heads,
        preferred_element_type=jnp.float32,
    )
    return (merge_heads(grad_query), merge_heads(grad_key), merge_heads(grad_value))


def layer_norm(hidden, gain, shift):
    centred = hidden - jnp.mean(hidden, axis=-1, keepdims=True)
    inverse = lax.rsqrt(jnp.mean(centred * centred, axis=-1, keepdims=True) + EPSILON)
    scaled = centred * inverse
    return (scaled * gain + shift, scaled, inverse)


def norm_back(grad_in, scaled, inverse, gain):
    grad_scaled = grad_in * gain
    grad_hidden = inverse * (
        grad_scaled
        - jnp.mean(grad_scaled, axis=-1, keepdims=True)
        - scaled * jnp.mean(grad_scaled * scaled, axis=-1, keepdims=True)
    )
    return (grad_hidden, jnp.sum(grad_in * scaled, axis=0), jnp.sum(grad_in, axis=0))


def pass_back(pair):
    return (
        passed_along(pair[0].astype(jnp.bfloat16), "ctx", 1).astype(jnp.float32),
        passed_along(pair[1].astype(jnp.bfloat16), "ctx", 1).astype(jnp.float32),
    )


def local(
    tokens,
    segments,
    cotangent,
    w_query,
    w_key,
    w_value,
    w_out,
    w_up,
    w_down,
    b_query,
    b_value,
    b_out,
    b_up,
    b_down,
    gain_attn,
    shift_attn,
    gain_mlp,
    shift_mlp,
):
    seq_count, span_rows, model_width = tokens.shape
    wire_parts = tuple(
        (
            master.astype(jnp.bfloat16)
            for master in (
                w_query,
                w_key,
                w_value,
                w_out,
                w_up,
                w_down,
                b_query,
                b_value,
                b_out,
                b_up,
                b_down,
                gain_attn,
                shift_attn,
                gain_mlp,
                shift_mlp,
            )
        )
    )
    (
        full_query,
        full_key,
        full_value,
        full_out,
        full_up,
        full_down,
        bias_query,
        bias_value,
        bias_out,
        bias_up,
        bias_down,
        gain_one,
        shift_one,
        gain_two,
        shift_two,
    ) = (
        lax.all_gather(wire_parts[0], ("dp", "ctx"), axis=0, tiled=True),
        lax.all_gather(wire_parts[1], ("dp", "ctx"), axis=0, tiled=True),
        lax.all_gather(wire_parts[2], ("dp", "ctx"), axis=0, tiled=True),
        lax.all_gather(wire_parts[3], ("dp", "ctx"), axis=0, tiled=True),
        lax.all_gather(wire_parts[4], ("dp", "ctx"), axis=0, tiled=True),
        lax.all_gather(wire_parts[5], ("dp", "ctx"), axis=0, tiled=True),
        lax.all_gather(wire_parts[6], ("dp", "ctx"), axis=0, tiled=True),
        lax.all_gather(wire_parts[7], ("dp", "ctx"), axis=0, tiled=True),
        lax.all_gather(wire_parts[8], ("dp", "ctx"), axis=0, tiled=True),
        lax.all_gather(wire_parts[9], ("dp", "ctx"), axis=0, tiled=True),
        lax.all_gather(wire_parts[10], ("dp", "ctx"), axis=0, tiled=True),
        lax.all_gather(wire_parts[11], ("dp", "ctx"), axis=0, tiled=True),
        lax.all_gather(wire_parts[12], ("dp", "ctx"), axis=0, tiled=True),
        lax.all_gather(wire_parts[13], ("dp", "ctx"), axis=0, tiled=True),
        lax.all_gather(wire_parts[14], ("dp", "ctx"), axis=0, tiled=True),
    )
    inputs = tokens.reshape(-1, model_width)
    shape_seq = (seq_count, span_rows, model_width)
    queries = (
        ((jnp.dot(inputs, full_query, preferred_element_type=jnp.float32) + bias_query) * QSCALE)
        .astype(jnp.bfloat16)
        .reshape(shape_seq)
    )
    key_rows = (
        jnp.dot(inputs, full_key, preferred_element_type=jnp.float32)
        .astype(jnp.bfloat16)
        .reshape(shape_seq)
    )
    values = (
        (jnp.dot(inputs, full_value, preferred_element_type=jnp.float32) + bias_value)
        .astype(jnp.bfloat16)
        .reshape(shape_seq)
    )
    seg_wire = segments.astype(jnp.bfloat16)

    def inner_step(carry_in, one_block):
        return (
            attend_block(carry_in, queries, seg_wire, one_block[0], one_block[1], one_block[2]),
            None,
        )

    stacked = (
        to_blocks(lax.all_gather(key_rows, "ctx", axis=1, tiled=True), span_rows),
        to_blocks(lax.all_gather(values, "ctx", axis=1, tiled=True), span_rows),
        to_blocks(lax.all_gather(seg_wire, "ctx", axis=1, tiled=True), span_rows),
    )
    result, unused = lax.scan(inner_step, empty_state(seq_count, span_rows, model_width), stacked)
    carried = result
    attn_out, log_sums = finish_state(carried)
    attn_flat = attn_out.reshape(-1, model_width)
    mixed_attn = jnp.dot(attn_flat, full_out, preferred_element_type=jnp.float32) + bias_out
    normed_one, scaled_one, inverse_one = layer_norm(
        inputs.astype(jnp.float32) + mixed_attn, gain_one, shift_one
    )
    hidden_in = normed_one.astype(jnp.bfloat16)
    pre_act = jnp.dot(hidden_in, full_up, preferred_element_type=jnp.float32) + bias_up
    activated = jax.nn.gelu(pre_act, approximate=False).astype(jnp.bfloat16)
    branch_two = jnp.dot(activated, full_down, preferred_element_type=jnp.float32) + bias_down
    result_out, scaled_two, inverse_two = layer_norm(normed_one + branch_two, gain_two, shift_two)
    back_query, back_key, back_value, back_out, back_up, back_down, back_gain_one, back_gain_two = (
        lax.all_gather(wire_parts[0], ("dp", "ctx"), axis=0, tiled=True),
        lax.all_gather(wire_parts[1], ("dp", "ctx"), axis=0, tiled=True),
        lax.all_gather(wire_parts[2], ("dp", "ctx"), axis=0, tiled=True),
        lax.all_gather(wire_parts[3], ("dp", "ctx"), axis=0, tiled=True),
        lax.all_gather(wire_parts[4], ("dp", "ctx"), axis=0, tiled=True),
        lax.all_gather(wire_parts[5], ("dp", "ctx"), axis=0, tiled=True),
        lax.all_gather(wire_parts[11], ("dp", "ctx"), axis=0, tiled=True),
        lax.all_gather(wire_parts[13], ("dp", "ctx"), axis=0, tiled=True),
    )
    grad_out = cotangent.reshape(-1, model_width).astype(jnp.float32)
    grad_second, grad_gain_two, grad_shift_two = norm_back(
        grad_out, scaled_two, inverse_two, back_gain_two
    )
    grad_branch = grad_second.astype(jnp.bfloat16)
    grad_bias_down = jnp.sum(grad_branch.astype(jnp.float32), axis=0)
    grad_down = jnp.dot(activated.T, grad_branch, preferred_element_type=jnp.float32)
    grad_act = jnp.dot(grad_branch, back_down.T, preferred_element_type=jnp.float32)
    unused_value, gelu_pull = jax.vjp(partial(jax.nn.gelu, approximate=False), pre_act)
    grad_pre = gelu_pull(grad_act)[0].astype(jnp.bfloat16)
    grad_bias_up = jnp.sum(grad_pre.astype(jnp.float32), axis=0)
    grad_up = jnp.dot(hidden_in.T, grad_pre, preferred_element_type=jnp.float32)
    grad_normed = grad_second + jnp.dot(grad_pre, back_up.T, preferred_element_type=jnp.float32)
    grad_first, grad_gain_one, grad_shift_one = norm_back(
        grad_normed, scaled_one, inverse_one, back_gain_one
    )
    grad_mix = grad_first.astype(jnp.bfloat16)
    grad_bias_out = jnp.sum(grad_mix.astype(jnp.float32), axis=0)
    grad_wout = jnp.dot(attn_flat.T, grad_mix, preferred_element_type=jnp.float32)
    grad_attn_out = (
        jnp.dot(grad_mix, back_out.T, preferred_element_type=jnp.float32)
        .astype(jnp.bfloat16)
        .reshape(shape_seq)
    )
    deltas = jnp.einsum(
        "bqhd,bqhd->bhq",
        split_heads(grad_attn_out),
        split_heads(attn_out),
        preferred_element_type=jnp.float32,
    )

    def cycle_step(cycle_index, carried):
        key_now, value_now, seg_now, dkey_now, dvalue_now, dquery_now = carried
        dquery_part, dkey_part, dvalue_part = grad_block(
            queries, seg_wire, grad_attn_out, log_sums, deltas, key_now, value_now, seg_now
        )
        key_now, value_now, seg_now = passed_along((key_now, value_now, seg_now), "ctx", 1)
        dkey_now, dvalue_now = pass_back((dkey_now + dkey_part, dvalue_now + dvalue_part))
        return (key_now, value_now, seg_now, dkey_now, dvalue_now, dquery_now + dquery_part)

    zero_grad = jnp.zeros(shape_seq, jnp.float32)
    key_now, value_now, seg_now, dkey_now, dvalue_now, dquery_now = lax.fori_loop(
        0,
        lax.axis_size("ctx") - 1,
        cycle_step,
        (key_rows, values, seg_wire, zero_grad, zero_grad, zero_grad),
    )
    dquery_part, dkey_part, dvalue_part = grad_block(
        queries, seg_wire, grad_attn_out, log_sums, deltas, key_now, value_now, seg_now
    )
    dkey_total, dvalue_total = pass_back((dkey_now + dkey_part, dvalue_now + dvalue_part))
    grad_query = (dquery_now + dquery_part).astype(jnp.bfloat16)
    grad_key = dkey_total.astype(jnp.bfloat16)
    grad_value = dvalue_total.astype(jnp.bfloat16)
    grad_query = grad_query.reshape(-1, model_width)
    grad_key = grad_key.reshape(-1, model_width)
    grad_value = grad_value.reshape(-1, model_width)
    grad_wquery = jnp.dot(inputs.T, grad_query, preferred_element_type=jnp.float32) * QSCALE
    grad_bias_query = jnp.sum(grad_query.astype(jnp.float32), axis=0) * QSCALE
    grad_wkey = jnp.dot(inputs.T, grad_key, preferred_element_type=jnp.float32)
    grad_wvalue = jnp.dot(inputs.T, grad_value, preferred_element_type=jnp.float32)
    grad_bias_value = jnp.sum(grad_value.astype(jnp.float32), axis=0)
    grad_input = (
        grad_first
        + QSCALE * jnp.dot(grad_query, back_query.T, preferred_element_type=jnp.float32)
        + jnp.dot(grad_key, back_key.T, preferred_element_type=jnp.float32)
        + jnp.dot(grad_value, back_value.T, preferred_element_type=jnp.float32)
    )
    shards = (
        lax.psum_scatter(grad_wquery, ("dp", "ctx"), scatter_dimension=0, tiled=True),
        lax.psum_scatter(grad_wkey, ("dp", "ctx"), scatter_dimension=0, tiled=True),
        lax.psum_scatter(grad_wvalue, ("dp", "ctx"), scatter_dimension=0, tiled=True),
        lax.psum_scatter(grad_wout, ("dp", "ctx"), scatter_dimension=0, tiled=True),
        lax.psum_scatter(grad_up, ("dp", "ctx"), scatter_dimension=0, tiled=True),
        lax.psum_scatter(grad_down, ("dp", "ctx"), scatter_dimension=0, tiled=True),
        lax.psum_scatter(grad_bias_query, ("dp", "ctx"), scatter_dimension=0, tiled=True),
        lax.psum_scatter(grad_bias_value, ("dp", "ctx"), scatter_dimension=0, tiled=True),
        lax.psum_scatter(grad_bias_out, ("dp", "ctx"), scatter_dimension=0, tiled=True),
        lax.psum_scatter(grad_bias_up, ("dp", "ctx"), scatter_dimension=0, tiled=True),
        lax.psum_scatter(grad_bias_down, ("dp", "ctx"), scatter_dimension=0, tiled=True),
        lax.psum_scatter(grad_gain_one, ("dp", "ctx"), scatter_dimension=0, tiled=True),
        lax.psum_scatter(grad_shift_one, ("dp", "ctx"), scatter_dimension=0, tiled=True),
        lax.psum_scatter(grad_gain_two, ("dp", "ctx"), scatter_dimension=0, tiled=True),
        lax.psum_scatter(grad_shift_two, ("dp", "ctx"), scatter_dimension=0, tiled=True),
    )
    return (
        result_out.astype(jnp.bfloat16).reshape(shape_seq),
        grad_input.astype(jnp.bfloat16).reshape(shape_seq),
        shards[0],
        shards[1],
        shards[2],
        shards[3],
        shards[4],
        shards[5],
        shards[6],
        shards[7],
        shards[8],
        shards[9],
        shards[10],
        shards[11],
        shards[12],
        shards[13],
        shards[14],
    )


def solution(mesh):
    in_specs = (
        P("dp", "ctx", None),
        P("dp", "ctx"),
        P("dp", "ctx", None),
        P(("dp", "ctx"), None),
        P(("dp", "ctx"), None),
        P(("dp", "ctx"), None),
        P(("dp", "ctx"), None),
        P(("dp", "ctx"), None),
        P(("dp", "ctx"), None),
        P(("dp", "ctx")),
        P(("dp", "ctx")),
        P(("dp", "ctx")),
        P(("dp", "ctx")),
        P(("dp", "ctx")),
        P(("dp", "ctx")),
        P(("dp", "ctx")),
        P(("dp", "ctx")),
        P(("dp", "ctx")),
    )
    out_specs = (
        P("dp", "ctx", None),
        P("dp", "ctx", None),
        P(("dp", "ctx"), None),
        P(("dp", "ctx"), None),
        P(("dp", "ctx"), None),
        P(("dp", "ctx"), None),
        P(("dp", "ctx"), None),
        P(("dp", "ctx"), None),
        P(("dp", "ctx")),
        P(("dp", "ctx")),
        P(("dp", "ctx")),
        P(("dp", "ctx")),
        P(("dp", "ctx")),
        P(("dp", "ctx")),
        P(("dp", "ctx")),
        P(("dp", "ctx")),
        P(("dp", "ctx")),
    )
    return jax.shard_map(local, mesh=mesh, in_specs=in_specs, out_specs=out_specs, check_vma=False)
```

profile of v0, /device:TPU:14, one launch (start us, length us, event | category | flops | bytes accessed | tf_op | source)
XLA Modules:
  0.0 2725.5 jit_solution(12828375347701291533)
XLA Ops:
  19.0 40.7 %all-reduce.18 = (bf16[1024]{0:T(1024)(128)(2,1)S(1)}, bf16[1024]{0:T(1024)(128)(2,1)S(1)}, bf16[1024]{0:T(1024)(128)(2,1)S(1)}, bf16[1024]{0:T(1024)(128)(2,1)S...) all-reduce(bf16[1024]{0:T(1024)(128)(2,1)S(1)} %dynamic-update-slic, ...), channel_id=1, replica_groups=mesh['dp'=4,'ctx'=8] {'dp','ctx'}, use_global_device_ids=true, to_apply=%add.2 | all-reduce | flops 8192 | bytes 32768
  73.6 52.8 %all-gather.10.cloned.1.call-done = bf16[1024,1024]{1,0:T(8,128)(2,1)} async-done(((bf16[32,1024]{1,0:T(8,128)(2,1)}), bf16[1024,1024]{1,0:T(8,128)(2,1)}) %all-gather.10.cloned.1.call-update) | async-done | bytes 2097168 | tf_op jit(solution)/shard_map/all_gather | solution.py:191
  145.8 29.1 %all-gather = bf16[32,1,128]{2,1,0:T(2,128)(2,1)S(1)} all-gather(bf16[1,1,128]{2,1,0:T(2,128)(2,1)S(1)} %convert_bitcast_fusion), channel_id=1, replica_groups=mesh['dp'=4,'ctx'=8] {'dp','ctx'}, dimensions={0}, use_global_device_ids=true | all-gather | bytes 8448 | tf_op jit(solution)/shard_map/all_gather | solution.py:199
  210.3 66.0 %all-gather.18.cloned.1.call-done = bf16[4,2048,1024]{2,1,0:T(8,128)(2,1)} async-done(((bf16[4,256,1024]{2,1,0:T(8,128)(2,1)}), bf16[4,2048,1024]{2,1,0:T(8,128)(2,1)}) %all-gather.18.cloned.1.call-update) | async-done | bytes 16777232 | tf_op jit(solution)/shard_map/all_gather | solution.py:233
  276.4 92.2 %all-gather.12.cloned.1.call-done = bf16[4,2048,1024]{2,1,0:T(8,128)(2,1)} async-done(((bf16[4,256,1024]{2,1,0:T(8,128)(2,1)}), bf16[4,2048,1024]{2,1,0:T(8,128)(2,1)}) %all-gather.12.cloned.1.call-update) | async-done | bytes 16777232 | tf_op jit(solution)/shard_map/all_gather | solution.py:232
  368.6 344.1 %while.38 = (s32[]{:T(128)}, f32[4,16,256]{2,1,0:T(8,128)S(1)}, f32[4,16,256]{2,1,0:T(8,128)S(1)}, f32[4,256,16,64]{1,3,2,0:T(8,128)}, bf16[4,256]{1,0:T(4,128)(...) while((s32[]{:T(128)}, f32[4,16,256]{2,1,0:T(8,128)S(1)}, ...), condition=%wide.wide.region_3.4_spmd.clone, body=%wide.wide.region_0.3_spmd.clone.sunk | while | flops 1110802432 | bytes 83894408 | solution.py:236
  726.3 50.7 %multiply_convert_fusion.2 = (bf16[1024,4096]{1,0:T(8,128)(2,1)}, f32[1024,4096]{1,0:T(8,128)}, f32[1024,4096]{1,0:T(8,128)}) fusion(f32[4096]{0:T(1024)S(1)} %bitcast.258, bf16[1024,4096]{1,0:T(8,128)(2,1)} %all-gather.22.cloned.1.call-done, f32[1024,1024]{1,0:T(8,128)} %copy-done.16, f32[1024]{0:T(1024)S(1)} %copy-done.55, f32[1024]{0:T(1024)S(1)} %copy-done.45, ...), kind=kOutput, calls=%fused_computation.49 | convolution fusion | flops 8872001536 | bytes 54558720 | tf_op jit(solution)/shard_map/dot_general | solution.py:245
  800.6 24.8 convert_reduce_fusion
  825.4 17.4 multiply_reduce_fusion.1
  864.0 862.0 %while.39 = (s32[]{:T(128)}, bf16[4,256,1024]{1,2,0:T(8,128)(2,1)}, bf16[4,256,1024]{1,2,0:T(8,128)(2,1)}, bf16[4,256]{1,0:T(4,128)(2,1)S(1)}, f32[4,256,1024]{1...) while((s32[]{:T(128)}, bf16[4,256,1024]{1,2,0:T(8,128)(2,1)}, ...), condition=%wide.wide.region_13.14_spmd.clone, body=%wide.wide.region_12.13_spmd.clone.sunk | while | flops 2728656896 | bytes 351224352 | solution.py:300
  922.7 18.4 collective-permute-done.4
  945.0 41.0 %collective-permute-done.2 = bf16[4,256]{1,0:T(4,128)(2,1)S(1)} collective-permute-done((bf16[4,256]{1,0:T(4,128)(2,1)S(1)}, bf16[4,256]{1,0:T(4,128)(2,1)S(1)}, u32[]{:S(2)}, u32[]{:S(2)}) %collective-permute-start.2) | collective-permute-done | bytes 2080 | tf_op jit(solution)/shard_map/while/body/eval_jaxpr/ppermute | solution.py:19
  1046.0 18.4 collective-permute-done.4
  1068.3 41.0 %collective-permute-done.2 = bf16[4,256]{1,0:T(4,128)(2,1)S(1)} collective-permute-done((bf16[4,256]{1,0:T(4,128)(2,1)S(1)}, bf16[4,256]{1,0:T(4,128)(2,1)S(1)}, u32[]{:S(2)}, u32[]{:S(2)}) %collective-permute-start.2) | collective-permute-done | bytes 2080 | tf_op jit(solution)/shard_map/while/body/eval_jaxpr/ppermute | solution.py:19
  1169.2 18.4 collective-permute-done.4
  1191.6 41.0 %collective-permute-done.2 = bf16[4,256]{1,0:T(4,128)(2,1)S(1)} collective-permute-done((bf16[4,256]{1,0:T(4,128)(2,1)S(1)}, bf16[4,256]{1,0:T(4,128)(2,1)S(1)}, u32[]{:S(2)}, u32[]{:S(2)}) %collective-permute-start.2) | collective-permute-done | bytes 2080 | tf_op jit(solution)/shard_map/while/body/eval_jaxpr/ppermute | solution.py:19
  1292.5 18.4 collective-permute-done.4
  1314.8 41.0 %collective-permute-done.2 = bf16[4,256]{1,0:T(4,128)(2,1)S(1)} collective-permute-done((bf16[4,256]{1,0:T(4,128)(2,1)S(1)}, bf16[4,256]{1,0:T(4,128)(2,1)S(1)}, u32[]{:S(2)}, u32[]{:S(2)}) %collective-permute-start.2) | collective-permute-done | bytes 2080 | tf_op jit(solution)/shard_map/while/body/eval_jaxpr/ppermute | solution.py:19
  1415.8 18.4 collective-permute-done.4
  1438.1 41.0 %collective-permute-done.2 = bf16[4,256]{1,0:T(4,128)(2,1)S(1)} collective-permute-done((bf16[4,256]{1,0:T(4,128)(2,1)S(1)}, bf16[4,256]{1,0:T(4,128)(2,1)S(1)}, u32[]{:S(2)}, u32[]{:S(2)}) %collective-permute-start.2) | collective-permute-done | bytes 2080 | tf_op jit(solution)/shard_map/while/body/eval_jaxpr/ppermute | solution.py:19
  1539.0 18.4 collective-permute-done.4
  1561.4 41.0 %collective-permute-done.2 = bf16[4,256]{1,0:T(4,128)(2,1)S(1)} collective-permute-done((bf16[4,256]{1,0:T(4,128)(2,1)S(1)}, bf16[4,256]{1,0:T(4,128)(2,1)S(1)}, u32[]{:S(2)}, u32[]{:S(2)}) %collective-permute-start.2) | collective-permute-done | bytes 2080 | tf_op jit(solution)/shard_map/while/body/eval_jaxpr/ppermute | solution.py:19
  1662.3 18.4 collective-permute-done.4
  1684.6 41.0 %collective-permute-done.2 = bf16[4,256]{1,0:T(4,128)(2,1)S(1)} collective-permute-done((bf16[4,256]{1,0:T(4,128)(2,1)S(1)}, bf16[4,256]{1,0:T(4,128)(2,1)S(1)}, u32[]{:S(2)}, u32[]{:S(2)}) %collective-permute-start.2) | collective-permute-done | bytes 2080 | tf_op jit(solution)/shard_map/while/body/eval_jaxpr/ppermute | solution.py:19
  1801.1 37.1 %collective-permute-done.6 = bf16[4,256,1024]{1,2,0:T(8,128)(2,1)S(1)} collective-permute-done((bf16[4,256,1024]{1,2,0:T(8,128)(2,1)S(1)}, bf16[4,256,1024]{1,2,0:T(8,128)(2,1)S(1)}, u32[]{:S(2)}, u32[]{:S(2)}) %collective-permute-start.6) | collective-permute-done | bytes 2097184 | tf_op jit(solution)/shard_map/ppermute | solution.py:19
  1861.7 34.1 %collective-permute-done.5 = bf16[4,256,1024]{1,2,0:T(8,128)(2,1)S(1)} collective-permute-done((bf16[4,256,1024]{1,2,0:T(8,128)(2,1)S(1)}, bf16[4,256,1024]{1,2,0:T(8,128)(2,1)S(1)}, u32[]{:S(2)}, u32[]{:S(2)}) %collective-permute-start.5) | collective-permute-done | bytes 2097184 | tf_op jit(solution)/shard_map/ppermute | solution.py:19
  1948.4 46.2 %all-reduce.17 = (f32[1024]{0:T(1024)S(1)}, f32[1024]{0:T(1024)S(1)}, f32[1024]{0:T(1024)S(1)}, f32[4096]{0:T(1024)S(1)}, f32[1024]{0:T(1024)S(1)}, /*index=5*/f...) all-reduce(f32[1024]{0:T(1024)S(1)} %broadcast_multiply_fusion, ...), channel_id=8, replica_groups=mesh['dp'=4,'ctx'=8] {'dp','ctx'}, use_global_device_ids=true, to_apply=%region_21.22.clone | all-reduce | flops 12288 | bytes 98304
  2014.7 20.9 reduce-scatter.13.cloned.1.call-done
  2035.6 139.9 %reduce-scatter.23.cloned.1.call-done = f32[32,1024]{1,0:T(8,128)} async-done(((f32[1024,1024]{1,0:T(8,128)}), f32[32,1024]{1,0:T(8,128)}) %reduce-scatter.23.cloned.1.call-update) | async-done | bytes 131088
  2175.5 139.5 %reduce-scatter.21.cloned.1.call-done = f32[32,1024]{1,0:T(8,128)} async-done(((f32[1024,1024]{1,0:T(8,128)}), f32[32,1024]{1,0:T(8,128)}) %reduce-scatter.21.cloned.1.call-update) | async-done | bytes 131088
  2314.9 216.6 %reduce-scatter.15.cloned.1.call-done = f32[32,4096]{1,0:T(8,128)} async-done(((f32[1024,4096]{1,0:T(8,128)}), f32[32,4096]{1,0:T(8,128)}) %reduce-scatter.15.cloned.1.call-update) | async-done | bytes 524304 | tf_op jit(solution)/shard_map/reduce_scatter | solution.py:332
  2531.5 187.2 %reduce-scatter.17.cloned.1.call-done = f32[128,1024]{1,0:T(8,128)} async-done(((f32[4096,1024]{1,0:T(8,128)}), f32[128,1024]{1,0:T(8,128)}) %reduce-scatter.17.cloned.1.call-update) | async-done | bytes 524304 | tf_op jit(solution)/shard_map/reduce_scatter | solution.py:333
  (625 shorter events, 1096.9 us)
Async XLA Ops:
  8.8 117.6 %all-gather.10.cloned.1.call-start = ((), (), s32[]{:S(2)}) async-start(), calls=%async_computation.6 | async-start | bytes 2162688 | tf_op jit(solution)/shard_map/all_gather | solution.py:191
  10.4 174.8 %all-gather.14.cloned.1.call-start = ((), (), s32[]{:S(2)}) async-start(), calls=%async_computation.8 | async-start | bytes 2162688 | tf_op jit(solution)/shard_map/all_gather | solution.py:190
  12.0 264.3 %all-gather.18.cloned.1.call-start = ((), (), s32[]{:S(2)}) async-start(), calls=%async_computation.10 | async-start | bytes 18874368 | tf_op jit(solution)/shard_map/all_gather | solution.py:233
  73.6 295.0 %all-gather.12.cloned.1.call-start = ((), (), s32[]{:S(2)}) async-start(), calls=%async_computation.7 | async-start | bytes 18874368 | tf_op jit(solution)/shard_map/all_gather | solution.py:232
  132.3 585.5 %all-gather.20.cloned.1.call-start = ((), (), s32[]{:S(2)}) async-start(), calls=%async_computation.11 | async-start | bytes 2162688 | tf_op jit(solution)/shard_map/all_gather | solution.py:193
  133.0 593.2 %all-gather.22.cloned.1.call-start = ((), (), s32[]{:S(2)}) async-start(), calls=%async_computation.12 | async-start | bytes 8650752 | tf_op jit(solution)/shard_map/all_gather | solution.py:194
  133.9 643.2 %all-gather.24.cloned.1.call-start = ((), (), s32[]{:S(2)}) async-start(), calls=%async_computation.13 | async-start | bytes 8650752 | tf_op jit(solution)/shard_map/all_gather | solution.py:195
  134.7 1880.0 %reduce-scatter.19.cloned.1.call-start = ((), (), s32[]{:S(2)}) async-start(), calls=%async_computation.17 | async-start | bytes 4325376
  905.4 80.7 %collective-permute-start = (bf16[4,256,1024]{1,2,0:T(8,128)(2,1)S(1)}, bf16[4,256,1024]{1,2,0:T(8,128)(2,1)}, u32[]{:S(2)}, u32[]{:S(2)}) collective-permute-start(bf16[4,256,1024]{1,2,0:T(8,128)(2,1)S(1)} %copy.197), channel_id=1, source_target_pairs={{0,1},{1,2},{2,3},{3,4},{4,5},{5,6},{6,7},{7,0},{8,9},{9,10},{10,1... | collective-permute-start | bytes 6291464 | tf_op jit(solution)/shard_map/while/body/eval_jaxpr/ppermute | solution.py:19
  905.7 80.4 %collective-permute-start.1 = (bf16[4,256,1024]{1,2,0:T(8,128)(2,1)}, bf16[4,256,1024]{1,2,0:T(8,128)(2,1)}, u32[]{:S(2)}, u32[]{:S(2)}) collective-permute-start(bf16[4,256,1024]{1,2,0:T(8,128)(2,1)} %copy.198), channel_id=1, source_target_pairs={{0,1},{1,2},{2,3},{3,4},{4,5},{5,6},{6,7},{7,0},{8,9},{9,10},{10,1... | collective-permute-start | bytes 6291464 | tf_op jit(solution)/shard_map/while/body/eval_jaxpr/ppermute | solution.py:19
  907.1 79.0 %collective-permute-start.2 = (bf16[4,256]{1,0:T(4,128)(2,1)S(1)}, bf16[4,256]{1,0:T(4,128)(2,1)S(1)}, u32[]{:S(2)}, u32[]{:S(2)}) collective-permute-start(bf16[4,256]{1,0:T(4,128)(2,1)S(1)} %copy.199), channel_id=1, source_target_pairs={{0,1},{1,2},{2,3},{3,4},{4,5},{5,6},{6,7},{7,0},{8,9},{9,10},{10,1... | collective-permute-start | bytes 6152 | tf_op jit(solution)/shard_map/while/body/eval_jaxpr/ppermute | solution.py:19
  1029.4 79.9 %collective-permute-start = (bf16[4,256,1024]{1,2,0:T(8,128)(2,1)S(1)}, bf16[4,256,1024]{1,2,0:T(8,128)(2,1)}, u32[]{:S(2)}, u32[]{:S(2)}) collective-permute-start(bf16[4,256,1024]{1,2,0:T(8,128)(2,1)S(1)} %copy.197), channel_id=1, source_target_pairs={{0,1},{1,2},{2,3},{3,4},{4,5},{5,6},{6,7},{7,0},{8,9},{9,10},{10,1... | collective-permute-start | bytes 6291464 | tf_op jit(solution)/shard_map/while/body/eval_jaxpr/ppermute | solution.py:19
  1029.7 79.6 %collective-permute-start.1 = (bf16[4,256,1024]{1,2,0:T(8,128)(2,1)}, bf16[4,256,1024]{1,2,0:T(8,128)(2,1)}, u32[]{:S(2)}, u32[]{:S(2)}) collective-permute-start(bf16[4,256,1024]{1,2,0:T(8,128)(2,1)} %copy.198), channel_id=1, source_target_pairs={{0,1},{1,2},{2,3},{3,4},{4,5},{5,6},{6,7},{7,0},{8,9},{9,10},{10,1... | collective-permute-start | bytes 6291464 | tf_op jit(solution)/shard_map/while/body/eval_jaxpr/ppermute | solution.py:19
  1030.1 79.2 %collective-permute-start.2 = (bf16[4,256]{1,0:T(4,128)(2,1)S(1)}, bf16[4,256]{1,0:T(4,128)(2,1)S(1)}, u32[]{:S(2)}, u32[]{:S(2)}) collective-permute-start(bf16[4,256]{1,0:T(4,128)(2,1)S(1)} %copy.199), channel_id=1, source_target_pairs={{0,1},{1,2},{2,3},{3,4},{4,5},{5,6},{6,7},{7,0},{8,9},{9,10},{10,1... | collective-permute-start | bytes 6152 | tf_op jit(solution)/shard_map/while/body/eval_jaxpr/ppermute | solution.py:19
  1153.5 79.0 %collective-permute-start = (bf16[4,256,1024]{1,2,0:T(8,128)(2,1)S(1)}, bf16[4,256,1024]{1,2,0:T(8,128)(2,1)}, u32[]{:S(2)}, u32[]{:S(2)}) collective-permute-start(bf16[4,256,1024]{1,2,0:T(8,128)(2,1)S(1)} %copy.197), channel_id=1, source_target_pairs={{0,1},{1,2},{2,3},{3,4},{4,5},{5,6},{6,7},{7,0},{8,9},{9,10},{10,1... | collective-permute-start | bytes 6291464 | tf_op jit(solution)/shard_map/while/body/eval_jaxpr/ppermute | solution.py:19
  1153.9 78.7 %collective-permute-start.1 = (bf16[4,256,1024]{1,2,0:T(8,128)(2,1)}, bf16[4,256,1024]{1,2,0:T(8,128)(2,1)}, u32[]{:S(2)}, u32[]{:S(2)}) collective-permute-start(bf16[4,256,1024]{1,2,0:T(8,128)(2,1)} %copy.198), channel_id=1, source_target_pairs={{0,1},{1,2},{2,3},{3,4},{4,5},{5,6},{6,7},{7,0},{8,9},{9,10},{10,1... | collective-permute-start | bytes 6291464 | tf_op jit(solution)/shard_map/while/body/eval_jaxpr/ppermute | solution.py:19
  1153.9 78.7 %collective-permute-start.2 = (bf16[4,256]{1,0:T(4,128)(2,1)S(1)}, bf16[4,256]{1,0:T(4,128)(2,1)S(1)}, u32[]{:S(2)}, u32[]{:S(2)}) collective-permute-start(bf16[4,256]{1,0:T(4,128)(2,1)S(1)} %copy.199), channel_id=1, source_target_pairs={{0,1},{1,2},{2,3},{3,4},{4,5},{5,6},{6,7},{7,0},{8,9},{9,10},{10,1... | collective-permute-start | bytes 6152 | tf_op jit(solution)/shard_map/while/body/eval_jaxpr/ppermute | solution.py:19
  1277.7 78.1 %collective-permute-start = (bf16[4,256,1024]{1,2,0:T(8,128)(2,1)S(1)}, bf16[4,256,1024]{1,2,0:T(8,128)(2,1)}, u32[]{:S(2)}, u32[]{:S(2)}) collective-permute-start(bf16[4,256,1024]{1,2,0:T(8,128)(2,1)S(1)} %copy.197), channel_id=1, source_target_pairs={{0,1},{1,2},{2,3},{3,4},{4,5},{5,6},{6,7},{7,0},{8,9},{9,10},{10,1... | collective-permute-start | bytes 6291464 | tf_op jit(solution)/shard_map/while/body/eval_jaxpr/ppermute | solution.py:19
  1278.0 77.8 %collective-permute-start.1 = (bf16[4,256,1024]{1,2,0:T(8,128)(2,1)}, bf16[4,256,1024]{1,2,0:T(8,128)(2,1)}, u32[]{:S(2)}, u32[]{:S(2)}) collective-permute-start(bf16[4,256,1024]{1,2,0:T(8,128)(2,1)} %copy.198), channel_id=1, source_target_pairs={{0,1},{1,2},{2,3},{3,4},{4,5},{5,6},{6,7},{7,0},{8,9},{9,10},{10,1... | collective-permute-start | bytes 6291464 | tf_op jit(solution)/shard_map/while/body/eval_jaxpr/ppermute | solution.py:19
  1278.1 77.8 %collective-permute-start.2 = (bf16[4,256]{1,0:T(4,128)(2,1)S(1)}, bf16[4,256]{1,0:T(4,128)(2,1)S(1)}, u32[]{:S(2)}, u32[]{:S(2)}) collective-permute-start(bf16[4,256]{1,0:T(4,128)(2,1)S(1)} %copy.199), channel_id=1, source_target_pairs={{0,1},{1,2},{2,3},{3,4},{4,5},{5,6},{6,7},{7,0},{8,9},{9,10},{10,1... | collective-permute-start | bytes 6152 | tf_op jit(solution)/shard_map/while/body/eval_jaxpr/ppermute | solution.py:19
  1401.9 77.2 %collective-permute-start = (bf16[4,256,1024]{1,2,0:T(8,128)(2,1)S(1)}, bf16[4,256,1024]{1,2,0:T(8,128)(2,1)}, u32[]{:S(2)}, u32[]{:S(2)}) collective-permute-start(bf16[4,256,1024]{1,2,0:T(8,128)(2,1)S(1)} %copy.197), channel_id=1, source_target_pairs={{0,1},{1,2},{2,3},{3,4},{4,5},{5,6},{6,7},{7,0},{8,9},{9,10},{10,1... | collective-permute-start | bytes 6291464 | tf_op jit(solution)/shard_map/while/body/eval_jaxpr/ppermute | solution.py:19
  1402.2 76.9 %collective-permute-start.1 = (bf16[4,256,1024]{1,2,0:T(8,128)(2,1)}, bf16[4,256,1024]{1,2,0:T(8,128)(2,1)}, u32[]{:S(2)}, u32[]{:S(2)}) collective-permute-start(bf16[4,256,1024]{1,2,0:T(8,128)(2,1)} %copy.198), channel_id=1, source_target_pairs={{0,1},{1,2},{2,3},{3,4},{4,5},{5,6},{6,7},{7,0},{8,9},{9,10},{10,1... | collective-permute-start | bytes 6291464 | tf_op jit(solution)/shard_map/while/body/eval_jaxpr/ppermute | solution.py:19
  1402.2 76.9 %collective-permute-start.2 = (bf16[4,256]{1,0:T(4,128)(2,1)S(1)}, bf16[4,256]{1,0:T(4,128)(2,1)S(1)}, u32[]{:S(2)}, u32[]{:S(2)}) collective-permute-start(bf16[4,256]{1,0:T(4,128)(2,1)S(1)} %copy.199), channel_id=1, source_target_pairs={{0,1},{1,2},{2,3},{3,4},{4,5},{5,6},{6,7},{7,0},{8,9},{9,10},{10,1... | collective-permute-start | bytes 6152 | tf_op jit(solution)/shard_map/while/body/eval_jaxpr/ppermute | solution.py:19
  1526.1 76.3 %collective-permute-start = (bf16[4,256,1024]{1,2,0:T(8,128)(2,1)S(1)}, bf16[4,256,1024]{1,2,0:T(8,128)(2,1)}, u32[]{:S(2)}, u32[]{:S(2)}) collective-permute-start(bf16[4,256,1024]{1,2,0:T(8,128)(2,1)S(1)} %copy.197), channel_id=1, source_target_pairs={{0,1},{1,2},{2,3},{3,4},{4,5},{5,6},{6,7},{7,0},{8,9},{9,10},{10,1... | collective-permute-start | bytes 6291464 | tf_op jit(solution)/shard_map/while/body/eval_jaxpr/ppermute | solution.py:19
  1526.4 76.0 %collective-permute-start.1 = (bf16[4,256,1024]{1,2,0:T(8,128)(2,1)}, bf16[4,256,1024]{1,2,0:T(8,128)(2,1)}, u32[]{:S(2)}, u32[]{:S(2)}) collective-permute-start(bf16[4,256,1024]{1,2,0:T(8,128)(2,1)} %copy.198), channel_id=1, source_target_pairs={{0,1},{1,2},{2,3},{3,4},{4,5},{5,6},{6,7},{7,0},{8,9},{9,10},{10,1... | collective-permute-start | bytes 6291464 | tf_op jit(solution)/shard_map/while/body/eval_jaxpr/ppermute | solution.py:19
  1526.4 76.0 %collective-permute-start.2 = (bf16[4,256]{1,0:T(4,128)(2,1)S(1)}, bf16[4,256]{1,0:T(4,128)(2,1)S(1)}, u32[]{:S(2)}, u32[]{:S(2)}) collective-permute-start(bf16[4,256]{1,0:T(4,128)(2,1)S(1)} %copy.199), channel_id=1, source_target_pairs={{0,1},{1,2},{2,3},{3,4},{4,5},{5,6},{6,7},{7,0},{8,9},{9,10},{10,1... | collective-permute-start | bytes 6152 | tf_op jit(solution)/shard_map/while/body/eval_jaxpr/ppermute | solution.py:19
  1650.2 75.4 %collective-permute-start = (bf16[4,256,1024]{1,2,0:T(8,128)(2,1)S(1)}, bf16[4,256,1024]{1,2,0:T(8,128)(2,1)}, u32[]{:S(2)}, u32[]{:S(2)}) collective-permute-start(bf16[4,256,1024]{1,2,0:T(8,128)(2,1)S(1)} %copy.197), channel_id=1, source_target_pairs={{0,1},{1,2},{2,3},{3,4},{4,5},{5,6},{6,7},{7,0},{8,9},{9,10},{10,1... | collective-permute-start | bytes 6291464 | tf_op jit(solution)/shard_map/while/body/eval_jaxpr/ppermute | solution.py:19
  1779.4 256.2 %reduce-scatter.13.cloned.1.call-start = ((), (), s32[]{:S(2)}) async-start(), calls=%async_computation.14 | async-start | bytes 4325376 | tf_op jit(solution)/shard_map/reduce_scatter | solution.py:331
  1786.6 388.8 %reduce-scatter.23.cloned.1.call-start = ((), (), s32[]{:S(2)}) async-start(), calls=%async_computation.19 | async-start | bytes 4325376
  1849.3 465.6 %reduce-scatter.21.cloned.1.call-start = ((), (), s32[]{:S(2)}) async-start(), calls=%async_computation.18 | async-start | bytes 4325376
  1906.8 624.6 %reduce-scatter.15.cloned.1.call-start = ((), (), s32[]{:S(2)}) async-start(), calls=%async_computation.15 | async-start | bytes 17301504 | tf_op jit(solution)/shard_map/reduce_scatter | solution.py:332
  1924.5 794.2 %reduce-scatter.17.cloned.1.call-start = ((), (), s32[]{:S(2)}) async-start(), calls=%async_computation.16 | async-start | bytes 17301504 | tf_op jit(solution)/shard_map/reduce_scatter | solution.py:333
  (129 other events, 2103.5 us)
Sparse Core Ops, SparseCore 0:
  11.5 56.1 all-gather.15
  71.1 55.3 all-gather.9
  129.8 55.2 all-gather.13
  186.9 89.3 all-gather.17
  278.7 89.8 all-gather.11
  371.9 55.6 all-gather.19
  431.0 77.0 all-gather.21
  511.5 76.0 all-gather.23
  1779.5 116.9 reduce-scatter.18
  1899.2 136.3 reduce-scatter.12
  2038.4 136.9 reduce-scatter.22
  2178.2 136.7 reduce-scatter.20
  2317.8 213.6 reduce-scatter.14
  2534.2 184.4 reduce-scatter.16
where the time goes:
time: 2730 us
  waiting for transfers between devices  1440 us (53%)
  matrix products  632 us (23%)
  other arithmetic  264 us (10%)
  local copies, waits for them, and re-layouts  204 us (7%)
  blocking collectives  125 us (5%)
  starting transfers between devices  47.5 us (2%)
    ppermute x37, waiting for transfers between devices, passed_along(): return lax.ppermute(value, axis, pairs)  506 us
    unnamed x17, waiting for transfers between devices  280 us
    reduce_scatter x1, waiting for transfers between devices, local(): lax.psum_scatter(grad_up, ('dp', 'ctx'), scatter_dimension=0, tiled=True)  217 us
    reduce_scatter x1, waiting for transfers between devices, local(): lax.psum_scatter(grad_down, ('dp', 'ctx'), scatter_dimension=0, tiled=True)  187 us
    dot_general x8, matrix products, attend_block(): jnp.einsum('bhqk,bkhd->bqhd', weights.astype(jnp.bfloat16), split_heads(v...  101 us
    all_gather x1, waiting for transfers between devices, local(): lax.all_gather(key_rows, 'ctx', axis=1, tiled=True)  92.2 us
    unnamed x2, blocking collectives  86.9 us
    dot_general x8, matrix products, attend_block(): jnp.einsum('bqhd,bkhd->bhqk', split_heads(queries), split_heads(key_rows)...  84.2 us
  transfers between devices with their start and end apart: 51, of which 32 were waited for; matrix products, arithmetic and copies ran while one was open for 27% of the time, Pallas kernels for 0%

commit v1 on v0

v1 whole, which is shorter than its diff:
```python
import functools

import jax
import jax.numpy as jnp
from jax import lax
from jax.experimental import pallas as pl
from jax.experimental.pallas import tpu as pltpu
from jax.sharding import PartitionSpec as P

HD = 64
MASKED = -1e30
EPSILON = 1e-05
QSCALE = 0.125
BF = jnp.bfloat16
F32 = jnp.float32
NT = (((1,), (1,)), ((), ()))
NN = (((1,), (0,)), ((), ()))
TN = (((0,), (0,)), ((), ()))
VMEM_LIMIT = 56 << 20
BOTH = ("dp", "ctx")


def mm(a, b, dims=NN):
    return lax.dot_general(a, b, dims, preferred_element_type=F32)


def params():
    return pltpu.CompilerParams(vmem_limit_bytes=VMEM_LIMIT)


def head_parts(block):
    lane = lax.broadcasted_iota(jnp.int32, block.shape, 1)
    zero = jnp.zeros_like(block)
    return [jnp.where(lane < HD, block, zero), jnp.where(lane < HD, zero, block)]


def attend_kernel(chunk, q_ref, k_ref, v_ref, sq_ref, sk_ref, o_ref, p_ref, l_ref, vt_ref, kn_ref):
    i = pl.program_id(1)
    total = k_ref.shape[0]
    block = q_ref.shape[0]

    @pl.when(i == 0)
    def _():
        vt_ref[...] = v_ref[...].T
        keys = k_ref[...].astype(F32)
        norms = jnp.sum((keys * keys).T.reshape(2, HD, total), axis=1)
        kn_ref[...] = jnp.sqrt(jnp.max(norms, axis=1, keepdims=True))

    q = q_ref[...]
    parts = head_parts(q)
    q32 = q.astype(F32)
    qn = jnp.sqrt(jnp.sum((q32 * q32).T.reshape(2, HD, block), axis=1))
    bound = qn * kn_ref[...]
    seg_q = sq_ref[...]
    ones = jnp.ones((16, chunk), BF)

    def scores(h, lo):
        s = mm(k_ref[lo : lo + chunk, :], parts[h], NT)
        return jnp.where(sk_ref[lo : lo + chunk, :] == seg_q, s, MASKED)

    def finish(shift):
        acc = [jnp.zeros((HD + 16, block), F32)] * 2
        for lo in range(0, total, chunk):
            for h in range(2):
                p = jnp.exp(scores(h, lo) - shift[h : h + 1]).astype(BF)
                p_ref[h, lo : lo + chunk, :] = p
                left = jnp.concatenate([vt_ref[h * HD : h * HD + HD, lo : lo + chunk], ones], axis=0)
                acc[h] = acc[h] + mm(left, p)
        sums = [acc[h][HD : HD + 1] for h in range(2)]
        out = jnp.concatenate([acc[h][:HD] / sums[h] for h in range(2)], axis=0)
        o_ref[...] = out.T.astype(BF)
        sums = jnp.concatenate(sums, axis=0)
        l_ref[...] = 1.0 / sums
        return sums

    sums = finish(bound)
    good = jnp.min(sums) > 1e-20

    @pl.when(jnp.logical_not(good))
    def _():
        most = [jnp.full((1, block), MASKED, F32)] * 2
        for lo in range(0, total, chunk):
            for h in range(2):
                most[h] = jnp.maximum(most[h], jnp.max(scores(h, lo), axis=0, keepdims=True))
        finish(jnp.concatenate(most, axis=0))


def attend(qkv, seg_row, seg_col, block=256, chunk=512):
    total = qkv.shape[1]
    pairs = qkv.shape[2] // 128
    specs = lambda c: pl.BlockSpec((None, total, 128), lambda h, i: (c, 0, h))
    return pl.pallas_call(
        functools.partial(attend_kernel, chunk),
        grid=(pairs, total // block),
        in_specs=[
            pl.BlockSpec((None, block, 128), lambda h, i: (0, i, h)),
            specs(1),
            specs(2),
            pl.BlockSpec((1, block), lambda h, i: (0, i)),
            pl.BlockSpec((total, 1), lambda h, i: (0, 0)),
        ],
        out_specs=[
            pl.BlockSpec((block, 128), lambda h, i: (i, h)),
            pl.BlockSpec((None, 2, total, block), lambda h, i: (h, 0, 0, i)),
            pl.BlockSpec((None, 2, block), lambda h, i: (h, 0, i)),
        ],
        out_shape=[
            jax.ShapeDtypeStruct((total, pairs * 128), BF),
            jax.ShapeDtypeStruct((pairs, 2, total, total), BF),
            jax.ShapeDtypeStruct((pairs, 2, total), F32),
        ],
        scratch_shapes=[pltpu.VMEM((128, total), BF), pltpu.VMEM((2, 1), F32)],
        compiler_params=params(),
        cost_estimate=pl.CostEstimate(flops=45 * 10**9, bytes_accessed=80 << 20, transcendentals=0),
        name="attend",
    )(qkv, qkv, qkv, seg_row, seg_col)


def attend_back_kernel(
    chunk, q_ref, k_ref, v_ref, o_ref, do_ref, p_ref, l_ref, dq_ref, dk_ref, dv_ref, kt_ref, dk_acc, dv_acc
):
    i = pl.program_id(1)
    total = k_ref.shape[0]
    block = q_ref.shape[0]

    @pl.when(i == 0)
    def _():
        kt_ref[...] = k_ref[...].T
        dk_acc[...] = jnp.zeros_like(dk_acc)
        dv_acc[...] = jnp.zeros_like(dv_acc)

    do = do_ref[...]
    q_parts = head_parts(q_ref[...])
    do_parts = head_parts(do)
    product = do.astype(F32) * o_ref[...].astype(F32)
    delta = jnp.sum(product.T.reshape(2, HD, block), axis=1)
    inverse = l_ref[...]
    grad_q = [jnp.zeros((HD, block), F32)] * 2
    for lo in range(0, total, chunk):
        rows = slice(lo, lo + chunk)
        values = v_ref[rows, :]
        for h in range(2):
            p = p_ref[h, rows, :].astype(F32) * inverse[h : h + 1]
            grad_p = mm(values, do_parts[h], NT)
            grad_s = (p * (grad_p - delta[h : h + 1])).astype(BF)
            dv_acc[rows, :] += mm(p.astype(BF), do_parts[h])
            dk_acc[rows, :] += mm(grad_s, q_parts[h])
            grad_q[h] = grad_q[h] + mm(kt_ref[h * HD : h * HD + HD, rows], grad_s)
    dq_ref[...] = jnp.concatenate(grad_q, axis=0).T.astype(BF)

    @pl.when(i == pl.num_programs(1) - 1)
    def _():
        dk_ref[...] = dk_acc[...].astype(BF)
        dv_ref[...] = dv_acc[...].astype(BF)


def attend_back(qkv, out, grad_out, probs, inverse, block=256, chunk=512):
    total = qkv.shape[1]
    pairs = qkv.shape[2] // 128
    whole = lambda c: pl.BlockSpec((None, total, 128), lambda h, i: (c, 0, h))
    rows = pl.BlockSpec((block, 128), lambda h, i: (i, h))
    keys = pl.BlockSpec((total, 128), lambda h, i: (0, h))
    return pl.pallas_call(
        functools.partial(attend_back_kernel, chunk),
        grid=(pairs, total // block),
        in_specs=[
            pl.BlockSpec((None, block, 128), lambda h, i: (0, i, h)),
            whole(1),
            whole(2),
            rows,
            rows,
            pl.BlockSpec((None, 2, total, block), lambda h, i: (h, 0, 0, i)),
            pl.BlockSpec((None, 2, block), lambda h, i: (h, 0, i)),
        ],
        out_specs=[rows, keys, keys],
        out_shape=[jax.ShapeDtypeStruct((total, pairs * 128), BF)] * 3,
        scratch_shapes=[
            pltpu.VMEM((128, total), BF),
            pltpu.VMEM((total, 128), F32),
            pltpu.VMEM((total, 128), F32),
        ],
        compiler_params=params(),
        cost_estimate=pl.CostEstimate(flops=85 * 10**9, bytes_accessed=80 << 20, transcendentals=0),
        name="attend_back",
    )(qkv, qkv, qkv, out, grad_out, probs, inverse)


def gelu_parts(u):
    scaled = jnp.abs(u) * 0.7071067811865476
    den = 1.0 + 0.3275911 * scaled
    t = pl.reciprocal(den, approx=True)
    t = t * (2.0 - den * t)
    e = jnp.exp(u * u * -0.5)
    poly = t * (
        0.127414796
        + t * (-0.142248368 + t * (0.7107068705 + t * (-0.7265760135 + t * 0.5307027145)))
    )
    tail = poly * e
    phi = jnp.where(u >= 0, 1.0 - tail, tail)
    return u * phi, phi + u * (e * 0.3989422804014327)


def mean(value):
    return jnp.mean(value, axis=-1, keepdims=True)


def normed(hidden):
    centred = hidden - mean(hidden)
    inverse = lax.rsqrt(mean(centred * centred) + EPSILON)
    return centred * inverse, inverse


def norm_back(grad_in, scaled, inverse, gain):
    grad_scaled = grad_in * gain
    return inverse * (grad_scaled - mean(grad_scaled) - scaled * mean(grad_scaled * scaled))


def fold(value):
    return jnp.sum(value.reshape(value.shape[0] // 8, 8, value.shape[1]), axis=0)


def add_fold(ref, first, value):
    part = fold(value)

    @pl.when(first)
    def _():
        ref[...] = part

    @pl.when(jnp.logical_not(first))
    def _():
        ref[...] += part


def mid_up_kernel(step, x_ref, o_ref, wo_ref, wu_ref, vec_ref, bu_ref, xh_ref, r_ref, xb_ref, g_ref, gp_ref):
    hidden = x_ref[...].astype(F32) + mm(o_ref[...], wo_ref[...]) + vec_ref[0:1, :]
    scaled, inverse = normed(hidden)
    xh_ref[...] = scaled
    r_ref[...] = inverse
    xb = (scaled * vec_ref[1:2, :] + vec_ref[2:3, :]).astype(BF)
    xb_ref[...] = xb
    for lo in range(0, wu_ref.shape[1], step):
        cols = slice(lo, lo + step)
        g, gp = gelu_parts(mm(xb, wu_ref[:, cols]) + bu_ref[:, cols])
        g_ref[:, cols] = g.astype(BF)
        gp_ref[:, cols] = gp.astype(BF)


def mid_up(x, o, w_out, w_up, vecs, b_up, block=256, step=512):
    rows, d = x.shape
    ff = w_up.shape[1]
    row = lambda n: pl.BlockSpec((block, n), lambda i: (i, 0))
    full = lambda a: pl.BlockSpec(a.shape, lambda i: (0, 0), pipeline_mode=pl.Buffered(1))
    return pl.pallas_call(
        functools.partial(mid_up_kernel, step),
        grid=(rows // block,),
        in_specs=[row(d), row(d), full(w_out), full(w_up), full(vecs), full(b_up)],
        out_specs=[row(d), row(1), row(d), row(ff), row(ff)],
        out_shape=[
            jax.ShapeDtypeStruct((rows, d), F32),
            jax.ShapeDtypeStruct((rows, 1), F32),
            jax.ShapeDtypeStruct((rows, d), BF),
            jax.ShapeDtypeStruct((rows, ff), BF),
            jax.ShapeDtypeStruct((rows, ff), BF),
        ],
        compiler_params=params(),
        cost_estimate=pl.CostEstimate(flops=11 * 10**9, bytes_accessed=36 << 20, transcendentals=0),
        name="mid_up",
    )(x, o, w_out, w_up, vecs, b_up)


def mid_down_kernel(
    step, g_ref, gp_ref, xh_ref, dy_ref, wd_ref, vec_ref, out_ref, dh_ref, dm_ref, du_ref, s_ref, su_ref
):
    first = pl.program_id(0) == 0
    x1 = xh_ref[...] * vec_ref[1:2, :] + vec_ref[2:3, :]
    hidden = x1 + mm(g_ref[...], wd_ref[...]) + vec_ref[3:4, :]
    scaled, inverse = normed(hidden)
    gain = vec_ref[4:5, :]
    out_ref[...] = (scaled * gain + vec_ref[5:6, :]).astype(BF)
    dy = dy_ref[...].astype(F32)
    dh = norm_back(dy, scaled, inverse, gain)
    dm = dh.astype(BF)
    dh_ref[...] = dh
    dm_ref[...] = dm
    add_fold(s_ref.at[0:8, :], first, dy * scaled)
    add_fold(s_ref.at[8:16, :], first, dy)
    add_fold(s_ref.at[16:24, :], first, dm.astype(F32))
    for lo in range(0, wd_ref.shape[0], step):
        cols = slice(lo, lo + step)
        du = (mm(dm, wd_ref[cols, :], NT) * gp_ref[:, cols].astype(F32)).astype(BF)
        du_ref[:, cols] = du
        add_fold(su_ref.at[:, cols], first, du.astype(F32))


def mid_down(g, gp, xh, dy, w_down, vecs, block=256, step=512):
    rows, d = xh.shape
    ff = g.shape[1]
    row = lambda n: pl.BlockSpec((block, n), lambda i: (i, 0))
    full = lambda a: pl.BlockSpec(a.shape, lambda i: (0, 0), pipeline_mode=pl.Buffered(1))
    keep = lambda r, n: pl.BlockSpec((r, n), lambda i: (0, 0))
    return pl.pallas_call(
        functools.partial(mid_down_kernel, step),
        grid=(rows // block,),
        in_specs=[row(ff), row(ff), row(d), row(d), full(w_down), full(vecs)],
        out_specs=[row(d), row(d), row(d), row(ff), keep(24, d), keep(8, ff)],
        out_shape=[
            jax.ShapeDtypeStruct((rows, d), BF),
            jax.ShapeDtypeStruct((rows, d), F32),
            jax.ShapeDtypeStruct((rows, d), BF),
            jax.ShapeDtypeStruct((rows, ff), BF),
            jax.ShapeDtypeStruct((24, d), F32),
            jax.ShapeDtypeStruct((8, ff), F32),
        ],
        compiler_params=params(),
        cost_estimate=pl.CostEstimate(flops=17 * 10**9, bytes_accessed=44 << 20, transcendentals=0),
        name="mid_down",
    )(g, gp, xh, dy, w_down, vecs)


def mid_back_kernel(dh_ref, du_ref, xh_ref, r_ref, wu_ref, wo_ref, vec_ref, dh1_ref, da_ref, do_ref, s_ref):
    first = pl.program_id(0) == 0
    dx = dh_ref[...] + mm(du_ref[...], wu_ref[...], NT)
    scaled = xh_ref[...]
    dh1 = norm_back(dx, scaled, r_ref[...], vec_ref[1:2, :])
    dh1_ref[...] = dh1
    da = dh1.astype(BF)
    da_ref[...] = da
    do_ref[...] = mm(da, wo_ref[...], NT).astype(BF)
    add_fold(s_ref.at[0:8, :], first, dx * scaled)
    add_fold(s_ref.at[8:16, :], first, dx)
    add_fold(s_ref.at[16:24, :], first, da.astype(F32))


def mid_back(dh, du, xh, r, w_up, w_out, vecs, block=256):
    rows, d = dh.shape
    row = lambda n: pl.BlockSpec((block, n), lambda i: (i, 0))
    full = lambda a: pl.BlockSpec(a.shape, lambda i: (0, 0), pipeline_mode=pl.Buffered(1))
    return pl.pallas_call(
        mid_back_kernel,
        grid=(rows // block,),
        in_specs=[row(d), row(du.shape[1]), row(d), row(1), full(w_up), full(w_out), full(vecs)],
        out_specs=[row(d), row(d), row(d), pl.BlockSpec((24, d), lambda i: (0, 0))],
        out_shape=[
            jax.ShapeDtypeStruct((rows, d), F32),
            jax.ShapeDtypeStruct((rows, d), BF),
            jax.ShapeDtypeStruct((rows, d), BF),
            jax.ShapeDtypeStruct((24, d), F32),
        ],
        compiler_params=params(),
        cost_estimate=pl.CostEstimate(flops=11 * 10**9, bytes_accessed=36 << 20, transcendentals=0),
        name="mid_back",
    )(dh, du, xh, r, w_up, w_out, vecs)


def swap(value, mask):
    count = lax.axis_size("ctx")
    return lax.ppermute(value, "ctx", [(d, d ^ mask) for d in range(count)])


def pick(value, index, axis=0):
    return lax.dynamic_index_in_dim(value, index, axis, keepdims=False)


def to_chip(value, chip, chips):
    return [pick(value, chip)] + [swap(pick(value, chip ^ r), 2 * r) for r in range(1, chips)]


def from_chip(pieces, chip):
    chips = len(pieces)
    back = jnp.stack([pieces[0]] + [swap(pieces[r], 2 * r) for r in range(1, chips)])
    return jnp.take(back, jnp.arange(chips) ^ chip, axis=0)


def halve(value, axis, bit, chip, last):
    own = (chip >> bit) & 1
    sent = swap(pick(value, 1 - own, axis), 2 << bit)
    total = pick(value, own, axis).astype(F32) + sent.astype(F32)
    return total.astype(BF)


def reduce_rows(grad, chip, core):
    groups, chips, _, rows, cols = grad.shape
    bits = chips.bit_length() - 1
    me = lax.axis_index("dp")
    shaped = grad.reshape((groups,) + (2,) * bits + (2, rows, cols))
    parts = []
    for part, order in ((shaped[: groups // 2], range(bits)), (shaped[groups // 2 :], range(bits - 1, -1, -1))):
        left = list(range(bits - 1, -1, -1))
        for bit in order:
            part = halve(part, 1 + left.index(bit), bit, chip, False)
            left.remove(bit)
        parts.append(part)
    both = jnp.concatenate(parts, axis=0)
    total = pick(both, me).astype(F32)
    for step in range(1, groups):
        pairs = [(s, (s + step) % groups) for s in range(groups)]
        total = total + lax.ppermute(pick(both, (me + step) % groups), "dp", pairs).astype(F32)
    total = total.astype(BF)
    mine, other = pick(total, core), swap(pick(total, 1 - core), 1)
    ordered = jnp.where(core == 0, jnp.stack([mine, other]), jnp.stack([other, mine]))
    return jnp.moveaxis(ordered, 0, 1).reshape(rows, 2 * cols).astype(F32)


def half_cols(value, which):
    width = value.shape[-1] // 2
    return lax.dynamic_slice_in_dim(value, which * width, width, value.ndim - 1)


def gather(value):
    return lax.all_gather(value, BOTH, axis=0, tiled=True)


def local(
    tokens, segments, cotangent, w_query, w_key, w_value, w_out, w_up, w_down,
    b_query, b_value, b_out, b_up, b_down, gain_attn, shift_attn, gain_mlp, shift_mlp,
):
    seqs, span, d = tokens.shape
    count = lax.axis_size("ctx")
    groups = lax.axis_size("dp")
    chips = count // 2
    me = lax.axis_index("ctx")
    chip, core = me // 2, me % 2
    ff = w_up.shape[1]
    half = d // 2
    shards = groups * count

    vec_names = (b_query, b_value, b_out, gain_attn, shift_attn, b_down, gain_mlp, shift_mlp)
    vec_pack = jnp.concatenate([v.astype(BF) for v in vec_names] + [b_up.astype(BF)]).reshape(1, -1)
    vec_all = gather(vec_pack).astype(F32)
    width = d // shards
    vec = [vec_all[:, n * width : (n + 1) * width].reshape(1, d) for n in range(8)]
    bias_query, bias_value = vec[0], vec[1]
    bias_up = vec_all[:, 8 * width :].reshape(1, ff)
    vecs = jnp.concatenate(vec[2:] + [jnp.zeros((2, d), F32)], axis=0)

    full_query, full_key, full_value = [gather(w.astype(BF)) for w in (w_query, w_key, w_value)]
    full_out, full_up, full_down = [gather(w.astype(BF)) for w in (w_out, w_up, w_down)]

    mine = jnp.concatenate(to_chip(tokens, chip, chips), axis=0)
    seg_mine = jnp.concatenate(to_chip(segments, chip, chips), axis=0)
    dy = jnp.concatenate(to_chip(cotangent, chip, chips), axis=0)
    mate = swap(mine, 1)
    seg = jnp.concatenate([seg_mine, swap(seg_mine, 1)])
    own = mine.shape[0]
    x_all = jnp.concatenate([mine, mate], axis=0)

    w_cat = jnp.stack(
        [half_cols(full_query, core) * jnp.asarray(QSCALE, BF), half_cols(full_key, core), half_cols(full_value, core)]
    )
    bias_cat = jnp.stack(
        [half_cols(bias_query, core) * QSCALE, jnp.zeros((1, half), F32), half_cols(bias_value, core)]
    )
    qkv = (jnp.einsum("td,cdn->ctn", x_all, w_cat, preferred_element_type=F32) + bias_cat).astype(BF)
    attn, probs, inverse = attend(qkv, seg.reshape(1, -1), seg.reshape(-1, 1))

    other_heads = swap(attn[own:], 1)
    heads = [attn[:own], other_heads]
    o_full = jnp.where(core == 0, jnp.concatenate(heads, axis=1), jnp.concatenate(heads[::-1], axis=1))
    xh, r, xb, g, gp = mid_up(mine, o_full, full_out, full_up, vecs, bias_up)
    out, dh2, dm, du, sums_two, sums_up = mid_down(g, gp, xh, dy, full_down, vecs)
    dh1, da, do, sums_one = mid_back(dh2, du, xh, r, full_up, full_out, vecs)
    result_out = from_chip(list(out.reshape(chips, span, d)), chip)

    do_other = swap(half_cols(do, 1 - core), 1)
    do_all = jnp.concatenate([half_cols(do, core), do_other], axis=0)

    def weight_grad(left, right, rows):
        sent = swap(mm(left, half_cols(right, 1 - core), TN).astype(BF), 1)
        whole = (mm(left, half_cols(right, core), TN) + sent.astype(F32)).astype(BF)
        return reduce_rows(whole.reshape(groups, chips, 2, rows, -1), chip, core)

    grad_down = weight_grad(g, dm, ff // shards)
    grad_up = weight_grad(xb, du, d // shards)
    grad_out = weight_grad(o_full, da, d // shards)

    grads = attend_back(qkv, attn, do_all, probs, inverse)
    grad_proj = [mm(x_all, part, TN) for part in grads]
    grad_proj[0] = grad_proj[0] * QSCALE
    rows = d // shards
    grad_query, grad_key, grad_value = [
        reduce_rows(part.astype(BF).reshape(groups, chips, 2, rows, half), chip, core) for part in grad_proj
    ]
    token_part = sum(mm(part, w_cat[n], NT) for n, part in enumerate(grads))
    grad_mine = dh1 + token_part[:own] + swap(token_part[own:].astype(BF), 1).astype(F32)
    grad_tokens = from_chip(list(grad_mine.astype(BF).reshape(chips, span, d)), chip)

    bias_q = jnp.sum(grads[0].astype(F32), axis=0) * QSCALE
    bias_v = jnp.sum(grads[2].astype(F32), axis=0)
    zero = jnp.zeros((half,), F32)

    def place(part):
        return jnp.where(core == 0, jnp.concatenate([part, zero]), jnp.concatenate([zero, part]))

    fold_rows = lambda sums: jnp.sum(sums.reshape(-1, 8, sums.shape[1]), axis=1)
    two, one = fold_rows(sums_two), fold_rows(sums_one)
    small = [place(bias_q), place(bias_v), one[2], one[0], one[1], two[2], two[0], two[1]]
    small = jnp.concatenate([v.reshape(shards, -1) for v in small] + [fold_rows(sums_up).reshape(shards, -1)], axis=1)
    small = lax.psum_scatter(small, BOTH, scatter_dimension=0, tiled=True).reshape(-1)
    parts = [small[n * width : (n + 1) * width] for n in range(8)]
    g_bq, g_bv, g_bo, g_ga, g_sa, g_bd, g_gm, g_sm = parts
    g_bu = small[8 * width :]
    return (
        result_out, grad_tokens, grad_query, grad_key, grad_value, grad_out, grad_up, grad_down,
        g_bq, g_bv, g_bo, g_bu, g_bd, g_ga, g_sa, g_gm, g_sm,
    )


def solution(mesh):
    act, flat, mat, vec = P("dp", "ctx", None), P("dp", "ctx"), P(BOTH, None), P(BOTH)
    return jax.shard_map(
        local,
        mesh=mesh,
        in_specs=(act, flat, act) + (mat,) * 6 + (vec,) * 9,
        out_specs=(act, act) + (mat,) * 6 + (vec,) * 9,
        check_vma=False,
    )
```

time: 2730 us -> 920 us (0.34)
  waiting for transfers between devices: 1440 us -> 348 us
  matrix products: 632 us -> 72.3 us
  Pallas kernels: 0 us -> 237 us
  other arithmetic: 264 us -> 34.1 us
  local copies, waits for them, and re-layouts: 204 us -> 53.2 us
  blocking collectives: 125 us -> 69.4 us
  starting transfers between devices: 47.5 us -> 76.6 us
    dot_general x74 -> x13, matrix products: 632 us -> 72.3 us  [the longest x12 61.4 us: mm(): return lax.dot_general(a, b, dims, preferred_element_type=F32)]
    reduce_scatter x3 -> x0, waiting for transfers between devices: 425 us -> none  [the longest x1 217 us: local(): lax.psum_scatter(grad_up, ('dp', 'ctx'), scatter_dimension=0, tiled=True)]
    ppermute x37 -> x71, waiting for transfers between devices: 506 us -> 182 us  [the longest x53 142 us: swap(): return lax.ppermute(value, 'ctx', [(d, d ^ mask) for d in range(count)])]
    unnamed x17 -> x6, waiting for transfers between devices: 280 us -> 0.1 us
    pallas_call x0 -> x5, Pallas kernels: none -> 237 us  [the longest x1 83.5 us: attend_back(): pl.pallas_call(functools.partial(attend_back_kernel, chunk), grid=(pairs,...]
    convert_element_type x55 -> x46, other arithmetic: 130 us -> 16.5 us  [the longest x6 8.84 us: local(): w.astype(BF)]
    reduce_sum x16 -> x5, other arithmetic: 94.6 us -> 2.54 us  [the longest x1 2.08 us: local(): bias_v = jnp.sum(grads[2].astype(F32), axis=0)]
    dynamic_slice x24 -> x31, local copies, waits for them, and re-layouts: 77.1 us -> 12.4 us  [the longest x6 8.57 us: half_cols(): return lax.dynamic_slice_in_dim(value, which * width, width, value.ndim - 1)]
  transfers between devices with their start and end apart: 51 -> 77, of which waited for: 32 -> 41; matrix products, arithmetic and copies ran while one was open for 27% -> 16% of each run, Pallas kernels for 0% -> 20%
where the time goes in v1:
time: 920 us; the launch traced here: 906 us
  waiting for transfers between devices  348 us (38%)
  Pallas kernels  237 us (26%)
  starting transfers between devices  76.6 us (8%)
  matrix products  72.3 us (8%)
  blocking collectives  69.4 us (8%)
  local copies, waits for them, and re-layouts  53.2 us (6%)
  other arithmetic  34.1 us (4%)
  between operations  15.9 us (2%)
    all_gather x6, waiting for transfers between devices, gather(): return lax.all_gather(value, BOTH, axis=0, tiled=True)  166 us
    ppermute x53, waiting for transfers between devices, swap(): return lax.ppermute(value, 'ctx', [(d, d ^ mask) for d in range(count)])  142 us
    pallas_call x1, Pallas kernels, attend_back(): pl.pallas_call(functools.partial(attend_back_kernel, chunk), grid=(pairs,...  83.5 us
    dot_general x12, matrix products, mm(): return lax.dot_general(a, b, dims, preferred_element_type=F32)  61.4 us
    pallas_call x1, Pallas kernels, attend(): pl.pallas_call(functools.partial(attend_kernel, chunk), grid=(pairs, tota...  59.4 us
    ppermute x53, starting transfers between devices, swap(): return lax.ppermute(value, 'ctx', [(d, d ^ mask) for d in range(count)])  47.3 us
    ppermute x18, waiting for transfers between devices, reduce_rows(): lax.ppermute(pick(both, (me + step) % groups), 'dp', pairs).astype(F32)  40 us
    unnamed x1, blocking collectives  39.5 us
  transfers between devices with their start and end apart: 77, of which 41 were waited for; matrix products, arithmetic and copies ran while one was open for 16% of the time, Pallas kernels for 20%

profile of v1, /device:TPU:14, one launch (start us, length us, event | category | flops | bytes accessed | tf_op | source)
XLA Modules:
  0.0 906.2 jit_solution(16600851915386673326)
XLA Ops:
  22.1 11.1 %collective-permute-done = bf16[256,1024]{1,0:T(8,128)(2,1)S(1)} collective-permute-done((bf16[256,1024]{1,0:T(8,128)(2,1)}, bf16[256,1024]{1,0:T(8,128)(2,1)S(1)}, u32[]{:S(2)}, u32[]{:S(2)}) %collective-permute-start) | collective-permute-done | bytes 524320 | tf_op jit(solution)/shard_map/ppermute | solution.py:357
  33.2 6.6 collective-permute-done.1
  39.8 5.4 collective-permute-done.2
  50.6 29.9 %all-gather.1 = bf16[32,1,384]{2,1,0:T(2,128)(2,1)S(1)} all-gather(bf16[1,1,384]{2,1,0:T(2,128)(2,1)S(1)} %reshape.282), channel_id=2, replica_groups=mesh['dp'=4,'ctx'=8] {'dp','ctx'}, dimensions={0}, use_global_device_ids=true | all-gather | bytes 25344 | tf_op jit(solution)/shard_map/all_gather | solution.py:410
  92.1 35.7 %all-gather.11.cloned.1.call-done = bf16[1024,1024]{1,0:T(8,128)(2,1)} async-done(((bf16[32,1024]{1,0:T(8,128)(2,1)}), bf16[1024,1024]{1,0:T(8,128)(2,1)}) %all-gather.11.cloned.1.call-update) | async-done | bytes 2097168 | tf_op jit(solution)/shard_map/all_gather | solution.py:410
  130.2 56.3 %all-gather.13.cloned.1.call-done = bf16[1024,1024]{1,0:T(8,128)(2,1)} async-done(((bf16[32,1024]{1,0:T(8,128)(2,1)}), bf16[1024,1024]{1,0:T(8,128)(2,1)}) %all-gather.13.cloned.1.call-update) | async-done | bytes 2097168 | tf_op jit(solution)/shard_map/all_gather | solution.py:410
  190.3 10.9 %fusion.q_ref.k_ref.v_ref = bf16[3,2048,512]{2,1,0:T(8,128)(2,1)} fusion(f32[3,512]{1,0:T(4,128)S(1)} %maximum_bitcast_fusion, bf16[2048,1024]{1,0:T(8,128)(2,1)} %constant_dynamic-update-slice_fusion, bf16[1,1024,512]{1,2,0:T(8,128)(2,1)S(1)} %bitcast.380, bf16[1,1024,512]{1,2,0:T(8,128)(2,1)S(1)} %bitcast.379, ...), kind=kOutput, calls=%fused_computation.6 | convolution fusion | flops 6451888128 | bytes 13637632 | tf_op jit(solution)/shard_map/td,cdn->ctn/dot_general | solution.py:453
  201.2 59.4 %attend.1 = (bf16[2048,512]{1,0:T(8,128)(2,1)}, bf16[4,2,2048,2048]{3,2,1,0:T(8,128)(2,1)}, f32[4,2,2048]{2,1,0:T(2,128)}) custom-call(bf16[3,2048,512]{2,1,0:T(8,128)(2,1)} %fusion.q_ref.k_ref.v_ref, bf16[3,2048,512]{2,1,0:T(8,128)(2,1)} %fusion.q_ref.k_ref.v_ref, bf16[3,2048,512]{2,1,0:T(8,128)(2,1)} %fusion.q_ref.k_ref.v_ref, s32[1,2048]{1,0:T(1,128)} %bitcast.406, ...), custom_call_target="tpu_custom_call" | custom-call | flops 44999999488 | bytes 83886080 | tf_op jit(solution)/shard_map/attend/pallas_call | solution.py:92
  266.1 6.4 collective-permute-start.11
  275.4 18.8 %collective-permute-done.10 = bf16[256,1024]{1,0:T(8,128)(2,1)} collective-permute-done((bf16[256,1024]{1,0:T(8,128)(2,1)}, bf16[256,1024]{1,0:T(8,128)(2,1)}, u32[]{:S(2)}, u32[]{:S(2)}) %collective-permute-start.10) | collective-permute-done | bytes 524320 | tf_op jit(solution)/shard_map/ppermute | solution.py:357
  294.2 9.7 %collective-permute-done.9 = bf16[256,1024]{1,0:T(8,128)(2,1)} collective-permute-done((bf16[256,1024]{1,0:T(8,128)(2,1)S(1)}, bf16[256,1024]{1,0:T(8,128)(2,1)}, u32[]{:S(2)}, u32[]{:S(2)}) %collective-permute-start.9) | collective-permute-done | bytes 524320 | tf_op jit(solution)/shard_map/ppermute | solution.py:357
  308.7 27.8 %all-gather.17.cloned.1.call-done.wu_ref = bf16[1024,4096]{1,0:T(8,128)(2,1)} async-done(((bf16[32,4096]{1,0:T(8,128)(2,1)}), bf16[1024,4096]{1,0:T(8,128)(2,1)}) %all-gather.17.cloned.1.call-update) | async-done | bytes 8388624 | tf_op jit(solution)/shard_map/all_gather | solution.py:410
  336.5 35.6 %mid_up.1 = (f32[1024,1024]{1,0:T(8,128)}, f32[1024,1]{1,0:T(8,128)}, bf16[1024,1024]{1,0:T(8,128)(2,1)}, bf16[1024,4096]{1,0:T(8,128)(2,1)}, bf16[1024,4096]{1,0:T(8,128)(2,1)}) custom-call(bf16[1024,1024]{1,0:T(8,128)(2,1)} %copy-done.12, bf16[1024,1024]{1,0:T(8,128)(2,1)} %maximum_select_fusion.o_ref, ...), custom_call_target="tpu_custom_call" | custom-call | flops 11000000512 | bytes 37748736 | tf_op jit(solution)/shard_map/mid_up/pallas_call | solution.py:253
  372.1 46.1 %all-gather.19.cloned.1.call-done.wd_ref = bf16[4096,1024]{1,0:T(8,128)(2,1)} async-done(((bf16[128,1024]{1,0:T(8,128)(2,1)}), bf16[4096,1024]{1,0:T(8,128)(2,1)}) %all-gather.19.cloned.1.call-update) | async-done | bytes 8388624 | tf_op jit(solution)/shard_map/all_gather | solution.py:410
  418.2 36.8 %mid_down.1 = (bf16[1024,1024]{1,0:T(8,128)(2,1)}, f32[1024,1024]{1,0:T(8,128)}, bf16[1024,1024]{1,0:T(8,128)(2,1)}, bf16[1024,4096]{1,0:T(8,128)(2,1)}, f32[24,1024]{1,0:T(8,128)}, /*index=5*/f32[8,4096]{1,0:T(8,128)}) custom-call(bf16[1024,4096]{1,0:T(8,128)(2,1)} %get-tuple-element.40.g_ref, bf16[1024,4096]{1,0:T(8,128)(2,1)} %get-tuple-element.41.gp_ref, ...), custom_call_target="tpu_custom_call" | custom-call | flops 16999999488 | bytes 46137344 | tf_op jit(solution)/shard_map/mid_down/pallas_call | solution.py:301
  455.0 21.4 %mid_back.1 = (f32[1024,1024]{1,0:T(8,128)}, bf16[1024,1024]{1,0:T(8,128)(2,1)}, bf16[1024,1024]{1,0:T(8,128)(2,1)}, f32[24,1024]{1,0:T(8,128)}) custom-call(f32[1024,1024]{1,0:T(8,128)} %get-tuple-element.44.dh_ref, bf16[1024,4096]{1,0:T(8,128)(2,1)} %get-tuple-element.45.du_ref, f32[1024,1024]{1,0:T(8,128)} %get-tuple-element.42.xh_ref, ...), custom_call_target="tpu_custom_call" | custom-call | flops 11000000512 | bytes 37748736 | tf_op jit(solution)/shard_map/mid_back/pallas_call | solution.py:338
  479.9 10.0 %convolution_convert_fusion = bf16[4096,512]{1,0:T(8,128)(2,1)} fusion(bf16[1024,4096]{1,0:T(8,128)(2,1)} %get-tuple-element.40.g_ref, bf16[1024,1024]{1,0:T(8,128)(2,1)S(1)} %copy-done.42, s32[]{:T(128)S(6)} %select_n.287), kind=kOutput, calls=%fused_computation.7 | convolution fusion | flops 4297064448 | bytes 13631492 | tf_op jit(solution)/shard_map/dot_general | solution.py:24
  494.9 8.5 fusion.8
  507.8 10.4 %collective-permute-done.13 = bf16[256,1024]{1,0:T(8,128)(2,1)} collective-permute-done((bf16[256,1024]{1,0:T(8,128)(2,1)}, bf16[256,1024]{1,0:T(8,128)(2,1)}, u32[]{:S(2)}, u32[]{:S(2)}) %collective-permute-start.13) | collective-permute-done | bytes 524320 | tf_op jit(solution)/shard_map/ppermute | solution.py:357
  524.6 83.5 %attend_back.1 = (bf16[2048,512]{1,0:T(8,128)(2,1)}, bf16[2048,512]{1,0:T(8,128)(2,1)}, bf16[2048,512]{1,0:T(8,128)(2,1)}) custom-call(bf16[3,2048,512]{2,1,0:T(8,128)(2,1)} %fusion.q_ref.k_ref.v_ref, bf16[3,2048,512]{2,1,0:T(8,128)(2,1)} %fusion.q_ref.k_ref.v_ref, bf16[3,2048,512]{2,1,0:T(8,128)(2,1)} %fusion.q_ref.k_ref.v_ref, ...), custom_call_target="tpu_custom_call" | custom-call | flops 85000003584 | bytes 83886080 | tf_op jit(solution)/shard_map/attend_back/pallas_call | solution.py:163
  610.4 4.7 convolution_convert_fusion.2
  637.2 6.2 add_add_fusion
  645.6 39.5 %all-reduce.4 = f32[32,384]{1,0:T(8,128)S(1)} all-reduce(f32[32,384]{1,0:T(8,128)S(1)} %concatenate.85), channel_id=3, replica_groups=mesh['dp'=4,'ctx'=8] {'dp','ctx'}, use_global_device_ids=true, to_apply=%region_5.7.clone | all-reduce | flops 12288 | bytes 98304
  755.0 7.9 collective-permute-done.17
  762.9 10.8 %collective-permute-done.18 = bf16[256,1024]{1,0:T(8,128)(2,1)S(1)} collective-permute-done((bf16[256,1024]{1,0:T(8,128)(2,1)S(1)}, bf16[256,1024]{1,0:T(8,128)(2,1)S(1)}, u32[]{:S(2)}, u32[]{:S(2)}) %collective-permute-start.18) | collective-permute-done | bytes 524320 | tf_op jit(solution)/shard_map/ppermute | solution.py:357
  776.1 9.7 %add_convert_fusion.1 = bf16[4096,512]{1,0:T(8,128)(2,1)S(1)} fusion(bf16[4096,512]{1,0:T(8,128)(2,1)} %collective-permute-done.62, bf16[1024,4096]{1,0:T(8,128)(2,1)} %get-tuple-element.40.g_ref, bf16[1024,1024]{1,0:T(8,128)(2,1)} %get-tuple-element.56, s32[]{:T(128)S(6)} %select_n.285), kind=kOutput, calls=%fused_computation.3 | convolution fusion | flops 4301258752 | bytes 17825796 | tf_op jit(solution)/shard_map/dot_general | solution.py:24
  790.1 6.7 add_convert_fusion.2
  799.7 12.7 %collective-permute-done.65 = bf16[2,2,2,128,512]{4,3,2,1,0:T(8,128)(2,1)S(1)} collective-permute-done((bf16[2,2,2,128,512]{4,3,2,1,0:T(8,128)(2,1)S(1)}, bf16[2,2,2,128,512]{4,3,2,1,0:T(8,128)(2,1)S(1)}, u32[]{:S(2)}, u32[]{:S(2)}) %collective-permute-start.65) | collective-permute-done | bytes 1048608 | tf_op jit(solution)/shard_map/ppermute | solution.py:357
  815.2 19.6 %collective-permute-done.56 = bf16[2,2,2,32,2048]{4,3,2,1,0:T(8,128)(2,1)S(1)} collective-permute-done((bf16[2,2,2,32,2048]{4,3,2,1,0:T(8,128)(2,1)S(1)}, bf16[2,2,2,32,2048]{4,3,2,1,0:T(8,128)(2,1)S(1)}, u32[]{:S(2)}, u32[]{:S(2)}) %collective-permute-start.56) | collective-permute-done | bytes 1048608 | tf_op jit(solution)/shard_map/ppermute | solution.py:357
  837.8 10.0 %collective-permute-done.66 = bf16[2,2,128,512]{3,2,1,0:T(8,128)(2,1)S(1)} collective-permute-done((bf16[2,2,128,512]{3,2,1,0:T(8,128)(2,1)S(1)}, bf16[2,2,128,512]{3,2,1,0:T(8,128)(2,1)S(1)}, u32[]{:S(2)}, u32[]{:S(2)}) %collective-permute-start.66) | collective-permute-done | bytes 524320 | tf_op jit(solution)/shard_map/ppermute | solution.py:357
  865.0 18.9 %collective-permute-done.68 = bf16[2,128,512]{2,1,0:T(8,128)(2,1)S(1)} collective-permute-done((bf16[2,128,512]{2,1,0:T(8,128)(2,1)S(1)}, bf16[2,128,512]{2,1,0:T(8,128)(2,1)S(1)}, u32[]{:S(2)}, u32[]{:S(2)}) %collective-permute-start.68) | collective-permute-done | bytes 262176 | tf_op jit(solution)/shard_map/ppermute | solution.py:397
  884.6 4.4 collective-permute-done.58
  (432 shorter events, 208.9 us)
Async XLA Ops:
  7.2 83.0 %all-gather.9.cloned.1.call-start = ((), (), s32[]{:S(2)}) async-start(), calls=%async_computation | async-start | bytes 2162688 | tf_op jit(solution)/shard_map/all_gather | solution.py:410
  9.0 118.8 %all-gather.11.cloned.1.call-start = ((), (), s32[]{:S(2)}) async-start(), calls=%async_computation.1 | async-start | bytes 2162688 | tf_op jit(solution)/shard_map/all_gather | solution.py:410
  10.6 175.9 %all-gather.13.cloned.1.call-start = ((), (), s32[]{:S(2)}) async-start(), calls=%async_computation.2 | async-start | bytes 2162688 | tf_op jit(solution)/shard_map/all_gather | solution.py:410
  12.2 296.5 %all-gather.15.cloned.1.call-start = ((), (), s32[]{:S(2)}) async-start(), calls=%async_computation.3 | async-start | bytes 2162688 | tf_op jit(solution)/shard_map/all_gather | solution.py:410
  13.8 322.7 %all-gather.17.cloned.1.call-start = ((), (), s32[]{:S(2)}) async-start(), calls=%async_computation.4 | async-start | bytes 8650752 | tf_op jit(solution)/shard_map/all_gather | solution.py:410
  15.7 402.5 %all-gather.19.cloned.1.call-start = ((), (), s32[]{:S(2)}) async-start(), calls=%async_computation.5 | async-start | bytes 8650752 | tf_op jit(solution)/shard_map/all_gather | solution.py:410
  46.6 40.5 %collective-permute-start.3 = (bf16[1024,1024]{1,0:T(8,128)(2,1)S(1)}, bf16[1024,1024]{1,0:T(8,128)(2,1)}, u32[]{:S(2)}, u32[]{:S(2)}) collective-permute-start(bf16[1024,1024]{1,0:T(8,128)(2,1)S(1)} %pad_maximum_fusion.x_ref), channel_id=1, source_target_pairs={{0,1},{1,0},{2,3},{3,2},{4,5},{5,4},{6,7},{7,6},{8,9},{9,8},{10,11... | collective-permute-start | bytes 6291464 | tf_op jit(solution)/shard_map/ppermute | solution.py:357
  46.8 34.2 %collective-permute-start.4 = (s32[256]{0:T(256)S(1)}, s32[256]{0:T(256)S(1)}, u32[]{:S(2)}, u32[]{:S(2)}) collective-permute-start(s32[256]{0:T(256)S(1)} %bitcast.409), channel_id=1, source_target_pairs={{0,2},{1,3},{2,0},{3,1},{4,6},{5,7},{6,4},{7,5},{8,10},{9,11},{10,... | collective-permute-start | bytes 3080 | tf_op jit(solution)/shard_map/ppermute | solution.py:357
  47.6 33.4 %collective-permute-start.5 = (s32[256]{0:T(256)S(1)}, s32[256]{0:T(256)S(1)}, u32[]{:S(2)}, u32[]{:S(2)}) collective-permute-start(s32[256]{0:T(256)S(1)} %bitcast.408), channel_id=1, source_target_pairs={{0,4},{1,5},{2,6},{3,7},{4,0},{5,1},{6,2},{7,3},{8,12},{9,13},{10,... | collective-permute-start | bytes 3080 | tf_op jit(solution)/shard_map/ppermute | solution.py:357
  48.9 32.1 %collective-permute-start.6 = (s32[256]{0:T(256)S(1)}, s32[256]{0:T(256)S(1)}, u32[]{:S(2)}, u32[]{:S(2)}) collective-permute-start(s32[256]{0:T(256)S(1)} %bitcast.407), channel_id=1, source_target_pairs={{0,6},{1,7},{2,4},{3,5},{4,2},{5,3},{6,0},{7,1},{8,14},{9,15},{10,... | collective-permute-start | bytes 3080 | tf_op jit(solution)/shard_map/ppermute | solution.py:357
  263.4 43.3 %collective-permute-start.8 = (bf16[1024,512]{1,0:T(8,128)(2,1)}, bf16[1024,512]{1,0:T(8,128)(2,1)S(1)}, u32[]{:S(2)}, u32[]{:S(2)}) collective-permute-start(bf16[1024,512]{1,0:T(8,128)(2,1)} %get-tuple-element.91), channel_id=1, source_target_pairs={{0,1},{1,0},{2,3},{3,2},{4,5},{5,4},{6,7},{7,6},{8,9},{9,8},{10,11... | collective-permute-start | bytes 3145736 | tf_op jit(solution)/shard_map/ppermute | solution.py:357
  264.8 29.4 %collective-permute-start.10 = (bf16[256,1024]{1,0:T(8,128)(2,1)}, bf16[256,1024]{1,0:T(8,128)(2,1)}, u32[]{:S(2)}, u32[]{:S(2)}) collective-permute-start(bf16[256,1024]{1,0:T(8,128)(2,1)} %get-tuple-element.89), channel_id=1, source_target_pairs={{0,4},{1,5},{2,6},{3,7},{4,0},{5,1},{6,2},{7,3},{8,12},{9,13},{10,... | collective-permute-start | bytes 1572872 | tf_op jit(solution)/shard_map/ppermute | solution.py:357
  266.1 28.1 %collective-permute-start.11 = (bf16[256,1024]{1,0:T(8,128)(2,1)}, bf16[256,1024]{1,0:T(8,128)(2,1)}, u32[]{:S(2)}, u32[]{:S(2)}) collective-permute-start(bf16[256,1024]{1,0:T(8,128)(2,1)} %get-tuple-element.88), channel_id=1, source_target_pairs={{0,6},{1,7},{2,4},{3,5},{4,2},{5,3},{6,0},{7,1},{8,14},{9,15},{10,... | collective-permute-start | bytes 1572872 | tf_op jit(solution)/shard_map/ppermute | solution.py:357
  272.5 31.4 %collective-permute-start.9 = (bf16[256,1024]{1,0:T(8,128)(2,1)S(1)}, bf16[256,1024]{1,0:T(8,128)(2,1)}, u32[]{:S(2)}, u32[]{:S(2)}) collective-permute-start(bf16[256,1024]{1,0:T(8,128)(2,1)S(1)} %get-tuple-element.87), channel_id=1, source_target_pairs={{0,2},{1,3},{2,0},{3,1},{4,6},{5,7},{6,4},{7,5},{8,10},{9,11},{10,... | collective-permute-start | bytes 1572872 | tf_op jit(solution)/shard_map/ppermute | solution.py:357
  479.2 42.7 %collective-permute-start.15 = (bf16[1024,512]{1,0:T(8,128)(2,1)}, bf16[1024,512]{1,0:T(8,128)(2,1)}, u32[]{:S(2)}, u32[]{:S(2)}) collective-permute-start(bf16[1024,512]{1,0:T(8,128)(2,1)} %get-tuple-element.81), channel_id=1, source_target_pairs={{0,1},{1,0},{2,3},{3,2},{4,5},{5,4},{6,7},{7,6},{8,9},{9,8},{10,11... | collective-permute-start | bytes 3145736 | tf_op jit(solution)/shard_map/ppermute | solution.py:357
  489.8 286.2 %collective-permute-start.62 = (bf16[4096,512]{1,0:T(8,128)(2,1)}, bf16[4096,512]{1,0:T(8,128)(2,1)}, u32[]{:S(2)}, u32[]{:S(2)}) collective-permute-start(bf16[4096,512]{1,0:T(8,128)(2,1)} %convolution_convert_fusion), channel_id=1, source_target_pairs={{0,1},{1,0},{2,3},{3,2},{4,5},{5,4},{6,7},{7,6},{8,9},{9,8},{10,11... | collective-permute-start | bytes 12582920 | tf_op jit(solution)/shard_map/ppermute | solution.py:357
  507.8 118.1 %collective-permute-start.44 = (bf16[1024,512]{1,0:T(8,128)(2,1)}, bf16[1024,512]{1,0:T(8,128)(2,1)}, u32[]{:S(2)}, u32[]{:S(2)}) collective-permute-start(bf16[1024,512]{1,0:T(8,128)(2,1)} %convolution_convert_fusion.1), channel_id=1, source_target_pairs={{0,1},{1,0},{2,3},{3,2},{4,5},{5,4},{6,7},{7,6},{8,9},{9,8},{10,11... | collective-permute-start | bytes 3145736 | tf_op jit(solution)/shard_map/ppermute | solution.py:357
  629.3 59.2 %collective-permute-start.47 = (bf16[2,2,2,32,512]{4,3,2,0,1:T(8,128)(2,1)}, bf16[2,2,2,32,512]{4,3,2,0,1:T(8,128)(2,1)}, u32[]{:S(2)}, u32[]{:S(2)}) collective-permute-start(bf16[2,2,2,32,512]{4,3,2,0,1:T(8,128)(2,1)} %bitcast.352), channel_id=1, source_target_pairs={{0,4},{1,5},{2,6},{3,7},{4,0},{5,1},{6,2},{7,3},{8,12},{9,13},{10,... | collective-permute-start | bytes 786440 | tf_op jit(solution)/shard_map/ppermute | solution.py:357
  630.6 60.3 %collective-permute-start.45 = (bf16[2,2,2,32,512]{4,3,2,0,1:T(8,128)(2,1)}, bf16[2,2,2,32,512]{4,3,2,0,1:T(8,128)(2,1)S(1)}, u32[]{:S(2)}, u32[]{:S(2)}) collective-permute-start(bf16[2,2,2,32,512]{4,3,2,0,1:T(8,128)(2,1)} %bitcast.353), channel_id=1, source_target_pairs={{0,2},{1,3},{2,0},{3,1},{4,6},{5,7},{6,4},{7,5},{8,10},{9,11},{10,... | collective-permute-start | bytes 786440 | tf_op jit(solution)/shard_map/ppermute | solution.py:357
  632.9 58.3 %collective-permute-start.38 = (bf16[2,2,2,32,512]{4,3,2,0,1:T(8,128)(2,1)}, bf16[2,2,2,32,512]{4,3,2,0,1:T(8,128)(2,1)}, u32[]{:S(2)}, u32[]{:S(2)}) collective-permute-start(bf16[2,2,2,32,512]{4,3,2,0,1:T(8,128)(2,1)} %bitcast.354), channel_id=1, source_target_pairs={{0,4},{1,5},{2,6},{3,7},{4,0},{5,1},{6,2},{7,3},{8,12},{9,13},{10,... | collective-permute-start | bytes 786440 | tf_op jit(solution)/shard_map/ppermute | solution.py:357
  634.3 60.0 %collective-permute-start.36 = (bf16[2,2,2,32,512]{4,3,2,0,1:T(8,128)(2,1)}, bf16[2,2,2,32,512]{4,3,2,0,1:T(8,128)(2,1)}, u32[]{:S(2)}, u32[]{:S(2)}) collective-permute-start(bf16[2,2,2,32,512]{4,3,2,0,1:T(8,128)(2,1)} %bitcast.355), channel_id=1, source_target_pairs={{0,2},{1,3},{2,0},{3,1},{4,6},{5,7},{6,4},{7,5},{8,10},{9,11},{10,... | collective-permute-start | bytes 786440 | tf_op jit(solution)/shard_map/ppermute | solution.py:357
  697.8 46.9 %collective-permute-start.16 = (bf16[1024,1024]{1,0:T(8,128)(2,1)S(1)}, bf16[1024,1024]{1,0:T(8,128)(2,1)S(1)}, u32[]{:S(2)}, u32[]{:S(2)}) collective-permute-start(bf16[1024,1024]{1,0:T(8,128)(2,1)S(1)} %slice.298), channel_id=1, source_target_pairs={{0,1},{1,0},{2,3},{3,2},{4,5},{5,4},{6,7},{7,6},{8,9},{9,8},{10,11... | collective-permute-start | bytes 6291464 | tf_op jit(solution)/shard_map/ppermute | solution.py:357
  740.5 48.1 %collective-permute-start.53 = (bf16[1024,2048]{1,0:T(8,128)(2,1)}, bf16[1024,2048]{1,0:T(8,128)(2,1)}, u32[]{:S(2)}, u32[]{:S(2)}) collective-permute-start(bf16[1024,2048]{1,0:T(8,128)(2,1)} %fusion.8), channel_id=1, source_target_pairs={{0,1},{1,0},{2,3},{3,2},{4,5},{5,4},{6,7},{7,6},{8,9},{9,8},{10,11... | collective-permute-start | bytes 12582920 | tf_op jit(solution)/shard_map/ppermute | solution.py:357
  797.3 37.5 %collective-permute-start.56 = (bf16[2,2,2,32,2048]{4,3,2,1,0:T(8,128)(2,1)S(1)}, bf16[2,2,2,32,2048]{4,3,2,1,0:T(8,128)(2,1)S(1)}, u32[]{:S(2)}, u32[]{:S(2)}) collective-permute-start(bf16[2,2,2,32,2048]{4,3,2,1,0:T(8,128)(2,1)S(1)} %dynamic-slice_bitcast_fusion.1), channel_id=1, source_target_pairs={{0,4},{1,5},{2,6},{3,7},{4,0},{5,1},{6,2},{7,3},{8,12},{9,13},{10,... | collective-permute-start | bytes 3145736 | tf_op jit(solution)/shard_map/ppermute | solution.py:357
  799.0 38.0 %collective-permute-start.54 = (bf16[2,2,2,32,2048]{4,3,2,0,1:T(8,128)(2,1)S(1)}, bf16[2,2,2,32,2048]{4,3,2,0,1:T(8,128)(2,1)S(1)}, u32[]{:S(2)}, u32[]{:S(2)}) collective-permute-start(bf16[2,2,2,32,2048]{4,3,2,0,1:T(8,128)(2,1)S(1)} %bitcast.378), channel_id=1, source_target_pairs={{0,2},{1,3},{2,0},{3,1},{4,6},{5,7},{6,4},{7,5},{8,10},{9,11},{10,... | collective-permute-start | bytes 3145736 | tf_op jit(solution)/shard_map/ppermute | solution.py:357
  812.8 35.1 %collective-permute-start.66 = (bf16[2,2,128,512]{3,2,1,0:T(8,128)(2,1)S(1)}, bf16[2,2,128,512]{3,2,1,0:T(8,128)(2,1)S(1)}, u32[]{:S(2)}, u32[]{:S(2)}) collective-permute-start(bf16[2,2,128,512]{3,2,1,0:T(8,128)(2,1)S(1)} %dynamic-slice_bitcast_fusion.2), channel_id=1, source_target_pairs={{0,2},{1,3},{2,0},{3,1},{4,6},{5,7},{6,4},{7,5},{8,10},{9,11},{10,... | collective-permute-start | bytes 1572872 | tf_op jit(solution)/shard_map/ppermute | solution.py:357
  814.9 33.1 %collective-permute-start.64 = (bf16[2,2,128,512]{3,2,1,0:T(8,128)(2,1)S(1)}, bf16[2,2,128,512]{3,2,1,0:T(8,128)(2,1)S(1)}, u32[]{:S(2)}, u32[]{:S(2)}) collective-permute-start(bf16[2,2,128,512]{3,2,1,0:T(8,128)(2,1)S(1)} %dynamic-slice_bitcast_fusion.3), channel_id=1, source_target_pairs={{0,4},{1,5},{2,6},{3,7},{4,0},{5,1},{6,2},{7,3},{8,12},{9,13},{10,... | collective-permute-start | bytes 1572872 | tf_op jit(solution)/shard_map/ppermute | solution.py:357
  850.5 33.4 %collective-permute-start.68 = (bf16[2,128,512]{2,1,0:T(8,128)(2,1)S(1)}, bf16[2,128,512]{2,1,0:T(8,128)(2,1)S(1)}, u32[]{:S(2)}, u32[]{:S(2)}) collective-permute-start(bf16[2,128,512]{2,1,0:T(8,128)(2,1)S(1)} %get-tuple-element.96), channel_id=1, source_target_pairs={{0,16},{8,24},{16,0},{24,8},{1,17},{9,25},{17,1},{25,9},{2,18},{10... | collective-permute-start | bytes 786440 | tf_op jit(solution)/shard_map/ppermute | solution.py:397
  853.5 30.7 %collective-permute-start.69 = (bf16[2,128,512]{2,1,0:T(8,128)(2,1)S(1)}, bf16[2,128,512]{2,1,0:T(8,128)(2,1)S(1)}, u32[]{:S(2)}, u32[]{:S(2)}) collective-permute-start(bf16[2,128,512]{2,1,0:T(8,128)(2,1)S(1)} %get-tuple-element.97), channel_id=1, source_target_pairs={{0,24},{8,0},{16,8},{24,16},{1,25},{9,1},{17,9},{25,17},{2,26},{10... | collective-permute-start | bytes 786440 | tf_op jit(solution)/shard_map/ppermute | solution.py:397
  857.7 31.3 %collective-permute-start.58 = (bf16[2,32,2048]{2,1,0:T(8,128)(2,1)S(1)}, bf16[2,32,2048]{2,1,0:T(8,128)(2,1)S(1)}, u32[]{:S(2)}, u32[]{:S(2)}) collective-permute-start(bf16[2,32,2048]{2,1,0:T(8,128)(2,1)S(1)} %get-tuple-element.98), channel_id=1, source_target_pairs={{0,8},{8,16},{16,24},{24,0},{1,9},{9,17},{17,25},{25,1},{2,10},{10... | collective-permute-start | bytes 786440 | tf_op jit(solution)/shard_map/ppermute | solution.py:397
  859.8 32.0 %collective-permute-start.59 = (bf16[2,32,2048]{2,1,0:T(8,128)(2,1)S(1)}, bf16[2,32,2048]{2,1,0:T(8,128)(2,1)S(1)}, u32[]{:S(2)}, u32[]{:S(2)}) collective-permute-start(bf16[2,32,2048]{2,1,0:T(8,128)(2,1)S(1)} %get-tuple-element.99), channel_id=1, source_target_pairs={{0,16},{8,24},{16,0},{24,8},{1,17},{9,25},{17,1},{25,9},{2,18},{10... | collective-permute-start | bytes 786440 | tf_op jit(solution)/shard_map/ppermute | solution.py:397
  865.0 29.5 %collective-permute-start.60 = (bf16[2,32,2048]{2,1,0:T(8,128)(2,1)S(1)}, bf16[2,32,2048]{2,1,0:T(8,128)(2,1)S(1)}, u32[]{:S(2)}, u32[]{:S(2)}) collective-permute-start(bf16[2,32,2048]{2,1,0:T(8,128)(2,1)S(1)} %get-tuple-element.100), channel_id=1, source_target_pairs={{0,24},{8,0},{16,8},{24,16},{1,25},{9,1},{17,9},{25,17},{2,26},{10... | collective-permute-start | bytes 786440 | tf_op jit(solution)/shard_map/ppermute | solution.py:397
  (92 other events, 1218.1 us)
Sparse Core Ops, SparseCore 0:
  11.5 57.5 all-gather.8
  72.5 55.2 all-gather.10
  131.2 55.2 all-gather.12
  189.2 55.2 all-gather.14
  247.2 89.2 all-gather.16
  339.2 78.9 all-gather.18

commit v2 on v1

v2 whole, which is shorter than its diff:
```python
import functools

import jax
import jax.numpy as jnp
from jax import lax
from jax.experimental import pallas as pl
from jax.experimental.pallas import tpu as pltpu
from jax.sharding import PartitionSpec as P

HD = 64
MASKED = -1e30
EPSILON = 1e-05
QSCALE = 0.125
BF = jnp.bfloat16
F32 = jnp.float32
NT = (((1,), (1,)), ((), ()))
NN = (((1,), (0,)), ((), ()))
TN = (((0,), (0,)), ((), ()))
VMEM_LIMIT = 56 << 20
BOTH = ("dp", "ctx")
ANY = pl.BlockSpec(memory_space=pl.ANY)
SMEM = pl.BlockSpec(memory_space=pltpu.SMEM)
TILE = 16


def mm(a, b, dims=NN):
    return lax.dot_general(a, b, dims, preferred_element_type=F32)


def params():
    return pltpu.CompilerParams(vmem_limit_bytes=VMEM_LIMIT)


def shard_copies(refs, order_ref, cols, target, sems, base=0, turn=None):
    copies = []
    total = target.shape[0]
    for ref in refs:
        rows = ref.shape[1]
        for n in range(ref.shape[0]):
            index = len(copies)
            row = order_ref[index] * rows
            if turn is not None:
                row = lax.rem(row + turn, total)
            row = pl.multiple_of(row, TILE)
            copies.append(pltpu.make_async_copy(ref.at[n, :, cols], target.at[pl.ds(row, rows), :], sems.at[base + index]))
    return copies


def shards_of(pieces):
    return sum(piece.shape[0] for piece in pieces)


def place_kernel(count, width, order_ref, *refs):
    refs, (w_ref, vec_ref, sems) = refs[:count], refs[count:]
    shards = shards_of(refs)
    first = pl.multiple_of(order_ref[shards], 128)
    copies = shard_copies(refs, order_ref, pl.ds(first, width), w_ref, sems)
    copies += shard_copies(refs, order_ref, slice(2 * width, refs[0].shape[2]), vec_ref, sems, shards)
    for copy in copies:
        copy.start()
    for copy in copies:
        copy.wait()


def place(pieces, order, width):
    rows = shards_of(pieces) * pieces[0].shape[1]
    return pl.pallas_call(
        functools.partial(place_kernel, len(pieces), width),
        in_specs=[SMEM] + [ANY] * len(pieces),
        out_shape=[
            jax.ShapeDtypeStruct((rows, width), BF),
            jax.ShapeDtypeStruct((rows, pieces[0].shape[2] - 2 * width), BF),
        ],
        scratch_shapes=[pltpu.SemaphoreType.DMA((2 * shards_of(pieces),))],
        compiler_params=params(),
        name="place",
    )(order, *pieces)


def head_parts(block):
    lane = lax.broadcasted_iota(jnp.int32, block.shape, 1)
    zero = jnp.zeros_like(block)
    return [jnp.where(lane < HD, block, zero), jnp.where(lane < HD, zero, block)]


def attend_kernel(chunk, extra, q_ref, k_ref, v_ref, sq_ref, sk_ref, *rest):
    o_ref, p_ref, l_ref, vt_ref, kn_ref = rest[extra:]
    i = pl.program_id(1)
    total = k_ref.shape[0]
    block = q_ref.shape[0]

    @pl.when(i == 0)
    def _():
        vt_ref[...] = v_ref[...].T
        keys = k_ref[...].astype(F32)
        norms = jnp.sum((keys * keys).T.reshape(2, HD, total), axis=1)
        kn_ref[...] = jnp.sqrt(jnp.max(norms, axis=1, keepdims=True))

    q = q_ref[...]
    parts = head_parts(q)
    q32 = q.astype(F32)
    qn = jnp.sqrt(jnp.sum((q32 * q32).T.reshape(2, HD, block), axis=1))
    bound = qn * kn_ref[...]
    seg_q = sq_ref[...]
    ones = jnp.ones((16, chunk), BF)

    def scores(h, lo):
        s = mm(k_ref[lo : lo + chunk, :], parts[h], NT)
        return jnp.where(sk_ref[lo : lo + chunk, :] == seg_q, s, MASKED)

    def finish(shift):
        acc = [jnp.zeros((HD + 16, block), F32)] * 2
        for lo in range(0, total, chunk):
            for h in range(2):
                p = jnp.exp(scores(h, lo) - shift[h : h + 1]).astype(BF)
                p_ref[h, lo : lo + chunk, :] = p
                left = jnp.concatenate([vt_ref[h * HD : h * HD + HD, lo : lo + chunk], ones], axis=0)
                acc[h] = acc[h] + mm(left, p)
        sums = [acc[h][HD : HD + 1] for h in range(2)]
        out = jnp.concatenate([acc[h][:HD] / sums[h] for h in range(2)], axis=0)
        o_ref[...] = out.T.astype(BF)
        sums = jnp.concatenate(sums, axis=0)
        l_ref[...] = 1.0 / sums
        return sums

    sums = finish(bound)
    good = jnp.min(sums) > 1e-20

    @pl.when(jnp.logical_not(good))
    def _():
        most = [jnp.full((1, block), MASKED, F32)] * 2
        for lo in range(0, total, chunk):
            for h in range(2):
                most[h] = jnp.maximum(most[h], jnp.max(scores(h, lo), axis=0, keepdims=True))
        finish(jnp.concatenate(most, axis=0))


def attend(qkv, seg_row, seg_col, base, pairs, held=None, waits=(), block=256, chunk=512):
    total = qkv.shape[0]
    specs = lambda c: pl.BlockSpec((total, 128), lambda h, i: (0, 3 * (base + h) + c))
    kept = [] if held is None else [held]
    return pl.pallas_call(
        functools.partial(attend_kernel, chunk, len(waits) + len(kept)),
        grid=(pairs, total // block),
        in_specs=[
            pl.BlockSpec((block, 128), lambda h, i: (i, 3 * (base + h))),
            specs(1),
            specs(2),
            pl.BlockSpec((1, block), lambda h, i: (0, i)),
            pl.BlockSpec((total, 1), lambda h, i: (0, 0)),
        ] + [ANY] * (len(kept) + len(waits)),
        out_specs=[
            pl.BlockSpec((block, 128), lambda h, i: (i, base + h)),
            pl.BlockSpec((None, 2, total, block), lambda h, i: (h, 0, 0, i)),
            pl.BlockSpec((None, 2, block), lambda h, i: (h, 0, i)),
        ],
        out_shape=[
            jax.ShapeDtypeStruct((total, qkv.shape[1] // 3), BF),
            jax.ShapeDtypeStruct((pairs, 2, total, total), BF),
            jax.ShapeDtypeStruct((pairs, 2, total), F32),
        ],
        scratch_shapes=[pltpu.VMEM((128, total), BF), pltpu.VMEM((2, 1), F32)],
        compiler_params=params(),
        cost_estimate=pl.CostEstimate(flops=pairs * 12 * 10**9, bytes_accessed=pairs << 24, transcendentals=0),
        input_output_aliases={5: 0} if kept else {},
        name="attend",
    )(qkv, qkv, qkv, seg_row, seg_col, *kept, *waits)


def attend_back_kernel(chunk, extra, q_ref, k_ref, v_ref, o_ref, do_ref, do2_ref, p_ref, l_ref, *rest):
    out_ref, mark_ref, kt_ref, dk_acc, dv_acc = rest[extra:]
    mark_ref[...] = jnp.zeros_like(mark_ref)
    i = pl.program_id(1)
    total = k_ref.shape[0]
    block = q_ref.shape[0]

    @pl.when(i == 0)
    def _():
        kt_ref[...] = k_ref[...].T
        dk_acc[...] = jnp.zeros_like(dk_acc)
        dv_acc[...] = jnp.zeros_like(dv_acc)

    do = jnp.where(i < pl.num_programs(1) // 2, do_ref[...], do2_ref[...])
    q_parts = head_parts(q_ref[...])
    do_parts = head_parts(do)
    product = do.astype(F32) * o_ref[...].astype(F32)
    delta = jnp.sum(product.T.reshape(2, HD, block), axis=1)
    inverse = l_ref[...]
    grad_q = [jnp.zeros((HD, block), F32)] * 2
    for lo in range(0, total, chunk):
        rows = slice(lo, lo + chunk)
        values = v_ref[rows, :]
        for h in range(2):
            p = p_ref[h, rows, :].astype(F32) * inverse[h : h + 1]
            grad_p = mm(values, do_parts[h], NT)
            grad_s = (p * (grad_p - delta[h : h + 1])).astype(BF)
            dv_acc[rows, :] += mm(p.astype(BF), do_parts[h])
            dk_acc[rows, :] += mm(grad_s, q_parts[h])
            grad_q[h] = grad_q[h] + mm(kt_ref[h * HD : h * HD + HD, rows], grad_s)
    out_ref[pl.ds(pl.multiple_of(i * block, block), block), 0:128] = jnp.concatenate(grad_q, axis=0).T.astype(BF)

    @pl.when(i == pl.num_programs(1) - 1)
    def _():
        out_ref[:, 128:256] = dk_acc[...].astype(BF)
        out_ref[:, 256:384] = dv_acc[...].astype(BF)


def attend_back(qkv, out, grad_mine, grad_mate, probs, inverse, base, held=None, waits=(), block=256, chunk=512):
    total = qkv.shape[0]
    kept = [] if held is None else [held]
    pairs = probs.shape[0]
    last = total // block // 2 - 1
    whole = lambda c: pl.BlockSpec((total, 128), lambda h, i: (0, 3 * (base + h) + c))
    rows = pl.BlockSpec((block, 128), lambda h, i: (i, base + h))
    return pl.pallas_call(
        functools.partial(attend_back_kernel, chunk, len(waits) + len(kept)),
        grid=(pairs, total // block),
        in_specs=[
            pl.BlockSpec((block, 128), lambda h, i: (i, 3 * (base + h))),
            whole(1),
            whole(2),
            rows,
            pl.BlockSpec((block, 128), lambda h, i: (jnp.minimum(i, last), base + h)),
            pl.BlockSpec((block, 128), lambda h, i: (jnp.maximum(i - last - 1, 0), base + h)),
            pl.BlockSpec((None, 2, total, block), lambda h, i: (h, 0, 0, i)),
            pl.BlockSpec((None, 2, block), lambda h, i: (h, 0, i)),
        ] + [ANY] * (len(kept) + len(waits)),
        out_specs=[pl.BlockSpec((total, 384), lambda h, i: (0, base + h)), pl.BlockSpec((8, 128), lambda h, i: (0, 0))],
        out_shape=[jax.ShapeDtypeStruct(qkv.shape, BF), jax.ShapeDtypeStruct((8, 128), F32)],
        scratch_shapes=[
            pltpu.VMEM((128, total), BF),
            pltpu.VMEM((total, 128), F32),
            pltpu.VMEM((total, 128), F32),
        ],
        compiler_params=params(),
        cost_estimate=pl.CostEstimate(flops=pairs * 21 * 10**9, bytes_accessed=pairs << 24, transcendentals=0),
        input_output_aliases={8: 0} if kept else {},
        name="attend_back",
    )(qkv, qkv, qkv, out, grad_mine, grad_mate, probs, inverse, *kept, *waits)


def gelu_parts(u):
    scaled = jnp.abs(u) * 0.7071067811865476
    den = 1.0 + 0.3275911 * scaled
    t = pl.reciprocal(den, approx=True)
    t = t * (2.0 - den * t)
    e = jnp.exp(u * u * -0.5)
    poly = t * (
        0.127414796
        + t * (-0.142248368 + t * (0.7107068705 + t * (-0.7265760135 + t * 0.5307027145)))
    )
    tail = poly * e
    phi = jnp.where(u >= 0, 1.0 - tail, tail)
    return u * phi, phi + u * (e * 0.3989422804014327)


def mean(value):
    return jnp.mean(value, axis=-1, keepdims=True)


def normed(hidden):
    centred = hidden - mean(hidden)
    inverse = lax.rsqrt(mean(centred * centred) + EPSILON)
    return centred * inverse, inverse


def norm_back(grad_in, scaled, inverse, gain):
    grad_scaled = grad_in * gain
    return inverse * (grad_scaled - mean(grad_scaled) - scaled * mean(grad_scaled * scaled))


def fold(value):
    return jnp.sum(value.reshape(value.shape[0] // 8, 8, value.shape[1]), axis=0)


def add_fold(ref, first, value):
    part = fold(value)

    @pl.when(first)
    def _():
        ref[...] = part

    @pl.when(jnp.logical_not(first))
    def _():
        ref[...] += part


def token_rows(x, span, block, at=lambda i: i):
    return pl.BlockSpec((block // span, span, x.shape[2]), lambda i: (at(i), 0, 0))


def qkv_kernel(xm_ref, xt_ref, w_ref, b_ref, out_ref):
    i = pl.program_id(0)
    x = jnp.where(i < pl.num_programs(0) // 2, xm_ref[...], xt_ref[...])
    out_ref[...] = (mm(x.reshape(out_ref.shape[0], -1), w_ref[...]) + b_ref[...]).astype(BF)


def project(x_mine, x_mate, span, weight, bias, block=256):
    steps = x_mine.shape[0] * span // block
    full = lambda a: pl.BlockSpec(a.shape, lambda i: (0, 0), pipeline_mode=pl.Buffered(1))
    width = weight.shape[1]
    return pl.pallas_call(
        qkv_kernel,
        grid=(2 * steps,),
        in_specs=[
            token_rows(x_mine, span, block, lambda i: jnp.minimum(i, steps - 1)),
            token_rows(x_mate, span, block, lambda i: jnp.maximum(i - steps, 0)),
            full(weight),
            full(bias),
        ],
        out_specs=pl.BlockSpec((block, width), lambda i: (i, 0)),
        out_shape=jax.ShapeDtypeStruct((2 * steps * block, width), BF),
        compiler_params=params(),
        cost_estimate=pl.CostEstimate(flops=7 * 10**9, bytes_accessed=14 << 20, transcendentals=0),
        name="project",
    )(x_mine, x_mate, weight, bias)


def mid_up_kernel(step, count, mates, order_ref, x_ref, om_ref, vec_ref, bu_ref, *refs):
    mate_refs, refs = refs[:mates], refs[mates:]
    pieces, (xh_ref, r_ref, xb_ref, g_ref, gp_ref, wo_ref, wu_ref, sems) = refs[:count], refs[count:]
    first = pl.program_id(0) == 0
    d, ff = wu_ref.shape
    shards = shards_of(pieces)

    def out_copies():
        return shard_copies(pieces, order_ref, slice(0, d), wo_ref, sems, 0, order_ref[shards])

    def up_copies():
        return shard_copies(pieces, order_ref, slice(d, d + ff), wu_ref, sems, shards)

    @pl.when(first)
    def _():
        for copy in out_copies() + up_copies():
            copy.start()
        for copy in out_copies():
            copy.wait()

    half = om_ref.shape[1]
    mixed = mm(om_ref[...], wo_ref[0:half, :])
    for ref in mate_refs:
        mixed = mixed + mm(ref[...], wo_ref[half : half + ref.shape[1], :])
        half += ref.shape[1]
    hidden = x_ref[...].reshape(mixed.shape).astype(F32) + mixed + vec_ref[0:1, :]
    scaled, inverse = normed(hidden)
    xh_ref[...] = scaled
    r_ref[...] = inverse
    xb = (scaled * vec_ref[1:2, :] + vec_ref[2:3, :]).astype(BF)
    xb_ref[...] = xb

    @pl.when(first)
    def _():
        for copy in up_copies():
            copy.wait()

    for lo in range(0, ff, step):
        cols = slice(lo, lo + step)
        g, gp = gelu_parts(mm(xb, wu_ref[:, cols]) + bu_ref[:, cols])
        g_ref[:, cols] = g.astype(BF)
        gp_ref[:, cols] = gp.astype(BF)


def mid_up(x, span, attn, o_mate, pieces, order, vecs, b_up, block=256, step=512):
    rows, d = x.shape[0] * span, x.shape[2]
    ff = b_up.shape[1]
    row = lambda n: pl.BlockSpec((block, n), lambda i: (i, 0))
    full = lambda a: pl.BlockSpec(a.shape, lambda i: (0, 0), pipeline_mode=pl.Buffered(1))
    return pl.pallas_call(
        functools.partial(mid_up_kernel, step, len(pieces), len(o_mate)),
        grid=(rows // block,),
        in_specs=[SMEM, token_rows(x, span, block), row(d // 2), full(vecs), full(b_up)]
        + [row(a.shape[1]) for a in o_mate]
        + [ANY] * len(pieces),
        out_specs=[row(d), row(1), row(d), row(ff), row(ff)],
        out_shape=[
            jax.ShapeDtypeStruct((rows, d), F32),
            jax.ShapeDtypeStruct((rows, 1), F32),
            jax.ShapeDtypeStruct((rows, d), BF),
            jax.ShapeDtypeStruct((rows, ff), BF),
            jax.ShapeDtypeStruct((rows, ff), BF),
        ],
        scratch_shapes=[
            pltpu.VMEM((d, d), BF),
            pltpu.VMEM((d, ff), BF),
            pltpu.SemaphoreType.DMA((2 * shards_of(pieces),)),
        ],
        compiler_params=params(),
        cost_estimate=pl.CostEstimate(flops=20 * 10**9, bytes_accessed=36 << 20, transcendentals=0),
        name="mid_up",
    )(order, x, attn, vecs, b_up, *o_mate, *pieces)


def mid_down_kernel(step, count, order_ref, g_ref, gp_ref, xh_ref, dy_ref, vec_ref, *refs):
    pieces, (out_ref, dh_ref, dm_ref, du_ref, s_ref, su_ref, wd_ref, sems) = refs[:count], refs[count:]
    first = pl.program_id(0) == 0
    d = wd_ref.shape[1]

    @pl.when(first)
    def _():
        copies = shard_copies(pieces, order_ref, slice(0, d), wd_ref, sems)
        for copy in copies:
            copy.start()
        for copy in copies:
            copy.wait()

    x1 = xh_ref[...] * vec_ref[1:2, :] + vec_ref[2:3, :]
    hidden = x1 + mm(g_ref[...], wd_ref[...]) + vec_ref[3:4, :]
    scaled, inverse = normed(hidden)
    gain = vec_ref[4:5, :]
    out_ref[...] = (scaled * gain + vec_ref[5:6, :]).astype(BF)
    dy = dy_ref[...].astype(F32)
    dh = norm_back(dy, scaled, inverse, gain)
    dm = dh.astype(BF)
    dh_ref[...] = dh
    dm_ref[...] = dm
    add_fold(s_ref.at[0:8, :], first, dy * scaled)
    add_fold(s_ref.at[8:16, :], first, dy)
    add_fold(s_ref.at[16:24, :], first, dm.astype(F32))
    for lo in range(0, wd_ref.shape[0], step):
        cols = slice(lo, lo + step)
        du = (mm(dm, wd_ref[cols, :], NT) * gp_ref[:, cols].astype(F32)).astype(BF)
        du_ref[:, cols] = du
        add_fold(su_ref.at[:, cols], first, du.astype(F32))


def mid_down(g, gp, xh, dy, pieces, order, vecs, block=256, step=2048):
    rows, d = xh.shape
    ff = g.shape[1]
    row = lambda n: pl.BlockSpec((block, n), lambda i: (i, 0))
    full = lambda a: pl.BlockSpec(a.shape, lambda i: (0, 0), pipeline_mode=pl.Buffered(1))
    keep = lambda r, n: pl.BlockSpec((r, n), lambda i: (0, 0))
    return pl.pallas_call(
        functools.partial(mid_down_kernel, step, len(pieces)),
        grid=(rows // block,),
        in_specs=[SMEM, row(ff), row(ff), row(d), row(d), full(vecs)] + [ANY] * len(pieces),
        out_specs=[row(d), row(d), row(d), row(ff), keep(24, d), keep(8, ff)],
        out_shape=[
            jax.ShapeDtypeStruct((rows, d), BF),
            jax.ShapeDtypeStruct((rows, d), F32),
            jax.ShapeDtypeStruct((rows, d), BF),
            jax.ShapeDtypeStruct((rows, ff), BF),
            jax.ShapeDtypeStruct((24, d), F32),
            jax.ShapeDtypeStruct((8, ff), F32),
        ],
        scratch_shapes=[pltpu.VMEM((ff, d), BF), pltpu.SemaphoreType.DMA((shards_of(pieces),))],
        compiler_params=params(),
        cost_estimate=pl.CostEstimate(flops=25 * 10**9, bytes_accessed=44 << 20, transcendentals=0),
        name="mid_down",
    )(order, g, gp, xh, dy, vecs, *pieces)


def mid_back_kernel(count, order_ref, dh_ref, du_ref, xh_ref, r_ref, vec_ref, *refs):
    pieces, (dh1_ref, da_ref, dom_ref, dot_ref, s_ref, wu_ref, wo_ref, sems) = refs[:count], refs[count:]
    first = pl.program_id(0) == 0
    d, ff = wu_ref.shape
    half = dom_ref.shape[1]
    shards = shards_of(pieces)

    @pl.when(first)
    def _():
        copies = shard_copies(pieces, order_ref, slice(d, d + ff), wu_ref, sems, shards)
        copies += shard_copies(pieces, order_ref, slice(0, d), wo_ref, sems, 0, order_ref[shards])
        for copy in copies:
            copy.start()
        for copy in copies:
            copy.wait()

    dx = dh_ref[...] + mm(du_ref[...], wu_ref[...], NT)
    scaled = xh_ref[...]
    dh1 = norm_back(dx, scaled, r_ref[...], vec_ref[1:2, :])
    dh1_ref[...] = dh1
    da = dh1.astype(BF)
    da_ref[...] = da
    dom_ref[...] = mm(da, wo_ref[0:half, :], NT).astype(BF)
    dot_ref[...] = mm(da, wo_ref[half:, :], NT).astype(BF)
    add_fold(s_ref.at[0:8, :], first, dx * scaled)
    add_fold(s_ref.at[8:16, :], first, dx)
    add_fold(s_ref.at[16:24, :], first, da.astype(F32))


def mid_back(dh, du, xh, r, pieces, order, vecs, block=256):
    rows, d = dh.shape
    ff = du.shape[1]
    row = lambda n: pl.BlockSpec((block, n), lambda i: (i, 0))
    full = lambda a: pl.BlockSpec(a.shape, lambda i: (0, 0), pipeline_mode=pl.Buffered(1))
    return pl.pallas_call(
        functools.partial(mid_back_kernel, len(pieces)),
        grid=(rows // block,),
        in_specs=[SMEM, row(d), row(ff), row(d), row(1), full(vecs)] + [ANY] * len(pieces),
        out_specs=[row(d), row(d), row(d // 2), row(d // 2), pl.BlockSpec((24, d), lambda i: (0, 0))],
        out_shape=[
            jax.ShapeDtypeStruct((rows, d), F32),
            jax.ShapeDtypeStruct((rows, d), BF),
            jax.ShapeDtypeStruct((rows, d // 2), BF),
            jax.ShapeDtypeStruct((rows, d // 2), BF),
            jax.ShapeDtypeStruct((24, d), F32),
        ],
        scratch_shapes=[
            pltpu.VMEM((d, ff), BF),
            pltpu.VMEM((d, d), BF),
            pltpu.SemaphoreType.DMA((2 * shards_of(pieces),)),
        ],
        compiler_params=params(),
        cost_estimate=pl.CostEstimate(flops=15 * 10**9, bytes_accessed=36 << 20, transcendentals=0),
        name="mid_back",
    )(order, dh, du, xh, r, vecs, *pieces)


def token_kernel(split, waits, chip_ref, grad_ref, w_ref, *refs):
    outs = refs[len(refs) - split :]
    total = mm(grad_ref[...], w_ref[...], NT)
    for ref in refs[: len(refs) - split - waits]:
        total = total + ref[...].astype(F32)
    total = total.astype(BF)
    if split == 1:
        outs[0][...] = total
        return
    for n in range(split):

        @pl.when(pl.program_id(0) == n)
        def _():
            outs[n][...] = total


def token_grad(grads, weight, shift, adds, chip, chips, split, waits=()):
    d = weight.shape[0]
    rows = grads.shape[0] // 2
    block = rows // chips
    base = shift * chips
    at = lambda i, c: c[0] ^ i if split else i
    plain = lambda a: pl.BlockSpec((block, a.shape[1]), lambda i, c: (at(i, c), 0))
    if split:
        out_specs = [pl.BlockSpec((block, d), lambda i, c: (0, 0))] * chips
        out_shape = [jax.ShapeDtypeStruct((block, d), BF)] * chips
    else:
        out_specs = [pl.BlockSpec((block, d), lambda i, c: (i, 0))]
        out_shape = [jax.ShapeDtypeStruct((rows, d), BF)]
    return pl.pallas_call(
        functools.partial(token_kernel, len(out_shape), len(waits)),
        grid_spec=pltpu.PrefetchScalarGridSpec(
            num_scalar_prefetch=1,
            grid=(chips,),
            in_specs=[
                pl.BlockSpec((block, grads.shape[1]), lambda i, c: (base + at(i, c), 0)),
                pl.BlockSpec(weight.shape, lambda i, c: (0, 0), pipeline_mode=pl.Buffered(1)),
            ]
            + [plain(a) for a in adds]
            + [ANY] * len(waits),
            out_specs=out_specs,
        ),
        out_shape=out_shape,
        compiler_params=params(),
        cost_estimate=pl.CostEstimate(flops=10**8, bytes_accessed=1 << 16, transcendentals=0),
        name="token_grad",
    )(jnp.reshape(chip, (1,)).astype(jnp.int32), grads, weight, *adds, *waits)


def order_kernel(chip_ref, *refs):
    pieces, (out_ref, sems) = refs[:-2], refs[-2:]
    copies = [
        pltpu.make_async_copy(piece, out_ref.at[chip_ref[0] ^ n], sems.at[n]) for n, piece in enumerate(pieces)
    ]
    for copy in copies:
        copy.start()
    for copy in copies:
        copy.wait()


def in_order(pieces, chip):
    chips = len(pieces)
    return pl.pallas_call(
        order_kernel,
        in_specs=[SMEM] + [ANY] * chips,
        out_shape=jax.ShapeDtypeStruct((chips,) + pieces[0].shape, BF),
        scratch_shapes=[pltpu.SemaphoreType.DMA((chips,))],
        compiler_params=params(),
        name="in_order",
    )(jnp.reshape(chip, (1,)).astype(jnp.int32), *pieces)


def by_chip(value, out_ref, lo):
    chips, dps, rows, _ = out_ref.shape
    value = value.reshape(dps, chips, rows, value.shape[1])
    for n in range(dps):
        out_ref[:, n, :, lo : lo + value.shape[3]] = value[n].astype(BF)


def proj_kernel(xm_ref, xt_ref, grad_ref, *refs):
    out_ref = refs[-1]
    own = grad_ref.shape[0] // 2
    xm = xm_ref[...].reshape(own, -1)
    xt = xt_ref[...].reshape(own, -1)
    by_chip(mm(xm, grad_ref[0:own, :], TN) + mm(xt, grad_ref[own:, :], TN), out_ref, 0)
    if grad_ref.shape[1] < out_ref.shape[3]:
        out_ref[:, :, :, grad_ref.shape[1] :] = refs[0][...]


def dp_steps(groups, least):
    return max(1, min(groups, least // 128))


def shard_specs(steps, groups, chips, rows, cols):
    spec = pl.BlockSpec((chips, groups // steps, rows, cols), lambda i, *_: (0, i, 0, 0))
    return spec, jax.ShapeDtypeStruct((chips, groups, rows, cols), BF)


def proj_grad(x_mine, x_mate, span, grads, first, pairs, groups, chips, waits=(), extra=None):
    own, d = x_mine.shape[0] * span, x_mine.shape[2]
    width = 384 * pairs
    more = [] if extra is None else [extra]
    steps = dp_steps(groups, d)
    col = pl.BlockSpec((x_mine.shape[0], span, d // steps), lambda i: (0, 0, i))
    rows = d // groups // chips
    spec, shape = shard_specs(steps, groups, chips, rows, width + sum(a.shape[3] for a in more))
    return pl.pallas_call(
        proj_kernel,
        grid=(steps,),
        in_specs=[col, col]
        + [pl.BlockSpec((2 * own, width), lambda i: (0, first // pairs), pipeline_mode=pl.Buffered(1))]
        + [shard_specs(steps, groups, chips, rows, a.shape[3])[0] for a in more]
        + [ANY] * len(waits),
        out_specs=spec,
        out_shape=shape,
        compiler_params=params(),
        cost_estimate=pl.CostEstimate(flops=10**8, bytes_accessed=1 << 16, transcendentals=0),
        name="proj_grad",
    )(x_mine, x_mate, grads, *more, *waits)


def weight_kernel(adds, waits, turn_ref, *refs):
    out_ref, refs = refs[-1], refs[: len(refs) - 1 - waits]
    count = (len(refs) - adds) // 2
    more = refs[2 * count :]
    lo = 0
    for n in range(count):
        value = mm(refs[2 * n][...], refs[2 * n + 1][...], TN)
        width = value.shape[1]
        chips, dps, rows, _ = out_ref.shape
        value = value.reshape(dps, chips, rows, width)
        for k in range(dps):
            part = value[k]
            if more:
                part = part + more[0][:, k, :, lo : lo + width].astype(F32)
            out_ref[:, k, :, lo : lo + width] = part.astype(BF)
        lo += width
    if lo < out_ref.shape[3]:
        out_ref[:, :, :, lo:] = more[-1][...]


def weight_grad(sides, turns, groups, chips, adds=(), waits=()):
    in_specs, args = [], []
    steps = dp_steps(groups, min(left.shape[1] for left, _ in sides))
    rows_of = lambda a: a.shape[1] // steps
    for n, (left, right) in enumerate(sides):
        tokens = left.shape[0]
        in_specs.append(
            pl.BlockSpec((tokens, rows_of(left)), lambda i, t, n=n: (0, lax.rem(i + t[1 + n] * (steps // 2), steps)))
        )
        in_specs.append(
            pl.BlockSpec((tokens, right.shape[1] // 2), lambda i, t: (0, t[0]), pipeline_mode=pl.Buffered(1))
        )
        args += [left, right]
    rows = sides[0][0].shape[1] // groups // chips
    cols = sum(right.shape[1] // 2 for _, right in sides)
    if len(adds) > 1:
        cols += adds[1].shape[3]
    in_specs += [shard_specs(steps, groups, chips, rows, a.shape[3])[0] for a in adds] + [ANY] * len(waits)
    spec, shape = shard_specs(steps, groups, chips, rows, cols)
    flops = sum(a.shape[0] * a.shape[1] * b.shape[1] for a, b in sides)
    return pl.pallas_call(
        functools.partial(weight_kernel, len(adds), len(waits)),
        grid_spec=pltpu.PrefetchScalarGridSpec(
            num_scalar_prefetch=1, grid=(steps,), in_specs=in_specs, out_specs=spec
        ),
        out_shape=shape,
        compiler_params=params(),
        cost_estimate=pl.CostEstimate(flops=flops, bytes_accessed=20 << 20, transcendentals=0),
        name="weight_grad",
    )(turns, *args, *adds, *waits)


def swap(value, mask):
    count = lax.axis_size("ctx")
    return lax.ppermute(value, "ctx", [(d, d ^ mask) for d in range(count)])


def along(value, step):
    count = lax.axis_size("dp")
    return lax.ppermute(value, "dp", [(s, (s + step) % count) for s in range(count)])


def pick(value, index, axis=0):
    return lax.dynamic_index_in_dim(value, index, axis, keepdims=False)


def over_chips(value):
    count = lax.axis_size("ctx")
    groups = [list(range(core, count, 2)) for core in range(2)]
    return lax.all_to_all(value, "ctx", 0, 0, axis_index_groups=groups)


def repeat(value):
    return jnp.broadcast_to(value[None], (lax.axis_size("ctx") // 2,) + value.shape)


def tick(value):
    return (value[(0,) * value.ndim].astype(F32) > 1e30).astype(jnp.int32)


def tie_kernel(*refs):
    pass


def tie(value, *waits):
    return pl.pallas_call(
        tie_kernel,
        in_specs=[ANY] * (1 + len(waits)),
        out_specs=ANY,
        out_shape=jax.ShapeDtypeStruct(value.shape, value.dtype),
        input_output_aliases={0: 0},
        name="tie",
    )(value, *waits)


class Gather:
    def __init__(self, own, place):
        self.place = place
        self.groups = lax.axis_size("dp")
        self.chips = lax.axis_size("ctx") // 2
        self.own = own
        self.whole = own.shape[0] % TILE != 0

    def along_dp(self, value):
        if self.whole:
            return []
        self.turns = [value] + [along(value, s) for s in range(1, self.groups)]
        return self.turns[1:]

    def over_chips(self, later):
        if self.whole:
            return []
        self.held = over_chips(repeat(jnp.stack(self.turns) + later.astype(BF)))
        return [self.held]

    def plane(self):
        if self.whole:
            return []
        got = [swap(self.own, 2 * r) for r in range(1, self.chips)]
        self.held = jnp.stack([self.own] + got)
        return got

    def dp_arrays(self):
        self.held = self.turns
        return self.turns

    def between_cores(self, *waits):
        me, chip, core = self.place
        if self.whole:
            return [lax.all_gather(self.own, BOTH, axis=0, tiled=True)[None]], jnp.zeros((1,), jnp.int32)
        count = 2 * self.chips
        turn = (me - jnp.arange(self.groups)) % self.groups * count
        chip_of = jnp.arange(self.chips)
        if isinstance(self.held, list):
            pieces, order = [], []
            for n, value in enumerate(self.held):
                value = tie(value, *waits) if waits else value
                pieces += [value, swap(value, 1)]
                order += [turn[n] + 2 * (chip_of ^ chip) + core, turn[n] + 2 * (chip_of ^ chip) + 1 - core]
        else:
            flat = self.held.reshape((-1,) + self.own.shape)
            flat = tie(flat, *waits) if waits else flat
            pieces = [flat, swap(flat, 1)]
            numbers = (turn[None] + 2 * chip_of[:, None]).reshape(-1)
            order = [numbers + core, numbers + 1 - core]
        return pieces, jnp.concatenate(order).astype(jnp.int32)


class Reduce:
    def __init__(self, grad, place, direct=False):
        self.place = place
        self.groups = grad.shape[1]
        if direct:
            chip = place[1]
            sent = [pick(grad, chip ^ r) for r in range(1, grad.shape[0])]
            self.got = [pick(grad, chip)] + [swap(v, 2 * (r + 1)) for r, v in enumerate(sent)]
        else:
            self.got = over_chips(grad)

    def chip_sum(self, *waits):
        if isinstance(self.got, list):
            last = tie(self.got[-1], *self.got[1:-1], *waits)
            self.part = sum(v.astype(F32) for v in self.got[:-1] + [last]).astype(BF)
        else:
            self.part = jnp.sum(tie(self.got, *waits).astype(F32), axis=0).astype(BF)
        return [self.part]

    def along_dp(self):
        me = self.place[0]
        sent = [pick(self.part, (me + step) % self.groups) for step in range(1, self.groups)]
        self.turns = [pick(self.part, me)] + [along(v, n + 1) for n, v in enumerate(sent)]

    def dp_sum(self, *waits):
        last = tie(self.turns[-1], *self.turns[1:-1], *waits)
        total = sum(v.astype(F32) for v in self.turns[:-1] + [last]).astype(BF)
        self.total = total.reshape(2, -1, total.shape[1])
        return [self.total]

    def finish(self):
        core = self.place[2]
        mine = pick(self.total, core).astype(F32)
        other = swap(pick(self.total, 1 - core), 1).astype(F32)
        return [jnp.where(core == 0, mine, other), jnp.where(core == 0, other, mine)], mine + other


def half_cols(value, which):
    width = value.shape[-1] // 2
    return lax.dynamic_slice_in_dim(value, which * width, width, value.ndim - 1)


def spread(vectors, shards, rows):
    flat = jnp.concatenate([v.reshape(shards, -1) for v in vectors], axis=1)
    return jnp.pad(flat, ((0, 0), (0, rows * 128 - flat.shape[1]))).reshape(shards, rows, 128)


def fold_rows(sums):
    return jnp.sum(sums.reshape(-1, 8, sums.shape[1]), axis=1)


def local(
    tokens, segments, cotangent, w_query, w_key, w_value, w_out, w_up, w_down,
    b_query, b_value, b_out, b_up, b_down, gain_attn, shift_attn, gain_mlp, shift_mlp,
):
    seqs, span, d = tokens.shape
    count = lax.axis_size("ctx")
    groups = lax.axis_size("dp")
    chips = count // 2
    ctx = lax.axis_index("ctx")
    chip, core = ctx // 2, ctx % 2
    place_of = (lax.axis_index("dp"), chip, core)
    ff = w_up.shape[1]
    half = d // 2
    shards = groups * count
    rows = d // shards
    width = d // shards
    pairs = half // 128
    bf = lambda v: v.astype(BF)

    vec_names = (b_query, b_value, b_out, gain_attn, shift_attn, b_down, gain_mlp, shift_mlp)
    vec_size = 8 * width + ff // shards
    extra = -(-(vec_size + seqs * span) // (rows * 128)) * 128
    vec_pack = jnp.concatenate([bf(v) for v in vec_names] + [bf(b_up), bf(segments.reshape(-1))])
    vec_pack = jnp.pad(vec_pack, (0, rows * extra - vec_pack.shape[0])).reshape(rows, extra)
    by_pair = [bf(w).reshape(rows, 2 * pairs, 1, 128) for w in (w_query * QSCALE, w_key, w_value)]
    pack_proj = jnp.concatenate(
        [jnp.concatenate(by_pair, axis=2).reshape(rows, 3 * d), vec_pack], axis=1
    )

    got = over_chips(tokens)
    own = chips * span
    proj = Gather(pack_proj, place_of)
    turns_of = proj.along_dp(proj.own)
    got = tie(got, *turns_of)
    mate = swap(got, 1)
    later = tick(got)
    held = proj.over_chips(later)
    pieces, order = proj.between_cores()
    everywhere = lambda v: lax.all_gather(bf(v) + later.astype(BF), BOTH, axis=0, tiled=True).reshape(2, -1, v.shape[1])
    up_pieces = [everywhere(jnp.concatenate([w_out, w_up], axis=1))]
    down_pieces = [everywhere(w_down)]
    down_order = jnp.arange(2, dtype=jnp.int32)
    if proj.whole:
        w_cat = half_cols(pieces[0][0, :, : 3 * d], core)
        vec_block = pieces[0][0, :, 3 * d :]
    else:
        w_cat, vec_block = place(pieces, jnp.append(order, core * 3 * half), 3 * half)
    packed = vec_block.reshape(shards, rows * extra)
    vec_all = packed[:, :vec_size].astype(F32)
    seg_all = packed[:, vec_size : vec_size + seqs * span].reshape(groups, chips, 2, seqs, span)
    seg_own = pick(pick(seg_all, place_of[0]), chip, 2)
    seg = jnp.concatenate([pick(seg_own, core, 1), pick(seg_own, 1 - core, 1)]).reshape(-1).astype(jnp.int32)
    vec = [vec_all[:, n * width : (n + 1) * width].reshape(1, d) for n in range(8)]
    bias_up = vec_all[:, 8 * width : 8 * width + ff // shards].reshape(1, ff)
    vecs = jnp.concatenate(vec[2:] + [jnp.zeros((2, d), F32)], axis=0)
    bias_by_pair = [v.reshape(1, 2 * pairs, 1, 128) for v in (vec[0] * QSCALE, jnp.zeros((1, d), F32), vec[1])]
    bias_cat = half_cols(jnp.concatenate(bias_by_pair, axis=2).reshape(1, 3 * d), core)

    qkv = project(got, mate, span, w_cat, bias_cat)
    seg_row, seg_col = seg.reshape(1, -1), seg.reshape(-1, 1)

    waits = []
    attn, probs, inverse, o_mate = None, [], [], []
    for n in range(pairs):
        attn, p, l = attend(qkv, seg_row, seg_col, n, 1, attn, waits)
        probs.append(p)
        inverse.append(l)
        waits = []
        if n % 2 == 1:
            o_mate.append(swap(attn[own:, (n - 1) * 128 : (n + 1) * 128], 1))
    dy = over_chips(cotangent + tick(attn).astype(BF)).reshape(own, d)
    up_order = jnp.stack([jnp.zeros((), jnp.int32), jnp.ones((), jnp.int32), d - core * half]).astype(jnp.int32)
    xh, r, xb, g, gp = mid_up(got, span, attn, o_mate, up_pieces, up_order, vecs, bias_up)
    out, dh2, dm, du, sums_two, sums_up = mid_down(g, gp, xh, dy, down_pieces, down_order, vecs)
    result_out = over_chips(out.reshape(chips, span, d))

    zero = jnp.zeros((), jnp.int32)
    turns = lambda half_of, *more: jnp.stack([half_of, *more]).astype(jnp.int32)
    got_down = swap(weight_grad([(g, dm)], turns(1 - core, zero), groups, chips), 1)
    dh1, da, do_mine, do_send, sums_one = mid_back(dh2, du, xh, r, up_pieces, up_order, vecs)
    do_mate = swap(do_send, 1)
    kept_down = weight_grad([(g, dm)], turns(core, zero), groups, chips, [got_down], [result_out])
    sum_down = Reduce(kept_down, place_of)

    o_both = jnp.concatenate([attn[:own]] + o_mate, axis=1)
    sides, shift = [(xb, du), (o_both, da)], core
    got_up = swap(weight_grad(sides, turns(1 - core, zero, shift), groups, chips, (), [kept_down]), 1)
    two, one = fold_rows(sums_two), fold_rows(sums_one)
    per_shard = lambda v: jnp.moveaxis(bf(v).reshape(groups, chips, -1, 128), 1, 0)
    vec_grads = per_shard(spread([one[2], one[0], one[1], two[2], two[0], two[1], fold_rows(sums_up)], shards, rows))

    grads, waits = None, []
    for n in range(pairs):
        grads, mark = attend_back(qkv, attn, do_mine, do_mate, probs[n], inverse[n], n, grads, waits)
        waits = []
        if n == 0:
            got_up = tie(got_up, mark)
            kept_up = weight_grad(sides, turns(core, zero, shift), groups, chips, [got_up, vec_grads])
            waits = sum_down.chip_sum(mark, kept_up)
            sum_down.along_dp()
            sum_up = Reduce(kept_up, place_of)
        elif n == 1:
            waits = sum_down.dp_sum(mark)
        elif n == 2:
            first = proj_grad(got, mate, span, grads, 0, 3, groups, chips)
            waits = sum_up.chip_sum(mark, first)
            sum_up.along_dp()
            sum_first = Reduce(first, place_of)
    grads = tie(grads, *sum_first.chip_sum(mark), *sum_up.dp_sum(mark))
    bias_sums = jnp.sum(grads.astype(F32), axis=0).reshape(pairs, 3, 128)
    blank = jnp.zeros((half,), F32)

    def whole_vector(c):
        part = bias_sums[:, c].reshape(-1)
        return jnp.where(core == 0, jnp.concatenate([part, blank]), jnp.concatenate([blank, part]))

    bias_grads = per_shard(spread([whole_vector(0), whole_vector(2)], shards, rows))
    token_send = token_grad(grads, w_cat, 1, (), chip, chips, False)[0]
    token_got = swap(token_send, 1)
    last = proj_grad(got, mate, span, grads, 3, 1, groups, chips, [token_send], bias_grads)
    sum_last = Reduce(last, place_of, True)
    grad_mine = token_grad(grads, w_cat, 0, (dh1, token_got), chip, chips, False, [last])[0]
    sum_last.chip_sum(grad_mine)
    grad_mine = tie(grad_mine, sum_last.part)
    grad_tokens = over_chips(grad_mine.reshape(chips, span, d))
    sum_last.part = jnp.concatenate([sum_first.part, sum_last.part], axis=2)
    sum_last.along_dp()
    sum_last.dp_sum(grad_tokens)
    sum_up.total = jnp.concatenate([sum_up.total, sum_last.total], axis=2)

    halves, _ = sum_down.finish()
    grad_down = jnp.concatenate(halves, axis=1)
    halves, both = sum_up.finish()
    cuts = [0, ff // 2, half, 128, 3 * half - 384, 384, 128]
    cuts = [sum(cuts[: n + 1]) for n in range(len(cuts))]
    cut = lambda v, n: v[:, cuts[n] : cuts[n + 1]]
    grad_up = jnp.concatenate([cut(v, 0) for v in halves], axis=1)
    grad_out = jnp.concatenate([cut(v, 1) for v in halves], axis=1)
    small = cut(both, 2).reshape(-1)
    g_bo, g_ga, g_sa, g_bd, g_gm, g_sm = [small[n * width : (n + 1) * width] for n in range(6)]
    g_bu = small[6 * width : 6 * width + ff // shards]
    small = cut(both, 5).reshape(-1)
    g_bq, g_bv = small[:width] * QSCALE, small[width : 2 * width]
    joined = jnp.concatenate([v.reshape(rows, -1, 3, 128) for h in halves for v in (cut(h, 3), cut(h, 4))], axis=1)
    grad_query, grad_key, grad_value = [joined[:, :, c].reshape(rows, d) for c in range(3)]
    return (
        result_out, grad_tokens, grad_query * QSCALE, grad_key, grad_value, grad_out, grad_up, grad_down,
        g_bq, g_bv, g_bo, g_bu, g_bd, g_ga, g_sa, g_gm, g_sm,
    )


def solution(mesh):
    act, flat, mat, vec = P("dp", "ctx", None), P("dp", "ctx"), P(BOTH, None), P(BOTH)
    return jax.shard_map(
        local,
        mesh=mesh,
        in_specs=(act, flat, act) + (mat,) * 6 + (vec,) * 9,
        out_specs=(act, act) + (mat,) * 6 + (vec,) * 9,
        check_vma=False,
    )
```

time: 920 us -> 668 us (0.73); the launches traced: 906 us -> 668 us
  waiting for transfers between devices: 348 us -> 49.9 us
  Pallas kernels: 237 us -> 347 us
  matrix products: 72.3 us -> 0 us
  starting transfers between devices: 76.6 us -> 123 us
  blocking collectives: 69.4 us -> 52 us
  local copies, waits for them, and re-layouts: 53.2 us -> 38.1 us
    all_gather x6 -> x2, waiting for transfers between devices: 166 us -> 0.02 us  [local(): lax.all_gather(bf(v) + later.astype(BF), BOTH, axis=0, tiled=True)]
    ppermute x53 -> x13, waiting for transfers between devices: 142 us -> 10.7 us  [swap(): return lax.ppermute(value, 'ctx', [(d, d ^ mask) for d in range(count)])]
    pallas_call x5 -> x32, Pallas kernels: 237 us -> 347 us  [the longest x4 93.9 us: attend_back(): pl.pallas_call(functools.partial(attend_back_kernel, chunk, len(waits) +...]
    dot_general x13 -> x0, matrix products: 72.3 us -> none  [the longest x12 61.4 us: mm(): return lax.dot_general(a, b, dims, preferred_element_type=F32)]
    all_to_all x0 -> x1, blocking collectives: none -> 52 us  [over_chips(): return lax.all_to_all(value, 'ctx', 0, 0, axis_index_groups=groups)]
    ppermute x18 -> x12, starting transfers between devices: 29.1 us -> 78.9 us  [along(): lax.ppermute(value, 'dp', [(s, (s + step) % count) for s in range(count)])]
    ppermute x53 -> x13, starting transfers between devices: 47.3 us -> 7.5 us  [swap(): return lax.ppermute(value, 'ctx', [(d, d ^ mask) for d in range(count)])]
    unnamed x1 -> x0, blocking collectives: 39.5 us -> none
  transfers between devices with their start and end apart: 77 -> 34, of which waited for: 41 -> 12; matrix products, arithmetic and copies ran while one was open for 16% -> 7% of each run, Pallas kernels for 20% -> 41%
where the time goes in v2:
time: 668 us
  Pallas kernels  347 us (52%)
  starting transfers between devices  123 us (18%)
  blocking collectives  52 us (8%)
  waiting for transfers between devices  49.9 us (7%)
  other arithmetic  41 us (6%)
  local copies, waits for them, and re-layouts  38.1 us (6%)
  between operations  16.8 us (3%)
    pallas_call x4, Pallas kernels, attend_back(): pl.pallas_call(functools.partial(attend_back_kernel, chunk, len(waits) +...  93.9 us
    ppermute x12, starting transfers between devices, along(): lax.ppermute(value, 'dp', [(s, (s + step) % count) for s in range(count)])  78.9 us
    pallas_call x4, Pallas kernels, attend(): pl.pallas_call(functools.partial(attend_kernel, chunk, len(waits) + len(k...  67.4 us
    all_to_all x1, blocking collectives, over_chips(): return lax.all_to_all(value, 'ctx', 0, 0, axis_index_groups=groups)  52 us
    pallas_call x4, Pallas kernels, weight_grad(): pl.pallas_call(functools.partial(weight_kernel, len(adds), len(waits)), g...  43.3 us
    all_to_all x7, starting transfers between devices, over_chips(): return lax.all_to_all(value, 'ctx', 0, 0, axis_index_groups=groups)  36.8 us
    pallas_call x1, Pallas kernels, mid_up(): pl.pallas_call(functools.partial(mid_up_kernel, step, len(pieces), len(o_...  35.9 us
    pallas_call x1, Pallas kernels, mid_down(): pl.pallas_call(functools.partial(mid_down_kernel, step, len(pieces)), gri...  33.6 us
  transfers between devices with their start and end apart: 34, of which 12 were waited for; matrix products, arithmetic and copies ran while one was open for 7% of the time, Pallas kernels for 41%

profile of v2, /device:TPU:14, one launch (start us, length us, event | category | flops | bytes accessed | tf_op | source)
XLA Modules:
  0.0 667.7 jit_solution(10970022960160770622)
XLA Ops:
  18.7 10.2 %collective-permute-done.refs_1_ = bf16[32,3200]{1,0:T(8,128)(2,1)S(1)} collective-permute-done((bf16[32,3200]{1,0:T(8,128)(2,1)S(1)}, bf16[32,3200]{1,0:T(8,128)(2,1)S(1)}, u32[]{:S(2)}, u32[]{:S(2)}) %collective-permute-start) | collective-permute-done | bytes 204832 | tf_op jit(solution)/shard_map/ppermute | solution.py:689
  42.6 52.0 %all_to_all.40 = bf16[4,4,32,3200]{3,2,1,0:T(8,128)(2,1)} all-to-all(bf16[4,4,32,3200]{3,2,1,0:T(8,128)(2,1)S(1)} %broadcast_in_dim.4), channel_id=1, replica_groups={{0,2,4,6},{1,3,5,7},{8,10,12,14},{9,11,13,15},{16,18,20,22},{17,19,21,2..., dimensions={0} | all-to-all | bytes 6553600 | tf_op jit(solution)/shard_map/all_to_all | solution.py:699
  96.1 7.8 %collective-permute-done.4.refs_1_ = bf16[16,32,3200]{2,1,0:T(8,128)(2,1)} collective-permute-done((bf16[16,32,3200]{2,1,0:T(8,128)(2,1)}, bf16[16,32,3200]{2,1,0:T(8,128)(2,1)}, u32[]{:S(2)}, u32[]{:S(2)}) %collective-permute-start.4) | collective-permute-done | bytes 3276832 | tf_op jit(solution)/shard_map/ppermute | solution.py:684
  103.8 5.4 place.1
  112.9 12.2 %project.1.q_ref.k_ref.v_ref = bf16[2048,1536]{1,0:T(8,128)(2,1)} custom-call(bf16[4,256,1024]{2,1,0:T(8,128)(2,1)} %tie.11.xm_ref.x_ref, bf16[4,256,1024]{2,1,0:T(8,128)(2,1)} %collective-permute-done.3.xt_ref, bf16[1024,1536]{1,0:T(8,128)(2,1)} %get-tuple-element.55.w_ref, f32[1,1536]{1,0:T(1,128)} %constant_dynamic-slice_fusion.2.b_ref), custom_call_target="tpu_custom_call" | custom-call | flops 7000000000 | bytes 14680064 | tf_op jit(solution)/shard_map/project/pallas_call | solution.py:302
  125.1 16.7 %attend.4 = (bf16[2048,512]{1,0:T(8,128)(2,1)}, bf16[1,2,2048,2048]{3,2,1,0:T(8,128)(2,1)}, f32[1,2,2048]{2,1,0:T(2,128)}) custom-call(bf16[2048,1536]{1,0:T(8,128)(2,1)} %project.1.q_ref.k_ref.v_ref, bf16[2048,1536]{1,0:T(8,128)(2,1)} %project.1.q_ref.k_ref.v_ref, bf16[2048,1536]{1,0:T(8,128)(2,1)} %project.1.q_ref.k_ref.v_ref, s32[1,2048]{1,0:T(1,128)} %bitcast.156, ...), custom_call_target="tpu_custom_call" | custom-call | flops 12000000000 | bytes 16777216 | tf_op jit(solution)/shard_map/attend/pallas_call | solution.py:142
  141.8 16.7 %attend.5 = (bf16[2048,512]{1,0:T(8,128)(2,1)}, bf16[1,2,2048,2048]{3,2,1,0:T(8,128)(2,1)}, f32[1,2,2048]{2,1,0:T(2,128)}) custom-call(bf16[2048,1536]{1,0:T(8,128)(2,1)} %project.1.q_ref.k_ref.v_ref, bf16[2048,1536]{1,0:T(8,128)(2,1)} %project.1.q_ref.k_ref.v_ref, bf16[2048,1536]{1,0:T(8,128)(2,1)} %project.1.q_ref.k_ref.v_ref, ...), custom_call_target="tpu_custom_call", output_to_operand_aliasing={{0}: (5, {})} | custom-call | flops 12000000000 | bytes 16777216 | tf_op jit(solution)/shard_map/attend/pallas_call | solution.py:142
  159.7 17.0 %attend.6 = (bf16[2048,512]{1,0:T(8,128)(2,1)}, bf16[1,2,2048,2048]{3,2,1,0:T(8,128)(2,1)}, f32[1,2,2048]{2,1,0:T(2,128)}) custom-call(bf16[2048,1536]{1,0:T(8,128)(2,1)} %project.1.q_ref.k_ref.v_ref, bf16[2048,1536]{1,0:T(8,128)(2,1)} %project.1.q_ref.k_ref.v_ref, bf16[2048,1536]{1,0:T(8,128)(2,1)} %project.1.q_ref.k_ref.v_ref, ...), custom_call_target="tpu_custom_call", output_to_operand_aliasing={{0}: (5, {})} | custom-call | flops 12000000000 | bytes 16777216 | tf_op jit(solution)/shard_map/attend/pallas_call | solution.py:142
  176.7 16.9 %attend.7 = (bf16[2048,512]{1,0:T(8,128)(2,1)}, bf16[1,2,2048,2048]{3,2,1,0:T(8,128)(2,1)}, f32[1,2,2048]{2,1,0:T(2,128)}) custom-call(bf16[2048,1536]{1,0:T(8,128)(2,1)} %project.1.q_ref.k_ref.v_ref, bf16[2048,1536]{1,0:T(8,128)(2,1)} %project.1.q_ref.k_ref.v_ref, bf16[2048,1536]{1,0:T(8,128)(2,1)} %project.1.q_ref.k_ref.v_ref, ...), custom_call_target="tpu_custom_call", output_to_operand_aliasing={{0}: (5, {})} | custom-call | flops 12000000000 | bytes 16777216 | tf_op jit(solution)/shard_map/attend/pallas_call | solution.py:142
  203.0 7.3 %all-to-all-start.2 = ((bf16[4,256,1024]{2,1,0:T(8,128)(2,1)}), bf16[4,256,1024]{2,1,0:T(8,128)(2,1)S(1)}, u32[]{:S(2)}, u32[]{:S(2)}) async-start(bf16[4,256,1024]{2,1,0:T(8,128)(2,1)} %broadcast_add_fusion), calls=%async_computation.2 | async-start | bytes 4194304 | tf_op jit(solution)/shard_map/all_to_all | solution.py:699
  211.0 35.9 %mid_up.1 = (f32[1024,1024]{1,0:T(8,128)}, f32[1024,1]{1,0:T(8,128)}, bf16[1024,1024]{1,0:T(8,128)(2,1)}, bf16[1024,4096]{1,0:T(8,128)(2,1)}, bf16[1024,4096]{1,0:T(8,128)(2,1)}) custom-call(s32[3]{0:T(128)} %pad_add_fusion.4.order_ref, bf16[4,256,1024]{2,1,0:T(8,128)(2,1)} %tie.11.xm_ref.x_ref, bf16[2048,512]{1,0:T(8,128)(2,1)} %get-tuple-element.60.om_ref.o_ref, ...), custom_call_target="tpu_custom_call" | custom-call | flops 20000000000 | bytes 37748736 | tf_op jit(solution)/shard_map/mid_up/pallas_call | solution.py:368
  248.3 33.6 %mid_down.1 = (bf16[1024,1024]{1,0:T(8,128)(2,1)}, f32[1024,1024]{1,0:T(8,128)}, bf16[1024,1024]{1,0:T(8,128)(2,1)}, bf16[1024,4096]{1,0:T(8,128)(2,1)}, f32[24,1024]{1,0:T(8,128)}, /*index=5*/f32[8,4096]{1,0:T(8,128)}) custom-call(s32[2]{0:T(128)} %iota.13.order_ref, bf16[1024,4096]{1,0:T(8,128)(2,1)} %get-tuple-element.61.g_ref.refs_0_, ...), custom_call_target="tpu_custom_call" | custom-call | flops 24999999488 | bytes 46137344 | tf_op jit(solution)/shard_map/mid_down/pallas_call | solution.py:432
  281.9 9.7 %weight_grad.4 = bf16[4,4,256,512]{3,2,1,0:T(8,128)(2,1)} custom-call(s32[2]{0:T(128)} %pad_add_fusion.turn_ref, bf16[1024,4096]{1,0:T(8,128)(2,1)} %get-tuple-element.61.g_ref.refs_0_, bf16[1024,1024]{1,0:T(8,128)(2,1)} %get-tuple-element.79.refs_1_), custom_call_target="tpu_custom_call" | custom-call | flops 4294967296 | bytes 20971520 | tf_op jit(solution)/shard_map/weight_grad/pallas_call | solution.py:670
  301.2 22.6 %mid_back.1 = (f32[1024,1024]{1,0:T(8,128)}, bf16[1024,1024]{1,0:T(8,128)(2,1)}, bf16[1024,512]{1,0:T(8,128)(2,1)}, bf16[1024,512]{1,0:T(8,128)(2,1)}, f32[24,1024]{1,0:T(8,128)}) custom-call(s32[3]{0:T(128)} %pad_add_fusion.4.order_ref, f32[1024,1024]{1,0:T(8,128)} %get-tuple-element.65.dh_ref, bf16[1024,4096]{1,0:T(8,128)(2,1)} %get-tuple-element.66.du_ref.refs_1_, ...), custom_call_target="tpu_custom_call" | custom-call | flops 15000000512 | bytes 37748736 | tf_op jit(solution)/shard_map/mid_back/pallas_call | solution.py:486
  325.1 10.3 %weight_grad.5.refs_4_ = bf16[4,4,256,512]{3,2,1,0:T(8,128)(2,1)} custom-call(s32[2]{0:T(128)} %pad_add_fusion.1.turn_ref, bf16[1024,4096]{1,0:T(8,128)(2,1)} %get-tuple-element.61.g_ref.refs_0_, bf16[1024,1024]{1,0:T(8,128)(2,1)} %get-tuple-element.79.refs_1_, bf16[4,4,256,512]{3,2,1,0:T(8,128)(2,1)} %collective-permute-done.8.refs_2_, ...), custom_call_target="tpu_custom_call" | custom-call | flops 4294967296 | bytes 20971520 | tf_op jit(solution)/shard_map/weight_grad/pallas_call | solution.py:670
  335.4 11.2 %weight_grad.6 = bf16[4,4,64,2560]{3,2,1,0:T(8,128)(2,1)} custom-call(s32[3]{0:T(128)} %fusion.31.turn_ref, bf16[1024,1024]{1,0:T(8,128)(2,1)} %get-tuple-element.81.refs_0_, bf16[1024,4096]{1,0:T(8,128)(2,1)} %get-tuple-element.66.du_ref.refs_1_, bf16[1024,1024]{1,0:T(8,128)(2,1)} %pad_maximum_fusion.refs_2_, bf16[1024,1024]{1,0:T(8,128)(2,1)} %get-tuple-element.82.refs_3_, ...), custom_call_target="tpu_custom_call" | custom-call | flops 5368709120 | bytes 20971520 | tf_op jit(solution)/shard_map/weight_grad/pallas_call | solution.py:670
  357.2 23.4 %attend_back.4 = (bf16[2048,1536]{1,0:T(8,128)(2,1)}, f32[8,128]{1,0:T(8,128)}) custom-call(bf16[2048,1536]{1,0:T(8,128)(2,1)} %project.1.q_ref.k_ref.v_ref, bf16[2048,1536]{1,0:T(8,128)(2,1)} %project.1.q_ref.k_ref.v_ref, bf16[2048,1536]{1,0:T(8,128)(2,1)} %project.1.q_ref.k_ref.v_ref, bf16[2048,512]{1,0:T(8,128)(2,1)} %get-tuple-element.60.om_ref.o_ref, ...), custom_call_target="tpu_custom_call" | custom-call | flops 20999999488 | bytes 16777216 | tf_op jit(solution)/shard_map/attend_back/pallas_call | solution.py:215
  380.6 12.1 %weight_grad.7.refs_2_ = bf16[4,4,64,2688]{3,2,1,0:T(8,128)(2,1)} custom-call(s32[3]{0:T(128)} %fusion.30.turn_ref, bf16[1024,1024]{1,0:T(8,128)(2,1)} %get-tuple-element.81.refs_0_, bf16[1024,4096]{1,0:T(8,128)(2,1)} %get-tuple-element.66.du_ref.refs_1_, bf16[1024,1024]{1,0:T(8,128)(2,1)} %pad_maximum_fusion.refs_2_, ...), custom_call_target="tpu_custom_call" | custom-call | flops 5368709120 | bytes 20971520 | tf_op jit(solution)/shard_map/weight_grad/pallas_call | solution.py:670
  392.7 6.4 all-to-all-done.4.refs_0_
  399.1 6.7 %all-to-all-start.5 = ((bf16[4,4,64,2688]{3,2,1,0:T(8,128)(2,1)}), bf16[4,4,64,2688]{3,2,1,0:T(8,128)(2,1)}, u32[]{:S(2)}, u32[]{:S(2)}) async-start(bf16[4,4,64,2688]{3,2,1,0:T(8,128)(2,1)} %weight_grad.7.refs_2_), calls=%async_computation.5 | async-start | bytes 11010048 | tf_op jit(solution)/shard_map/all_to_all | solution.py:699
  409.0 38.5 %collective-permute-start.10 = (bf16[256,512]{1,0:T(8,128)(2,1)S(1)}, bf16[256,512]{1,0:T(8,128)(2,1)S(1)}, u32[]{:S(2)}, u32[]{:S(2)}) collective-permute-start(bf16[256,512]{1,0:T(8,128)(2,1)S(1)} %get-tuple-element.112), channel_id=1, source_target_pairs={{0,8},{8,16},{16,24},{24,0},{1,9},{9,17},{17,25},{25,1},{2,10},{10... | collective-permute-start | bytes 786440 | tf_op jit(solution)/shard_map/ppermute | solution.py:689
  447.5 26.9 %collective-permute-start.11 = (bf16[256,512]{1,0:T(8,128)(2,1)S(1)}, bf16[256,512]{1,0:T(8,128)(2,1)S(1)}, u32[]{:S(2)}, u32[]{:S(2)}) collective-permute-start(bf16[256,512]{1,0:T(8,128)(2,1)S(1)} %get-tuple-element.110), channel_id=1, source_target_pairs={{0,16},{8,24},{16,0},{24,8},{1,17},{9,25},{17,1},{25,9},{2,18},{10... | collective-permute-start | bytes 786440 | tf_op jit(solution)/shard_map/ppermute | solution.py:689
  474.3 23.4 %attend_back.5 = (bf16[2048,1536]{1,0:T(8,128)(2,1)}, f32[8,128]{1,0:T(8,128)}) custom-call(bf16[2048,1536]{1,0:T(8,128)(2,1)} %project.1.q_ref.k_ref.v_ref, bf16[2048,1536]{1,0:T(8,128)(2,1)} %project.1.q_ref.k_ref.v_ref, bf16[2048,1536]{1,0:T(8,128)(2,1)} %project.1.q_ref.k_ref.v_ref, ...), custom_call_target="tpu_custom_call", output_to_operand_aliasing={{0}: (8, {})} | custom-call | flops 20999999488 | bytes 16777216 | tf_op jit(solution)/shard_map/attend_back/pallas_call | solution.py:215
  500.6 23.4 %attend_back.6 = (bf16[2048,1536]{1,0:T(8,128)(2,1)}, f32[8,128]{1,0:T(8,128)}) custom-call(bf16[2048,1536]{1,0:T(8,128)(2,1)} %project.1.q_ref.k_ref.v_ref, bf16[2048,1536]{1,0:T(8,128)(2,1)} %project.1.q_ref.k_ref.v_ref, bf16[2048,1536]{1,0:T(8,128)(2,1)} %project.1.q_ref.k_ref.v_ref, ...), custom_call_target="tpu_custom_call", output_to_operand_aliasing={{0}: (8, {})} | custom-call | flops 20999999488 | bytes 16777216 | tf_op jit(solution)/shard_map/attend_back/pallas_call | solution.py:215
  524.1 9.9 %proj_grad.2.refs_2_ = bf16[4,4,64,1152]{3,2,1,0:T(8,128)(2,1)} custom-call(bf16[4,256,1024]{2,1,0:T(8,128)(2,1)} %tie.11.xm_ref.x_ref, bf16[4,256,1024]{2,1,0:T(8,128)(2,1)} %collective-permute-done.3.xt_ref, bf16[2048,1536]{1,0:T(8,128)(2,1)} %get-tuple-element.88.grad_ref.rest_0_), custom_call_target="tpu_custom_call" | custom-call | flops 100000000 | bytes 65536 | tf_op jit(solution)/shard_map/proj_grad/pallas_call | solution.py:615
  538.1 4.8 reduce_sum.76.rest_1_
  549.1 23.7 %attend_back.7 = (bf16[2048,1536]{1,0:T(8,128)(2,1)}, f32[8,128]{1,0:T(8,128)}) custom-call(bf16[2048,1536]{1,0:T(8,128)(2,1)} %project.1.q_ref.k_ref.v_ref, bf16[2048,1536]{1,0:T(8,128)(2,1)} %project.1.q_ref.k_ref.v_ref, bf16[2048,1536]{1,0:T(8,128)(2,1)} %project.1.q_ref.k_ref.v_ref, ...), custom_call_target="tpu_custom_call", output_to_operand_aliasing={{0}: (8, {})} | custom-call | flops 20999999488 | bytes 16777216 | tf_op jit(solution)/shard_map/attend_back/pallas_call | solution.py:215
  581.0 7.4 %token_grad.2.refs_1_ = bf16[1024,1024]{1,0:T(8,128)(2,1)} custom-call(s32[1]{0:T(128)} %bitcast.17.chip_ref, bf16[2048,1536]{1,0:T(8,128)(2,1)} %tie.18.grad_ref, bf16[1024,1536]{1,0:T(8,128)(2,1)} %get-tuple-element.55.w_ref), custom_call_target="tpu_custom_call" | custom-call | flops 100000000 | bytes 65536 | tf_op jit(solution)/shard_map/token_grad/pallas_call | solution.py:538
  593.3 6.2 proj_grad.3.refs_2_
  605.5 8.8 %token_grad.3.refs_3_.refs_0_ = bf16[1024,1024]{1,0:T(8,128)(2,1)} custom-call(s32[1]{0:T(128)} %bitcast.17.chip_ref, bf16[2048,1536]{1,0:T(8,128)(2,1)} %tie.18.grad_ref, bf16[1024,1536]{1,0:T(8,128)(2,1)} %get-tuple-element.55.w_ref, f32[1024,1024]{1,0:T(8,128)} %get-tuple-element.92.refs_0_, bf16[1024,1024]{1,0:T(8,128)(2,1)} %copy-done.13, ...), custom_call_target="tpu_custom_call" | custom-call | flops 100000000 | bytes 65536 | tf_op jit(solution)/shard_map/token_grad/pallas_call | solution.py:538
  618.8 5.2 all-to-all-start.7
  629.7 11.0 %collective-permute-done.20.refs_1_ = bf16[64,1664]{1,0:T(8,128)(2,1)S(1)} collective-permute-done((bf16[64,1664]{1,0:T(8,128)(2,1)S(1)}, bf16[64,1664]{1,0:T(8,128)(2,1)S(1)}, u32[]{:S(2)}, u32[]{:S(2)}) %collective-permute-start.20) | collective-permute-done | bytes 213024 | tf_op jit(solution)/shard_map/ppermute | solution.py:689
  (307 shorter events, 127.5 us)
Async XLA Ops:
  7.3 27.8 %all-to-all-start = ((bf16[4,256,1024]{2,1,0:T(8,128)(2,1)}), bf16[4,256,1024]{2,1,0:T(8,128)(2,1)S(1)}, u32[]{:S(2)}, u32[]{:S(2)}) async-start(bf16[4,256,1024]{2,1,0:T(8,128)(2,1)} %param.18), calls=%async_computation | async-start | bytes 4194304 | tf_op jit(solution)/shard_map/all_to_all | solution.py:699
  11.7 199.3 %all-gather.3.cloned.1.call-start = ((), (), s32[]{:S(2)}) async-start(), calls=%async_computation.8 | async-start | bytes 10813440 | tf_op jit(solution)/shard_map/all_gather | solution.py:867
  12.9 15.9 %collective-permute-start = (bf16[32,3200]{1,0:T(8,128)(2,1)S(1)}, bf16[32,3200]{1,0:T(8,128)(2,1)S(1)}, u32[]{:S(2)}, u32[]{:S(2)}) collective-permute-start(bf16[32,3200]{1,0:T(8,128)(2,1)S(1)} %get-tuple-element.123), channel_id=1, source_target_pairs={{0,8},{8,16},{16,24},{24,0},{1,9},{9,17},{17,25},{25,1},{2,10},{10... | collective-permute-start | bytes 614408 | tf_op jit(solution)/shard_map/ppermute | solution.py:689
  14.6 17.1 %collective-permute-start.1 = (bf16[32,3200]{1,0:T(8,128)(2,1)S(1)}, bf16[32,3200]{1,0:T(8,128)(2,1)S(1)}, u32[]{:S(2)}, u32[]{:S(2)}) collective-permute-start(bf16[32,3200]{1,0:T(8,128)(2,1)S(1)} %get-tuple-element.123), channel_id=1, source_target_pairs={{0,16},{8,24},{16,0},{24,8},{1,17},{9,25},{17,1},{25,9},{2,18},{10... | collective-permute-start | bytes 614408 | tf_op jit(solution)/shard_map/ppermute | solution.py:689
  15.8 17.6 %collective-permute-start.2 = (bf16[32,3200]{1,0:T(8,128)(2,1)S(1)}, bf16[32,3200]{1,0:T(8,128)(2,1)S(1)}, u32[]{:S(2)}, u32[]{:S(2)}) collective-permute-start(bf16[32,3200]{1,0:T(8,128)(2,1)S(1)} %get-tuple-element.123), channel_id=1, source_target_pairs={{0,24},{8,0},{16,8},{24,16},{1,25},{9,1},{17,9},{25,17},{2,26},{10... | collective-permute-start | bytes 614408 | tf_op jit(solution)/shard_map/ppermute | solution.py:689
  39.2 207.8 %all-gather.5.cloned.1.call-start = ((), (), s32[]{:S(2)}) async-start(), calls=%async_computation.9 | async-start | bytes 8650752 | tf_op jit(solution)/shard_map/all_gather | solution.py:867
  94.6 18.2 %collective-permute-start.3 = (bf16[4,256,1024]{2,1,0:T(8,128)(2,1)S(1)}, bf16[4,256,1024]{2,1,0:T(8,128)(2,1)}, u32[]{:S(2)}, u32[]{:S(2)}) collective-permute-start(bf16[4,256,1024]{2,1,0:T(8,128)(2,1)S(1)} %copy-done.1), channel_id=1, source_target_pairs={{0,1},{1,0},{2,3},{3,2},{4,5},{5,4},{6,7},{7,6},{8,9},{9,8},{10,11... | collective-permute-start | bytes 6291464 | tf_op jit(solution)/shard_map/ppermute | solution.py:684
  159.6 51.3 %collective-permute-start.5 = (bf16[1024,256]{1,0:T(8,128)(2,1)S(1)}, bf16[1024,256]{1,0:T(8,128)(2,1)}, u32[]{:S(2)}, u32[]{:S(2)}) collective-permute-start(bf16[1024,256]{1,0:T(8,128)(2,1)S(1)} %slice.156), channel_id=1, source_target_pairs={{0,1},{1,0},{2,3},{3,2},{4,5},{5,4},{6,7},{7,6},{8,9},{9,8},{10,11... | collective-permute-start | bytes 1572872 | tf_op jit(solution)/shard_map/ppermute | solution.py:684
  194.7 16.2 %collective-permute-start.6 = (bf16[1024,256]{1,0:T(8,128)(2,1)S(1)}, bf16[1024,256]{1,0:T(8,128)(2,1)}, u32[]{:S(2)}, u32[]{:S(2)}) collective-permute-start(bf16[1024,256]{1,0:T(8,128)(2,1)S(1)} %slice.157), channel_id=1, source_target_pairs={{0,1},{1,0},{2,3},{3,2},{4,5},{5,4},{6,7},{7,6},{8,9},{9,8},{10,11... | collective-permute-start | bytes 1572872 | tf_op jit(solution)/shard_map/ppermute | solution.py:684
  203.0 43.9 %all-to-all-start.2 = ((bf16[4,256,1024]{2,1,0:T(8,128)(2,1)}), bf16[4,256,1024]{2,1,0:T(8,128)(2,1)S(1)}, u32[]{:S(2)}, u32[]{:S(2)}) async-start(bf16[4,256,1024]{2,1,0:T(8,128)(2,1)} %broadcast_add_fusion), calls=%async_computation.2 | async-start | bytes 4194304 | tf_op jit(solution)/shard_map/all_to_all | solution.py:699
  291.6 32.2 %collective-permute-start.8 = (bf16[4,4,256,512]{3,2,1,0:T(8,128)(2,1)}, bf16[4,4,256,512]{3,2,1,0:T(8,128)(2,1)}, u32[]{:S(2)}, u32[]{:S(2)}) collective-permute-start(bf16[4,4,256,512]{3,2,1,0:T(8,128)(2,1)} %weight_grad.4), channel_id=1, source_target_pairs={{0,1},{1,0},{2,3},{3,2},{4,5},{5,4},{6,7},{7,6},{8,9},{9,8},{10,11... | collective-permute-start | bytes 12582920 | tf_op jit(solution)/shard_map/ppermute | solution.py:684
  292.3 31.5 %all-to-all-start.3 = ((bf16[4,256,1024]{2,1,0:T(8,128)(2,1)}), bf16[4,256,1024]{2,1,0:T(8,128)(2,1)S(1)}, u32[]{:S(2)}, u32[]{:S(2)}) async-start(bf16[4,256,1024]{2,1,0:T(8,128)(2,1)} %bitcast.132), calls=%async_computation.3 | async-start | bytes 4194304 | tf_op jit(solution)/shard_map/all_to_all | solution.py:699
  346.6 34.0 %collective-permute-start.9 = (bf16[4,4,64,2560]{3,2,1,0:T(8,128)(2,1)}, bf16[4,4,64,2560]{3,2,1,0:T(8,128)(2,1)}, u32[]{:S(2)}, u32[]{:S(2)}) collective-permute-start(bf16[4,4,64,2560]{3,2,1,0:T(8,128)(2,1)} %weight_grad.6), channel_id=1, source_target_pairs={{0,1},{1,0},{2,3},{3,2},{4,5},{5,4},{6,7},{7,6},{8,9},{9,8},{10,11... | collective-permute-start | bytes 15728648 | tf_op jit(solution)/shard_map/ppermute | solution.py:684
  346.6 9.6 %collective-permute-start.7 = (bf16[1024,512]{1,0:T(8,128)(2,1)S(1)}, bf16[1024,512]{1,0:T(8,128)(2,1)S(1)}, u32[]{:S(2)}, u32[]{:S(2)}) collective-permute-start(bf16[1024,512]{1,0:T(8,128)(2,1)S(1)} %copy-done.39), channel_id=1, source_target_pairs={{0,1},{1,0},{2,3},{3,2},{4,5},{5,4},{6,7},{7,6},{8,9},{9,8},{10,11... | collective-permute-start | bytes 3145736 | tf_op jit(solution)/shard_map/ppermute | solution.py:684
  347.2 52.0 %all-to-all-start.4 = ((bf16[4,4,256,512]{3,2,1,0:T(8,128)(2,1)}), bf16[4,4,256,512]{3,2,1,0:T(8,128)(2,1)}, u32[]{:S(2)}, u32[]{:S(2)}) async-start(bf16[4,4,256,512]{3,2,1,0:T(8,128)(2,1)} %weight_grad.5.refs_4_), calls=%async_computation.4 | async-start | bytes 8388608 | tf_op jit(solution)/shard_map/all_to_all | solution.py:699
  399.1 134.8 %all-to-all-start.5 = ((bf16[4,4,64,2688]{3,2,1,0:T(8,128)(2,1)}), bf16[4,4,64,2688]{3,2,1,0:T(8,128)(2,1)}, u32[]{:S(2)}, u32[]{:S(2)}) async-start(bf16[4,4,64,2688]{3,2,1,0:T(8,128)(2,1)} %weight_grad.7.refs_2_), calls=%async_computation.5 | async-start | bytes 11010048 | tf_op jit(solution)/shard_map/all_to_all | solution.py:699
  409.0 88.8 %collective-permute-start.10 = (bf16[256,512]{1,0:T(8,128)(2,1)S(1)}, bf16[256,512]{1,0:T(8,128)(2,1)S(1)}, u32[]{:S(2)}, u32[]{:S(2)}) collective-permute-start(bf16[256,512]{1,0:T(8,128)(2,1)S(1)} %get-tuple-element.112), channel_id=1, source_target_pairs={{0,8},{8,16},{16,24},{24,0},{1,9},{9,17},{17,25},{25,1},{2,10},{10... | collective-permute-start | bytes 786440 | tf_op jit(solution)/shard_map/ppermute | solution.py:689
  447.5 50.3 %collective-permute-start.11 = (bf16[256,512]{1,0:T(8,128)(2,1)S(1)}, bf16[256,512]{1,0:T(8,128)(2,1)S(1)}, u32[]{:S(2)}, u32[]{:S(2)}) collective-permute-start(bf16[256,512]{1,0:T(8,128)(2,1)S(1)} %get-tuple-element.110), channel_id=1, source_target_pairs={{0,16},{8,24},{16,0},{24,8},{1,17},{9,25},{17,1},{25,9},{2,18},{10... | collective-permute-start | bytes 786440 | tf_op jit(solution)/shard_map/ppermute | solution.py:689
  474.3 23.5 %collective-permute-start.12 = (bf16[256,512]{1,0:T(8,128)(2,1)S(1)}, bf16[256,512]{1,0:T(8,128)(2,1)S(1)}, u32[]{:S(2)}, u32[]{:S(2)}) collective-permute-start(bf16[256,512]{1,0:T(8,128)(2,1)S(1)} %get-tuple-element.111), channel_id=1, source_target_pairs={{0,24},{8,0},{16,8},{24,16},{1,25},{9,1},{17,9},{25,17},{2,26},{10... | collective-permute-start | bytes 786440 | tf_op jit(solution)/shard_map/ppermute | solution.py:689
  533.9 38.9 %all-to-all-start.6 = ((bf16[4,4,64,1152]{3,2,1,0:T(8,128)(2,1)}), bf16[4,4,64,1152]{3,2,1,0:T(8,128)(2,1)S(1)}, u32[]{:S(2)}, u32[]{:S(2)}) async-start(bf16[4,4,64,1152]{3,2,1,0:T(8,128)(2,1)} %proj_grad.2.refs_2_), calls=%async_computation.6 | async-start | bytes 4718592 | tf_op jit(solution)/shard_map/all_to_all | solution.py:699
  545.2 32.1 %collective-permute-start.13 = (bf16[64,2688]{1,0:T(8,128)(2,1)}, bf16[64,2688]{1,0:T(8,128)(2,1)S(1)}, u32[]{:S(2)}, u32[]{:S(2)}) collective-permute-start(bf16[64,2688]{1,0:T(8,128)(2,1)} %get-tuple-element.106), channel_id=1, source_target_pairs={{0,8},{8,16},{16,24},{24,0},{1,9},{9,17},{17,25},{25,1},{2,10},{10... | collective-permute-start | bytes 1032200 | tf_op jit(solution)/shard_map/ppermute | solution.py:689
  547.3 29.9 %collective-permute-start.14 = (bf16[64,2688]{1,0:T(8,128)(2,1)}, bf16[64,2688]{1,0:T(8,128)(2,1)S(1)}, u32[]{:S(2)}, u32[]{:S(2)}) collective-permute-start(bf16[64,2688]{1,0:T(8,128)(2,1)} %get-tuple-element.104), channel_id=1, source_target_pairs={{0,16},{8,24},{16,0},{24,8},{1,17},{9,25},{17,1},{25,9},{2,18},{10... | collective-permute-start | bytes 1032200 | tf_op jit(solution)/shard_map/ppermute | solution.py:689
  549.1 28.2 %collective-permute-start.15 = (bf16[64,2688]{1,0:T(8,128)(2,1)}, bf16[64,2688]{1,0:T(8,128)(2,1)S(1)}, u32[]{:S(2)}, u32[]{:S(2)}) collective-permute-start(bf16[64,2688]{1,0:T(8,128)(2,1)} %get-tuple-element.105), channel_id=1, source_target_pairs={{0,24},{8,0},{16,8},{24,16},{1,25},{9,1},{17,9},{25,17},{2,26},{10... | collective-permute-start | bytes 1032200 | tf_op jit(solution)/shard_map/ppermute | solution.py:689
  588.4 15.8 %collective-permute-start.16 = (bf16[1024,1024]{1,0:T(8,128)(2,1)}, bf16[1024,1024]{1,0:T(8,128)(2,1)S(1)}, u32[]{:S(2)}, u32[]{:S(2)}) collective-permute-start(bf16[1024,1024]{1,0:T(8,128)(2,1)} %token_grad.2.refs_1_), channel_id=1, source_target_pairs={{0,1},{1,0},{2,3},{3,2},{4,5},{5,4},{6,7},{7,6},{8,9},{9,8},{10,11... | collective-permute-start | bytes 6291464 | tf_op jit(solution)/shard_map/ppermute | solution.py:684
  600.6 13.7 %collective-permute-start.17 = (bf16[4,64,512]{2,1,0:T(8,128)(2,1)S(1)}, bf16[4,64,512]{2,1,0:T(8,128)(2,1)S(1)}, u32[]{:S(2)}, u32[]{:S(2)}) collective-permute-start(bf16[4,64,512]{2,1,0:T(8,128)(2,1)S(1)} %get-tuple-element.109), channel_id=1, source_target_pairs={{0,2},{1,3},{2,0},{3,1},{4,6},{5,7},{6,4},{7,5},{8,10},{9,11},{10,... | collective-permute-start | bytes 786440 | tf_op jit(solution)/shard_map/ppermute | solution.py:684
  601.3 14.1 %collective-permute-start.18 = (bf16[4,64,512]{2,1,0:T(8,128)(2,1)S(1)}, bf16[4,64,512]{2,1,0:T(8,128)(2,1)S(1)}, u32[]{:S(2)}, u32[]{:S(2)}) collective-permute-start(bf16[4,64,512]{2,1,0:T(8,128)(2,1)S(1)} %get-tuple-element.107), channel_id=1, source_target_pairs={{0,4},{1,5},{2,6},{3,7},{4,0},{5,1},{6,2},{7,3},{8,12},{9,13},{10,... | collective-permute-start | bytes 786440 | tf_op jit(solution)/shard_map/ppermute | solution.py:684
  601.4 14.0 %collective-permute-start.19 = (bf16[4,64,512]{2,1,0:T(8,128)(2,1)S(1)}, bf16[4,64,512]{2,1,0:T(8,128)(2,1)S(1)}, u32[]{:S(2)}, u32[]{:S(2)}) collective-permute-start(bf16[4,64,512]{2,1,0:T(8,128)(2,1)S(1)} %get-tuple-element.108), channel_id=1, source_target_pairs={{0,6},{1,7},{2,4},{3,5},{4,2},{5,3},{6,0},{7,1},{8,14},{9,15},{10,... | collective-permute-start | bytes 786440 | tf_op jit(solution)/shard_map/ppermute | solution.py:684
  618.8 27.8 %all-to-all-start.7 = ((bf16[4,256,1024]{2,1,0:T(8,128)(2,1)}), bf16[4,256,1024]{2,1,0:T(8,128)(2,1)S(1)}, u32[]{:S(2)}, u32[]{:S(2)}) async-start(bf16[4,256,1024]{2,1,0:T(8,128)(2,1)} %bitcast.127), calls=%async_computation.7 | async-start | bytes 4194304 | tf_op jit(solution)/shard_map/all_to_all | solution.py:699
  624.1 16.6 %collective-permute-start.20 = (bf16[64,1664]{1,0:T(8,128)(2,1)S(1)}, bf16[64,1664]{1,0:T(8,128)(2,1)S(1)}, u32[]{:S(2)}, u32[]{:S(2)}) collective-permute-start(bf16[64,1664]{1,0:T(8,128)(2,1)S(1)} %get-tuple-element.114), channel_id=1, source_target_pairs={{0,8},{8,16},{16,24},{24,0},{1,9},{9,17},{17,25},{25,1},{2,10},{10... | collective-permute-start | bytes 638984 | tf_op jit(solution)/shard_map/ppermute | solution.py:689
  626.0 17.1 %collective-permute-start.21 = (bf16[64,1664]{1,0:T(8,128)(2,1)S(1)}, bf16[64,1664]{1,0:T(8,128)(2,1)S(1)}, u32[]{:S(2)}, u32[]{:S(2)}) collective-permute-start(bf16[64,1664]{1,0:T(8,128)(2,1)S(1)} %get-tuple-element.113), channel_id=1, source_target_pairs={{0,16},{8,24},{16,0},{24,8},{1,17},{9,25},{17,1},{25,9},{2,18},{10... | collective-permute-start | bytes 638984 | tf_op jit(solution)/shard_map/ppermute | solution.py:689
  629.0 16.7 %collective-permute-start.22 = (bf16[64,1664]{1,0:T(8,128)(2,1)S(1)}, bf16[64,1664]{1,0:T(8,128)(2,1)}, u32[]{:S(2)}, u32[]{:S(2)}) collective-permute-start(bf16[64,1664]{1,0:T(8,128)(2,1)S(1)} %get-tuple-element.115), channel_id=1, source_target_pairs={{0,24},{8,0},{16,8},{24,16},{1,25},{9,1},{17,9},{25,17},{2,26},{10... | collective-permute-start | bytes 638984 | tf_op jit(solution)/shard_map/ppermute | solution.py:689
  629.6 19.6 %collective-permute-start.24 = (bf16[128,512]{1,0:T(8,128)(2,1)}, bf16[128,512]{1,0:T(8,128)(2,1)}, u32[]{:S(2)}, u32[]{:S(2)}) collective-permute-start(bf16[128,512]{1,0:T(8,128)(2,1)} %dynamic-slice_bitcast_fusion.9), channel_id=1, source_target_pairs={{0,1},{1,0},{2,3},{3,2},{4,5},{5,4},{6,7},{7,6},{8,9},{9,8},{10,11... | collective-permute-start | bytes 393224 | tf_op jit(solution)/shard_map/ppermute | solution.py:684
  (51 other events, 366.2 us)
Sparse Core Ops, SparseCore 0:
  39.3 100.9 all-gather.2
  143.2 76.2 all-gather.4

commit v3 on v2

--- a/solution.py
+++ b/solution.py
@@ -31,14 +31,14 @@
     return pltpu.CompilerParams(vmem_limit_bytes=VMEM_LIMIT)
 
 
-def shard_copies(refs, order_ref, cols, target, sems, base=0, turn=None):
+def shard_copies(refs, order_ref, cols, target, sems, base=0, turn=None, every=1, skip=0):
     copies = []
     total = target.shape[0]
     for ref in refs:
         rows = ref.shape[1]
         for n in range(ref.shape[0]):
             index = len(copies)
-            row = order_ref[index] * rows
+            row = (order_ref[index] * every + skip) * rows
             if turn is not None:
                 row = lax.rem(row + turn, total)
             row = pl.multiple_of(row, TILE)
@@ -48,6 +48,38 @@
 
 def shards_of(pieces):
     return sum(piece.shape[0] for piece in pieces)
+
+
+def pack_kernel(wq_ref, wk_ref, wv_ref, wo_ref, wu_ref, wd_ref, vec_ref, proj_ref, up_ref, *down):
+    rows, d = wq_ref.shape
+    ff = wu_ref.shape[1]
+    for n, (ref, scale) in enumerate(((wq_ref, QSCALE), (wk_ref, None), (wv_ref, None))):
+        for pair in range(d // 128):
+            part = ref[:, pair * 128 : (pair + 1) * 128]
+            part = part if scale is None else part * scale
+            proj_ref[:, pair * 384 + n * 128 : pair * 384 + (n + 1) * 128] = part.astype(BF)
+    proj_ref[:, 3 * d :] = vec_ref[...]
+    up_ref[:, 0:d] = wo_ref[...].astype(BF)
+    up_ref[:, d : d + ff] = wu_ref[...].astype(BF)
+    if down:
+        down[0][...] = wd_ref[...].astype(BF)
+    else:
+        for n in range(wd_ref.shape[0] // rows):
+            up_ref[:, d + ff + n * d : d + ff + (n + 1) * d] = wd_ref[n * rows : (n + 1) * rows, :].astype(BF)
+
+
+def pack(w_query, w_key, w_value, w_out, w_up, w_down, vec):
+    rows, d = w_query.shape
+    ff = w_up.shape[1]
+    joined = rows % TILE == 0
+    more = w_down.shape[0] // rows * d if joined else 0
+    shapes = [(rows, 3 * d + vec.shape[1]), (rows, d + ff + more)] + ([] if joined else [w_down.shape])
+    return pl.pallas_call(
+        pack_kernel,
+        out_shape=[jax.ShapeDtypeStruct(shape, BF) for shape in shapes],
+        compiler_params=params(),
+        name="pack",
+    )(w_query, w_key, w_value, w_out, w_up, w_down, vec)
 
 
 def place_kernel(count, width, order_ref, *refs):
@@ -135,7 +167,7 @@
         finish(jnp.concatenate(most, axis=0))
 
 
-def attend(qkv, seg_row, seg_col, base, pairs, held=None, waits=(), block=256, chunk=512):
+def attend(qkv, seg_row, seg_col, base, pairs, held=None, waits=(), block=512, chunk=1024):
     total = qkv.shape[0]
     specs = lambda c: pl.BlockSpec((total, 128), lambda h, i: (0, 3 * (base + h) + c))
     kept = [] if held is None else [held]
@@ -169,7 +201,6 @@
 
 def attend_back_kernel(chunk, extra, q_ref, k_ref, v_ref, o_ref, do_ref, do2_ref, p_ref, l_ref, *rest):
     out_ref, mark_ref, kt_ref, dk_acc, dv_acc = rest[extra:]
-    mark_ref[...] = jnp.zeros_like(mark_ref)
     i = pl.program_id(1)
     total = k_ref.shape[0]
     block = q_ref.shape[0]
@@ -197,18 +228,22 @@
             dv_acc[rows, :] += mm(p.astype(BF), do_parts[h])
             dk_acc[rows, :] += mm(grad_s, q_parts[h])
             grad_q[h] = grad_q[h] + mm(kt_ref[h * HD : h * HD + HD, rows], grad_s)
-    out_ref[pl.ds(pl.multiple_of(i * block, block), block), 0:128] = jnp.concatenate(grad_q, axis=0).T.astype(BF)
+    grad_q = jnp.concatenate(grad_q, axis=0).T.astype(BF)
+    out_ref[pl.ds(pl.multiple_of(i * block, block), block), 0:128] = grad_q
+    add_fold(mark_ref.at[0:8, :], i == 0, grad_q.astype(F32))
 
     @pl.when(i == pl.num_programs(1) - 1)
     def _():
         out_ref[:, 128:256] = dk_acc[...].astype(BF)
-        out_ref[:, 256:384] = dv_acc[...].astype(BF)
-
-
-def attend_back(qkv, out, grad_mine, grad_mate, probs, inverse, base, held=None, waits=(), block=256, chunk=512):
+        grad_v = dv_acc[...].astype(BF)
+        out_ref[:, 256:384] = grad_v
+        mark_ref[8:16, :] = fold(grad_v.astype(F32))
+
+
+def attend_back(qkv, out, grad_mine, grad_mate, probs, inverse, base, held=None, waits=(), block=256, chunk=1024):
     total = qkv.shape[0]
     kept = [] if held is None else [held]
-    pairs = probs.shape[0]
+    pairs, skip = 1, base % probs.shape[0]
     last = total // block // 2 - 1
     whole = lambda c: pl.BlockSpec((total, 128), lambda h, i: (0, 3 * (base + h) + c))
     rows = pl.BlockSpec((block, 128), lambda h, i: (i, base + h))
@@ -222,11 +257,11 @@
             rows,
             pl.BlockSpec((block, 128), lambda h, i: (jnp.minimum(i, last), base + h)),
             pl.BlockSpec((block, 128), lambda h, i: (jnp.maximum(i - last - 1, 0), base + h)),
-            pl.BlockSpec((None, 2, total, block), lambda h, i: (h, 0, 0, i)),
-            pl.BlockSpec((None, 2, block), lambda h, i: (h, 0, i)),
+            pl.BlockSpec((None, 2, total, block), lambda h, i: (skip + h, 0, 0, i)),
+            pl.BlockSpec((None, 2, block), lambda h, i: (skip + h, 0, i)),
         ] + [ANY] * (len(kept) + len(waits)),
-        out_specs=[pl.BlockSpec((total, 384), lambda h, i: (0, base + h)), pl.BlockSpec((8, 128), lambda h, i: (0, 0))],
-        out_shape=[jax.ShapeDtypeStruct(qkv.shape, BF), jax.ShapeDtypeStruct((8, 128), F32)],
+        out_specs=[pl.BlockSpec((total, 384), lambda h, i: (0, base + h)), pl.BlockSpec((16, 128), lambda h, i: (0, 0))],
+        out_shape=[jax.ShapeDtypeStruct(qkv.shape, BF), jax.ShapeDtypeStruct((16, 128), F32)],
         scratch_shapes=[
             pltpu.VMEM((128, total), BF),
             pltpu.VMEM((total, 128), F32),
@@ -240,18 +275,8 @@
 
 
 def gelu_parts(u):
-    scaled = jnp.abs(u) * 0.7071067811865476
-    den = 1.0 + 0.3275911 * scaled
-    t = pl.reciprocal(den, approx=True)
-    t = t * (2.0 - den * t)
-    e = jnp.exp(u * u * -0.5)
-    poly = t * (
-        0.127414796
-        + t * (-0.142248368 + t * (0.7107068705 + t * (-0.7265760135 + t * 0.5307027145)))
-    )
-    tail = poly * e
-    phi = jnp.where(u >= 0, 1.0 - tail, tail)
-    return u * phi, phi + u * (e * 0.3989422804014327)
+    phi = 0.5 + 0.5 * lax.erf(u * 0.7071067811865476)
+    return u * phi, phi + u * (jnp.exp(u * u * -0.5) * 0.3989422804014327)
 
 
 def mean(value):
@@ -390,14 +415,17 @@
     )(order, x, attn, vecs, b_up, *o_mate, *pieces)
 
 
-def mid_down_kernel(step, count, order_ref, g_ref, gp_ref, xh_ref, dy_ref, vec_ref, *refs):
+def mid_down_kernel(step, count, blocks, order_ref, g_ref, gp_ref, xh_ref, dy_ref, vec_ref, *refs):
     pieces, (out_ref, dh_ref, dm_ref, du_ref, s_ref, su_ref, wd_ref, sems) = refs[:count], refs[count:]
     first = pl.program_id(0) == 0
     d = wd_ref.shape[1]
 
     @pl.when(first)
     def _():
-        copies = shard_copies(pieces, order_ref, slice(0, d), wd_ref, sems)
+        copies = []
+        for n in range(blocks[1]):
+            cols = slice(blocks[0] + n * d, blocks[0] + (n + 1) * d)
+            copies += shard_copies(pieces, order_ref, cols, wd_ref, sems, len(copies), None, blocks[1], n)
         for copy in copies:
             copy.start()
         for copy in copies:
@@ -423,14 +451,14 @@
         add_fold(su_ref.at[:, cols], first, du.astype(F32))
 
 
-def mid_down(g, gp, xh, dy, pieces, order, vecs, block=256, step=2048):
+def mid_down(g, gp, xh, dy, pieces, order, blocks, vecs, block=256, step=2048):
     rows, d = xh.shape
     ff = g.shape[1]
     row = lambda n: pl.BlockSpec((block, n), lambda i: (i, 0))
     full = lambda a: pl.BlockSpec(a.shape, lambda i: (0, 0), pipeline_mode=pl.Buffered(1))
     keep = lambda r, n: pl.BlockSpec((r, n), lambda i: (0, 0))
     return pl.pallas_call(
-        functools.partial(mid_down_kernel, step, len(pieces)),
+        functools.partial(mid_down_kernel, step, len(pieces), blocks),
         grid=(rows // block,),
         in_specs=[SMEM, row(ff), row(ff), row(d), row(d), full(vecs)] + [ANY] * len(pieces),
         out_specs=[row(d), row(d), row(d), row(ff), keep(24, d), keep(8, ff)],
@@ -442,7 +470,7 @@
             jax.ShapeDtypeStruct((24, d), F32),
             jax.ShapeDtypeStruct((8, ff), F32),
         ],
-        scratch_shapes=[pltpu.VMEM((ff, d), BF), pltpu.SemaphoreType.DMA((shards_of(pieces),))],
+        scratch_shapes=[pltpu.VMEM((ff, d), BF), pltpu.SemaphoreType.DMA((shards_of(pieces) * blocks[1],))],
         compiler_params=params(),
         cost_estimate=pl.CostEstimate(flops=25 * 10**9, bytes_accessed=44 << 20, transcendentals=0),
         name="mid_down",
@@ -850,24 +878,26 @@
     extra = -(-(vec_size + seqs * span) // (rows * 128)) * 128
     vec_pack = jnp.concatenate([bf(v) for v in vec_names] + [bf(b_up), bf(segments.reshape(-1))])
     vec_pack = jnp.pad(vec_pack, (0, rows * extra - vec_pack.shape[0])).reshape(rows, extra)
-    by_pair = [bf(w).reshape(rows, 2 * pairs, 1, 128) for w in (w_query * QSCALE, w_key, w_value)]
-    pack_proj = jnp.concatenate(
-        [jnp.concatenate(by_pair, axis=2).reshape(rows, 3 * d), vec_pack], axis=1
-    )
+    packed = pack(w_query, w_key, w_value, w_out, w_up, w_down, vec_pack)
 
     got = over_chips(tokens)
     own = chips * span
-    proj = Gather(pack_proj, place_of)
+    proj = Gather(packed[0], place_of)
     turns_of = proj.along_dp(proj.own)
     got = tie(got, *turns_of)
     mate = swap(got, 1)
     later = tick(got)
     held = proj.over_chips(later)
     pieces, order = proj.between_cores()
-    everywhere = lambda v: lax.all_gather(bf(v) + later.astype(BF), BOTH, axis=0, tiled=True).reshape(2, -1, v.shape[1])
-    up_pieces = [everywhere(jnp.concatenate([w_out, w_up], axis=1))]
-    down_pieces = [everywhere(w_down)]
-    down_order = jnp.arange(2, dtype=jnp.int32)
+    def everywhere(value):
+        return lax.all_gather(tie(value, got), BOTH, axis=0, tiled=True).reshape(2, -1, value.shape[1])
+
+    up_pieces = [everywhere(packed[1])]
+    if rows % TILE == 0:
+        down_pieces, blocks = [up_pieces[0].reshape(shards, rows, -1)], (d + ff, w_down.shape[0] // rows)
+    else:
+        down_pieces, blocks = [everywhere(packed[2])], (0, 1)
+    down_order = jnp.arange(down_pieces[0].shape[0], dtype=jnp.int32)
     if proj.whole:
         w_cat = half_cols(pieces[0][0, :, : 3 * d], core)
         vec_block = pieces[0][0, :, 3 * d :]
@@ -887,19 +917,16 @@
     qkv = project(got, mate, span, w_cat, bias_cat)
     seg_row, seg_col = seg.reshape(1, -1), seg.reshape(-1, 1)
 
-    waits = []
     attn, probs, inverse, o_mate = None, [], [], []
-    for n in range(pairs):
-        attn, p, l = attend(qkv, seg_row, seg_col, n, 1, attn, waits)
+    for n in range(0, pairs, 2):
+        attn, p, l = attend(qkv, seg_row, seg_col, n, 2, attn)
         probs.append(p)
         inverse.append(l)
-        waits = []
-        if n % 2 == 1:
-            o_mate.append(swap(attn[own:, (n - 1) * 128 : (n + 1) * 128], 1))
-    dy = over_chips(cotangent + tick(attn).astype(BF)).reshape(own, d)
+        o_mate.append(swap(attn[own:, n * 128 : (n + 2) * 128], 1))
+    dy = over_chips(cotangent + tick(inverse[0]).astype(BF)).reshape(own, d)
     up_order = jnp.stack([jnp.zeros((), jnp.int32), jnp.ones((), jnp.int32), d - core * half]).astype(jnp.int32)
     xh, r, xb, g, gp = mid_up(got, span, attn, o_mate, up_pieces, up_order, vecs, bias_up)
-    out, dh2, dm, du, sums_two, sums_up = mid_down(g, gp, xh, dy, down_pieces, down_order, vecs)
+    out, dh2, dm, du, sums_two, sums_up = mid_down(g, gp, xh, dy, down_pieces, down_order, blocks, vecs)
     result_out = over_chips(out.reshape(chips, span, d))
 
     zero = jnp.zeros((), jnp.int32)
@@ -917,10 +944,11 @@
     per_shard = lambda v: jnp.moveaxis(bf(v).reshape(groups, chips, -1, 128), 1, 0)
     vec_grads = per_shard(spread([one[2], one[0], one[1], two[2], two[0], two[1], fold_rows(sums_up)], shards, rows))
 
-    grads, waits = None, []
+    grads, waits, marks = None, [], []
     for n in range(pairs):
-        grads, mark = attend_back(qkv, attn, do_mine, do_mate, probs[n], inverse[n], n, grads, waits)
+        grads, mark = attend_back(qkv, attn, do_mine, do_mate, probs[n // 2], inverse[n // 2], n, grads, waits)
         waits = []
+        marks.append(mark)
         if n == 0:
             got_up = tie(got_up, mark)
             kept_up = weight_grad(sides, turns(core, zero, shift), groups, chips, [got_up, vec_grads])
@@ -933,23 +961,26 @@
             first = proj_grad(got, mate, span, grads, 0, 3, groups, chips)
             waits = sum_up.chip_sum(mark, first)
             sum_up.along_dp()
-            sum_first = Reduce(first, place_of)
-    grads = tie(grads, *sum_first.chip_sum(mark), *sum_up.dp_sum(mark))
-    bias_sums = jnp.sum(grads.astype(F32), axis=0).reshape(pairs, 3, 128)
+            sum_first = Reduce(tie(first, sum_up.part), place_of)
+    grads = tie(grads, tie(sum_first.got, mark), *[tie(v, mark) for v in sum_up.turns[1:]])
+    bias_sums = jnp.stack([fold_rows(v) for v in marks])
     blank = jnp.zeros((half,), F32)
 
     def whole_vector(c):
         part = bias_sums[:, c].reshape(-1)
         return jnp.where(core == 0, jnp.concatenate([part, blank]), jnp.concatenate([blank, part]))
 
-    bias_grads = per_shard(spread([whole_vector(0), whole_vector(2)], shards, rows))
+    bias_grads = per_shard(spread([whole_vector(0), whole_vector(1)], shards, rows))
     token_send = token_grad(grads, w_cat, 1, (), chip, chips, False)[0]
     token_got = swap(token_send, 1)
     last = proj_grad(got, mate, span, grads, 3, 1, groups, chips, [token_send], bias_grads)
     sum_last = Reduce(last, place_of, True)
     grad_mine = token_grad(grads, w_cat, 0, (dh1, token_got), chip, chips, False, [last])[0]
-    sum_last.chip_sum(grad_mine)
-    grad_mine = tie(grad_mine, sum_last.part)
+    arrived = sum_last.got[1:]
+    grad_mine = tie(grad_mine, *arrived)
+    sum_last.chip_sum()
+    sum_first.chip_sum(*arrived)
+    sum_up.dp_sum(*arrived)
     grad_tokens = over_chips(grad_mine.reshape(chips, span, d))
     sum_last.part = jnp.concatenate([sum_first.part, sum_last.part], axis=2)
     sum_last.along_dp()

time: 668 us -> 642 us (0.961); the launches traced: 668 us -> 632 us
  Pallas kernels: 347 us -> 330 us
  other arithmetic: 41 us -> 28.3 us
  starting transfers between devices: 123 us -> 112 us
    ppermute x12, starting transfers between devices: 78.9 us -> 44.5 us  [along(): lax.ppermute(value, 'dp', [(s, (s + step) % count) for s in range(count)])]
    all_to_all x7, starting transfers between devices: 36.8 us -> 58.5 us  [over_chips(): return lax.all_to_all(value, 'ctx', 0, 0, axis_index_groups=groups)]
    pallas_call x1, Pallas kernels: 35.9 us -> 26.6 us  [mid_up(): pl.pallas_call(functools.partial(mid_up_kernel, step, len(pieces), len(o_...]
    pallas_call x4 -> x2, Pallas kernels: 67.4 us -> 60.5 us  [attend(): pl.pallas_call(functools.partial(attend_kernel, chunk, len(waits) + len(k...]
    unnamed x108 -> x130, local copies, waits for them, and re-layouts: 19.1 us -> 23.1 us
    pallas_call x1 -> x2, Pallas kernels: 33.6 us -> 37.1 us  [the longest x1 34.7 us: mid_down(): pl.pallas_call(functools.partial(mid_down_kernel, step, len(pieces), bloc...]
  transfers between devices with their start and end apart: 34 -> 33, of which waited for: 12 -> 10; matrix products, arithmetic and copies ran while one was open for 7% -> 6% of each run, Pallas kernels for 41% -> 41%
where the time goes in v3:
time: 642 us; the launch traced here: 632 us
  Pallas kernels  330 us (51%)
  starting transfers between devices  112 us (17%)
  blocking collectives  53.1 us (8%)
  waiting for transfers between devices  51.4 us (8%)
  local copies, waits for them, and re-layouts  40.6 us (6%)
  other arithmetic  28.3 us (4%)
  between operations  16.9 us (3%)
    pallas_call x4, Pallas kernels, attend_back(): pl.pallas_call(functools.partial(attend_back_kernel, chunk, len(waits) +...  90.7 us
    pallas_call x2, Pallas kernels, attend(): pl.pallas_call(functools.partial(attend_kernel, chunk, len(waits) + len(k...  60.5 us
    all_to_all x7, starting transfers between devices, over_chips(): return lax.all_to_all(value, 'ctx', 0, 0, axis_index_groups=groups)  58.5 us
    all_to_all x1, blocking collectives, over_chips(): return lax.all_to_all(value, 'ctx', 0, 0, axis_index_groups=groups)  53.1 us
    ppermute x12, starting transfers between devices, along(): lax.ppermute(value, 'dp', [(s, (s + step) % count) for s in range(count)])  44.5 us
    pallas_call x4, Pallas kernels, weight_grad(): pl.pallas_call(functools.partial(weight_kernel, len(adds), len(waits)), g...  43.2 us
    pallas_call x1, Pallas kernels, mid_down(): pl.pallas_call(functools.partial(mid_down_kernel, step, len(pieces), bloc...  34.7 us
    ppermute x12, waiting for transfers between devices, along(): lax.ppermute(value, 'dp', [(s, (s + step) % count) for s in range(count)])  33.3 us
  transfers between devices with their start and end apart: 33, of which 10 were waited for; matrix products, arithmetic and copies ran while one was open for 6% of the time, Pallas kernels for 41%

profile of v3, /device:TPU:14, one launch (start us, length us, event | category | flops | bytes accessed | tf_op | source)
XLA Modules:
  0.0 632.2 jit_solution(17446206513977810854)
XLA Ops:
  7.3 4.3 all-to-all-start
  19.5 11.6 %collective-permute-done.refs_1_ = bf16[32,3200]{1,0:T(8,128)(2,1)S(1)} collective-permute-done((bf16[32,3200]{1,0:T(8,128)(2,1)}, bf16[32,3200]{1,0:T(8,128)(2,1)S(1)}, u32[]{:S(2)}, u32[]{:S(2)}) %collective-permute-start) | collective-permute-done | bytes 204832 | tf_op jit(solution)/shard_map/ppermute | solution.py:717
  40.8 53.1 %all_to_all.40 = bf16[4,4,32,3200]{3,2,1,0:T(8,128)(2,1)} all-to-all(bf16[4,4,32,3200]{3,2,1,0:T(8,128)(2,1)S(1)} %broadcast_in_dim.4), channel_id=1, replica_groups={{0,2,4,6},{1,3,5,7},{8,10,12,14},{9,11,13,15},{16,18,20,22},{17,19,21,2..., dimensions={0} | all-to-all | bytes 6553600 | tf_op jit(solution)/shard_map/all_to_all | solution.py:727
  95.3 7.8 %collective-permute-done.4.refs_1_ = bf16[16,32,3200]{2,1,0:T(8,128)(2,1)} collective-permute-done((bf16[16,32,3200]{2,1,0:T(8,128)(2,1)}, bf16[16,32,3200]{2,1,0:T(8,128)(2,1)}, u32[]{:S(2)}, u32[]{:S(2)}) %collective-permute-start.4) | collective-permute-done | bytes 3276832 | tf_op jit(solution)/shard_map/ppermute | solution.py:712
  103.1 5.0 place.1
  111.6 12.3 %project.1.q_ref.k_ref.v_ref = bf16[2048,1536]{1,0:T(8,128)(2,1)} custom-call(bf16[4,256,1024]{2,1,0:T(8,128)(2,1)} %tie.17.xm_ref.refs_1_.x_ref, bf16[4,256,1024]{2,1,0:T(8,128)(2,1)} %collective-permute-done.3.xt_ref, bf16[1024,1536]{1,0:T(8,128)(2,1)} %get-tuple-element.52.w_ref, f32[1,1536]{1,0:T(1,128)} %constant_dynamic-slice_fusion.2.b_ref), custom_call_target="tpu_custom_call" | custom-call | flops 7000000000 | bytes 14680064 | tf_op jit(solution)/shard_map/project/pallas_call | solution.py:327
  123.9 28.2 %attend.2 = (bf16[2048,512]{1,0:T(8,128)(2,1)}, bf16[2,2,2048,2048]{3,2,1,0:T(8,128)(2,1)}, f32[2,2,2048]{2,1,0:T(2,128)}) custom-call(bf16[2048,1536]{1,0:T(8,128)(2,1)} %project.1.q_ref.k_ref.v_ref, bf16[2048,1536]{1,0:T(8,128)(2,1)} %project.1.q_ref.k_ref.v_ref, bf16[2048,1536]{1,0:T(8,128)(2,1)} %project.1.q_ref.k_ref.v_ref, s32[1,2048]{1,0:T(1,128)} %bitcast.165, ...), custom_call_target="tpu_custom_call" | custom-call | flops 24000000000 | bytes 33554432 | tf_op jit(solution)/shard_map/attend/pallas_call | solution.py:174
  157.2 32.3 %attend.3 = (bf16[2048,512]{1,0:T(8,128)(2,1)}, bf16[2,2,2048,2048]{3,2,1,0:T(8,128)(2,1)}, f32[2,2,2048]{2,1,0:T(2,128)}) custom-call(bf16[2048,1536]{1,0:T(8,128)(2,1)} %project.1.q_ref.k_ref.v_ref, bf16[2048,1536]{1,0:T(8,128)(2,1)} %project.1.q_ref.k_ref.v_ref, bf16[2048,1536]{1,0:T(8,128)(2,1)} %project.1.q_ref.k_ref.v_ref, ...), custom_call_target="tpu_custom_call", output_to_operand_aliasing={{0}: (5, {})} | custom-call | flops 24000000000 | bytes 33554432 | tf_op jit(solution)/shard_map/attend/pallas_call | solution.py:174
  196.4 28.8 %all-to-all-start.2 = ((bf16[4,256,1024]{2,1,0:T(8,128)(2,1)}), bf16[4,256,1024]{2,1,0:T(8,128)(2,1)S(1)}, u32[]{:S(2)}, u32[]{:S(2)}) async-start(bf16[4,256,1024]{2,1,0:T(8,128)(2,1)} %broadcast_add_fusion), calls=%async_computation.2 | async-start | bytes 4194304 | tf_op jit(solution)/shard_map/all_to_all | solution.py:727
  225.9 26.6 %mid_up.1 = (f32[1024,1024]{1,0:T(8,128)}, f32[1024,1]{1,0:T(8,128)}, bf16[1024,1024]{1,0:T(8,128)(2,1)}, bf16[1024,4096]{1,0:T(8,128)(2,1)}, bf16[1024,4096]{1,0:T(8,128)(2,1)}) custom-call(s32[3]{0:T(128)} %pad_add_fusion.4.order_ref, bf16[4,256,1024]{2,1,0:T(8,128)(2,1)} %tie.17.xm_ref.refs_1_.x_ref, bf16[2048,512]{1,0:T(8,128)(2,1)} %get-tuple-element.55.om_ref.o_ref, ...), custom_call_target="tpu_custom_call" | custom-call | flops 20000000000 | bytes 37748736 | tf_op jit(solution)/shard_map/mid_up/pallas_call | solution.py:393
  253.9 34.7 %mid_down.1 = (bf16[1024,1024]{1,0:T(8,128)(2,1)}, f32[1024,1024]{1,0:T(8,128)}, bf16[1024,1024]{1,0:T(8,128)(2,1)}, bf16[1024,4096]{1,0:T(8,128)(2,1)}, f32[24,1024]{1,0:T(8,128)}, /*index=5*/f32[8,4096]{1,0:T(8,128)}) custom-call(s32[32]{0:T(128)} %iota.13.order_ref, bf16[1024,4096]{1,0:T(8,128)(2,1)} %get-tuple-element.57.g_ref.refs_0_, ...), custom_call_target="tpu_custom_call" | custom-call | flops 24999999488 | bytes 46137344 | tf_op jit(solution)/shard_map/mid_down/pallas_call | solution.py:460
  288.6 9.6 %weight_grad.4 = bf16[4,4,256,512]{3,2,1,0:T(8,128)(2,1)} custom-call(s32[2]{0:T(128)} %pad_add_fusion.turn_ref, bf16[1024,4096]{1,0:T(8,128)(2,1)} %get-tuple-element.57.g_ref.refs_0_, bf16[1024,1024]{1,0:T(8,128)(2,1)} %get-tuple-element.71.refs_1_), custom_call_target="tpu_custom_call" | custom-call | flops 4294967296 | bytes 20971520 | tf_op jit(solution)/shard_map/weight_grad/pallas_call | solution.py:698
  298.7 4.4 all-to-all-start.3
  307.9 22.4 %mid_back.1 = (f32[1024,1024]{1,0:T(8,128)}, bf16[1024,1024]{1,0:T(8,128)(2,1)}, bf16[1024,512]{1,0:T(8,128)(2,1)}, bf16[1024,512]{1,0:T(8,128)(2,1)}, f32[24,1024]{1,0:T(8,128)}) custom-call(s32[3]{0:T(128)} %pad_add_fusion.4.order_ref, f32[1024,1024]{1,0:T(8,128)} %get-tuple-element.62.dh_ref, bf16[1024,4096]{1,0:T(8,128)(2,1)} %get-tuple-element.63.du_ref.refs_1_, ...), custom_call_target="tpu_custom_call" | custom-call | flops 15000000512 | bytes 37748736 | tf_op jit(solution)/shard_map/mid_back/pallas_call | solution.py:514
  331.6 10.3 %weight_grad.5.refs_4_ = bf16[4,4,256,512]{3,2,1,0:T(8,128)(2,1)} custom-call(s32[2]{0:T(128)} %pad_add_fusion.1.turn_ref, bf16[1024,4096]{1,0:T(8,128)(2,1)} %get-tuple-element.57.g_ref.refs_0_, bf16[1024,1024]{1,0:T(8,128)(2,1)} %get-tuple-element.71.refs_1_, bf16[4,4,256,512]{3,2,1,0:T(8,128)(2,1)} %collective-permute-done.8.refs_2_, ...), custom_call_target="tpu_custom_call" | custom-call | flops 4294967296 | bytes 20971520 | tf_op jit(solution)/shard_map/weight_grad/pallas_call | solution.py:698
  341.9 11.1 %weight_grad.6 = bf16[4,4,64,2560]{3,2,1,0:T(8,128)(2,1)} custom-call(s32[3]{0:T(128)} %fusion.31.turn_ref, bf16[1024,1024]{1,0:T(8,128)(2,1)} %get-tuple-element.73.refs_0_, bf16[1024,4096]{1,0:T(8,128)(2,1)} %get-tuple-element.63.du_ref.refs_1_, bf16[1024,1024]{1,0:T(8,128)(2,1)} %pad_maximum_fusion.refs_2_, bf16[1024,1024]{1,0:T(8,128)(2,1)} %get-tuple-element.74.refs_3_, ...), custom_call_target="tpu_custom_call" | custom-call | flops 5368709120 | bytes 20971520 | tf_op jit(solution)/shard_map/weight_grad/pallas_call | solution.py:698
  353.6 4.8 all-to-all-start.4
  363.6 22.6 %attend_back.4 = (bf16[2048,1536]{1,0:T(8,128)(2,1)}, f32[16,128]{1,0:T(8,128)}) custom-call(bf16[2048,1536]{1,0:T(8,128)(2,1)} %project.1.q_ref.k_ref.v_ref, bf16[2048,1536]{1,0:T(8,128)(2,1)} %project.1.q_ref.k_ref.v_ref, bf16[2048,1536]{1,0:T(8,128)(2,1)} %project.1.q_ref.k_ref.v_ref, bf16[2048,512]{1,0:T(8,128)(2,1)} %get-tuple-element.55.om_ref.o_ref, ...), custom_call_target="tpu_custom_call" | custom-call | flops 20999999488 | bytes 16777216 | tf_op jit(solution)/shard_map/attend_back/pallas_call | solution.py:250
  386.2 12.2 %weight_grad.7.refs_2_ = bf16[4,4,64,2688]{3,2,1,0:T(8,128)(2,1)} custom-call(s32[3]{0:T(128)} %fusion.30.turn_ref, bf16[1024,1024]{1,0:T(8,128)(2,1)} %get-tuple-element.73.refs_0_, bf16[1024,4096]{1,0:T(8,128)(2,1)} %get-tuple-element.63.du_ref.refs_1_, bf16[1024,1024]{1,0:T(8,128)(2,1)} %pad_maximum_fusion.refs_2_, ...), custom_call_target="tpu_custom_call" | custom-call | flops 5368709120 | bytes 20971520 | tf_op jit(solution)/shard_map/weight_grad/pallas_call | solution.py:698
  398.3 7.1 %all-to-all-done.4.refs_0_ = bf16[4,4,256,512]{3,2,1,0:T(8,128)(2,1)} async-done(((bf16[4,4,256,512]{3,2,1,0:T(8,128)(2,1)}), bf16[4,4,256,512]{3,2,1,0:T(8,128)(2,1)}, u32[]{:S(2)}, u32[]{:S(2)}) %all-to-all-start.4) | async-done | bytes 4194336 | tf_op jit(solution)/shard_map/all_to_all | solution.py:727
  405.5 6.6 %all-to-all-start.5 = ((bf16[4,4,64,2688]{3,2,1,0:T(8,128)(2,1)}), bf16[4,4,64,2688]{3,2,1,0:T(8,128)(2,1)}, u32[]{:S(2)}, u32[]{:S(2)}) async-start(bf16[4,4,64,2688]{3,2,1,0:T(8,128)(2,1)} %weight_grad.7.refs_2_), calls=%async_computation.5 | async-start | bytes 11010048 | tf_op jit(solution)/shard_map/all_to_all | solution.py:727
  415.1 30.4 %collective-permute-start.10 = (bf16[256,512]{1,0:T(8,128)(2,1)S(1)}, bf16[256,512]{1,0:T(8,128)(2,1)S(1)}, u32[]{:S(2)}, u32[]{:S(2)}) collective-permute-start(bf16[256,512]{1,0:T(8,128)(2,1)S(1)} %get-tuple-element.104), channel_id=1, source_target_pairs={{0,8},{8,16},{16,24},{24,0},{1,9},{9,17},{17,25},{25,1},{2,10},{10... | collective-permute-start | bytes 786440 | tf_op jit(solution)/shard_map/ppermute | solution.py:717
  447.1 22.9 %attend_back.5 = (bf16[2048,1536]{1,0:T(8,128)(2,1)}, f32[16,128]{1,0:T(8,128)}) custom-call(bf16[2048,1536]{1,0:T(8,128)(2,1)} %project.1.q_ref.k_ref.v_ref, bf16[2048,1536]{1,0:T(8,128)(2,1)} %project.1.q_ref.k_ref.v_ref, bf16[2048,1536]{1,0:T(8,128)(2,1)} %project.1.q_ref.k_ref.v_ref, ...), custom_call_target="tpu_custom_call", output_to_operand_aliasing={{0}: (8, {})} | custom-call | flops 20999999488 | bytes 16777216 | tf_op jit(solution)/shard_map/attend_back/pallas_call | solution.py:250
  472.9 22.6 %attend_back.6 = (bf16[2048,1536]{1,0:T(8,128)(2,1)}, f32[16,128]{1,0:T(8,128)}) custom-call(bf16[2048,1536]{1,0:T(8,128)(2,1)} %project.1.q_ref.k_ref.v_ref, bf16[2048,1536]{1,0:T(8,128)(2,1)} %project.1.q_ref.k_ref.v_ref, bf16[2048,1536]{1,0:T(8,128)(2,1)} %project.1.q_ref.k_ref.v_ref, ...), custom_call_target="tpu_custom_call", output_to_operand_aliasing={{0}: (8, {})} | custom-call | flops 20999999488 | bytes 16777216 | tf_op jit(solution)/shard_map/attend_back/pallas_call | solution.py:250
  495.5 9.8 %proj_grad.2.refs_2_.refs_0_ = bf16[4,4,64,1152]{3,2,1,0:T(8,128)(2,1)} custom-call(bf16[4,256,1024]{2,1,0:T(8,128)(2,1)} %tie.17.xm_ref.refs_1_.x_ref, bf16[4,256,1024]{2,1,0:T(8,128)(2,1)} %collective-permute-done.3.xt_ref, bf16[2048,1536]{1,0:T(8,128)(2,1)} %get-tuple-element.80.grad_ref.rest_0_), custom_call_target="tpu_custom_call" | custom-call | flops 100000000 | bytes 65536 | tf_op jit(solution)/shard_map/proj_grad/pallas_call | solution.py:643
  514.7 4.4 all-to-all-start.6
  519.1 22.6 %attend_back.7 = (bf16[2048,1536]{1,0:T(8,128)(2,1)}, f32[16,128]{1,0:T(8,128)}) custom-call(bf16[2048,1536]{1,0:T(8,128)(2,1)} %project.1.q_ref.k_ref.v_ref, bf16[2048,1536]{1,0:T(8,128)(2,1)} %project.1.q_ref.k_ref.v_ref, bf16[2048,1536]{1,0:T(8,128)(2,1)} %project.1.q_ref.k_ref.v_ref, ...), custom_call_target="tpu_custom_call", output_to_operand_aliasing={{0}: (8, {})} | custom-call | flops 20999999488 | bytes 16777216 | tf_op jit(solution)/shard_map/attend_back/pallas_call | solution.py:250
  546.2 7.4 %token_grad.2.refs_1_ = bf16[1024,1024]{1,0:T(8,128)(2,1)} custom-call(s32[1]{0:T(128)} %bitcast.17.chip_ref, bf16[2048,1536]{1,0:T(8,128)(2,1)} %tie.28.grad_ref, bf16[1024,1536]{1,0:T(8,128)(2,1)} %get-tuple-element.52.w_ref), custom_call_target="tpu_custom_call" | custom-call | flops 100000000 | bytes 65536 | tf_op jit(solution)/shard_map/token_grad/pallas_call | solution.py:566
  554.9 6.2 proj_grad.3.refs_2_
  567.1 8.8 %token_grad.3.refs_0_ = bf16[1024,1024]{1,0:T(8,128)(2,1)} custom-call(s32[1]{0:T(128)} %bitcast.17.chip_ref, bf16[2048,1536]{1,0:T(8,128)(2,1)} %tie.28.grad_ref, bf16[1024,1536]{1,0:T(8,128)(2,1)} %get-tuple-element.52.w_ref, f32[1024,1024]{1,0:T(8,128)} %get-tuple-element.84.refs_0_, bf16[1024,1024]{1,0:T(8,128)(2,1)} %copy-done.24, ...), custom_call_target="tpu_custom_call" | custom-call | flops 100000000 | bytes 65536 | tf_op jit(solution)/shard_map/token_grad/pallas_call | solution.py:566
  578.6 5.1 all-to-all-start.7
  592.8 11.6 %collective-permute-done.20.refs_1_ = bf16[64,1664]{1,0:T(8,128)(2,1)S(1)} collective-permute-done((bf16[64,1664]{1,0:T(8,128)(2,1)S(1)}, bf16[64,1664]{1,0:T(8,128)(2,1)S(1)}, u32[]{:S(2)}, u32[]{:S(2)}) %collective-permute-start.20) | collective-permute-done | bytes 213024 | tf_op jit(solution)/shard_map/ppermute | solution.py:717
  (321 shorter events, 107.6 us)
Async XLA Ops:
  7.3 28.3 %all-to-all-start = ((bf16[4,256,1024]{2,1,0:T(8,128)(2,1)}), bf16[4,256,1024]{2,1,0:T(8,128)(2,1)S(1)}, u32[]{:S(2)}, u32[]{:S(2)}) async-start(bf16[4,256,1024]{2,1,0:T(8,128)(2,1)} %param.18), calls=%async_computation | async-start | bytes 4194304 | tf_op jit(solution)/shard_map/all_to_all | solution.py:727
  11.6 214.2 %all-gather.2.cloned.1.call-start = ((), (), s32[]{:S(2)}) async-start(), calls=%async_computation.8 | async-start | bytes 19464192 | tf_op jit(solution)/shard_map/all_gather | solution.py:893
  14.9 16.2 %collective-permute-start = (bf16[32,3200]{1,0:T(8,128)(2,1)}, bf16[32,3200]{1,0:T(8,128)(2,1)S(1)}, u32[]{:S(2)}, u32[]{:S(2)}) collective-permute-start(bf16[32,3200]{1,0:T(8,128)(2,1)} %get-tuple-element.51), channel_id=1, source_target_pairs={{0,8},{8,16},{16,24},{24,0},{1,9},{9,17},{17,25},{25,1},{2,10},{10... | collective-permute-start | bytes 614408 | tf_op jit(solution)/shard_map/ppermute | solution.py:717
  16.5 17.4 %collective-permute-start.1 = (bf16[32,3200]{1,0:T(8,128)(2,1)}, bf16[32,3200]{1,0:T(8,128)(2,1)S(1)}, u32[]{:S(2)}, u32[]{:S(2)}) collective-permute-start(bf16[32,3200]{1,0:T(8,128)(2,1)} %get-tuple-element.51), channel_id=1, source_target_pairs={{0,16},{8,24},{16,0},{24,8},{1,17},{9,25},{17,1},{25,9},{2,18},{10... | collective-permute-start | bytes 614408 | tf_op jit(solution)/shard_map/ppermute | solution.py:717
  17.7 17.8 %collective-permute-start.2 = (bf16[32,3200]{1,0:T(8,128)(2,1)}, bf16[32,3200]{1,0:T(8,128)(2,1)S(1)}, u32[]{:S(2)}, u32[]{:S(2)}) collective-permute-start(bf16[32,3200]{1,0:T(8,128)(2,1)} %get-tuple-element.51), channel_id=1, source_target_pairs={{0,24},{8,0},{16,8},{24,16},{1,25},{9,1},{17,9},{25,17},{2,26},{10... | collective-permute-start | bytes 614408 | tf_op jit(solution)/shard_map/ppermute | solution.py:717
  93.9 9.2 %collective-permute-start.4 = (bf16[16,32,3200]{2,1,0:T(8,128)(2,1)}, bf16[16,32,3200]{2,1,0:T(8,128)(2,1)}, u32[]{:S(2)}, u32[]{:S(2)}) collective-permute-start(bf16[16,32,3200]{2,1,0:T(8,128)(2,1)} %bitcast.8.refs_0_), channel_id=1, source_target_pairs={{0,1},{1,0},{2,3},{3,2},{4,5},{5,4},{6,7},{7,6},{8,9},{9,8},{10,11... | collective-permute-start | bytes 9830408 | tf_op jit(solution)/shard_map/ppermute | solution.py:712
  93.9 17.7 %collective-permute-start.3 = (bf16[4,256,1024]{2,1,0:T(8,128)(2,1)S(1)}, bf16[4,256,1024]{2,1,0:T(8,128)(2,1)}, u32[]{:S(2)}, u32[]{:S(2)}) collective-permute-start(bf16[4,256,1024]{2,1,0:T(8,128)(2,1)S(1)} %copy-done.1), channel_id=1, source_target_pairs={{0,1},{1,0},{2,3},{3,2},{4,5},{5,4},{6,7},{7,6},{8,9},{9,8},{10,11... | collective-permute-start | bytes 6291464 | tf_op jit(solution)/shard_map/ppermute | solution.py:712
  153.2 72.7 %collective-permute-start.5 = (bf16[1024,256]{1,0:T(8,128)(2,1)S(1)}, bf16[1024,256]{1,0:T(8,128)(2,1)}, u32[]{:S(2)}, u32[]{:S(2)}) collective-permute-start(bf16[1024,256]{1,0:T(8,128)(2,1)S(1)} %slice.156), channel_id=1, source_target_pairs={{0,1},{1,0},{2,3},{3,2},{4,5},{5,4},{6,7},{7,6},{8,9},{9,8},{10,11... | collective-permute-start | bytes 1572872 | tf_op jit(solution)/shard_map/ppermute | solution.py:712
  190.6 35.2 %collective-permute-start.6 = (bf16[1024,256]{1,0:T(8,128)(2,1)S(1)}, bf16[1024,256]{1,0:T(8,128)(2,1)}, u32[]{:S(2)}, u32[]{:S(2)}) collective-permute-start(bf16[1024,256]{1,0:T(8,128)(2,1)S(1)} %slice.157), channel_id=1, source_target_pairs={{0,1},{1,0},{2,3},{3,2},{4,5},{5,4},{6,7},{7,6},{8,9},{9,8},{10,11... | collective-permute-start | bytes 1572872 | tf_op jit(solution)/shard_map/ppermute | solution.py:712
  196.4 56.1 %all-to-all-start.2 = ((bf16[4,256,1024]{2,1,0:T(8,128)(2,1)}), bf16[4,256,1024]{2,1,0:T(8,128)(2,1)S(1)}, u32[]{:S(2)}, u32[]{:S(2)}) async-start(bf16[4,256,1024]{2,1,0:T(8,128)(2,1)} %broadcast_add_fusion), calls=%async_computation.2 | async-start | bytes 4194304 | tf_op jit(solution)/shard_map/all_to_all | solution.py:727
  298.2 32.1 %collective-permute-start.8 = (bf16[4,4,256,512]{3,2,1,0:T(8,128)(2,1)}, bf16[4,4,256,512]{3,2,1,0:T(8,128)(2,1)}, u32[]{:S(2)}, u32[]{:S(2)}) collective-permute-start(bf16[4,4,256,512]{3,2,1,0:T(8,128)(2,1)} %weight_grad.4), channel_id=1, source_target_pairs={{0,1},{1,0},{2,3},{3,2},{4,5},{5,4},{6,7},{7,6},{8,9},{9,8},{10,11... | collective-permute-start | bytes 12582920 | tf_op jit(solution)/shard_map/ppermute | solution.py:712
  298.7 31.5 %all-to-all-start.3 = ((bf16[4,256,1024]{2,1,0:T(8,128)(2,1)}), bf16[4,256,1024]{2,1,0:T(8,128)(2,1)S(1)}, u32[]{:S(2)}, u32[]{:S(2)}) async-start(bf16[4,256,1024]{2,1,0:T(8,128)(2,1)} %bitcast.142), calls=%async_computation.3 | async-start | bytes 4194304 | tf_op jit(solution)/shard_map/all_to_all | solution.py:727
  353.0 33.1 %collective-permute-start.9 = (bf16[4,4,64,2560]{3,2,1,0:T(8,128)(2,1)}, bf16[4,4,64,2560]{3,2,1,0:T(8,128)(2,1)}, u32[]{:S(2)}, u32[]{:S(2)}) collective-permute-start(bf16[4,4,64,2560]{3,2,1,0:T(8,128)(2,1)} %weight_grad.6), channel_id=1, source_target_pairs={{0,1},{1,0},{2,3},{3,2},{4,5},{5,4},{6,7},{7,6},{8,9},{9,8},{10,11... | collective-permute-start | bytes 15728648 | tf_op jit(solution)/shard_map/ppermute | solution.py:712
  353.1 9.5 %collective-permute-start.7 = (bf16[1024,512]{1,0:T(8,128)(2,1)S(1)}, bf16[1024,512]{1,0:T(8,128)(2,1)S(1)}, u32[]{:S(2)}, u32[]{:S(2)}) collective-permute-start(bf16[1024,512]{1,0:T(8,128)(2,1)S(1)} %copy-done.48), channel_id=1, source_target_pairs={{0,1},{1,0},{2,3},{3,2},{4,5},{5,4},{6,7},{7,6},{8,9},{9,8},{10,11... | collective-permute-start | bytes 3145736 | tf_op jit(solution)/shard_map/ppermute | solution.py:712
  353.6 51.8 %all-to-all-start.4 = ((bf16[4,4,256,512]{3,2,1,0:T(8,128)(2,1)}), bf16[4,4,256,512]{3,2,1,0:T(8,128)(2,1)}, u32[]{:S(2)}, u32[]{:S(2)}) async-start(bf16[4,4,256,512]{3,2,1,0:T(8,128)(2,1)} %weight_grad.5.refs_4_), calls=%async_computation.4 | async-start | bytes 8388608 | tf_op jit(solution)/shard_map/all_to_all | solution.py:727
  405.5 99.9 %all-to-all-start.5 = ((bf16[4,4,64,2688]{3,2,1,0:T(8,128)(2,1)}), bf16[4,4,64,2688]{3,2,1,0:T(8,128)(2,1)}, u32[]{:S(2)}, u32[]{:S(2)}) async-start(bf16[4,4,64,2688]{3,2,1,0:T(8,128)(2,1)} %weight_grad.7.refs_2_), calls=%async_computation.5 | async-start | bytes 11010048 | tf_op jit(solution)/shard_map/all_to_all | solution.py:727
  415.1 54.8 %collective-permute-start.10 = (bf16[256,512]{1,0:T(8,128)(2,1)S(1)}, bf16[256,512]{1,0:T(8,128)(2,1)S(1)}, u32[]{:S(2)}, u32[]{:S(2)}) collective-permute-start(bf16[256,512]{1,0:T(8,128)(2,1)S(1)} %get-tuple-element.104), channel_id=1, source_target_pairs={{0,8},{8,16},{16,24},{24,0},{1,9},{9,17},{17,25},{25,1},{2,10},{10... | collective-permute-start | bytes 786440 | tf_op jit(solution)/shard_map/ppermute | solution.py:717
  445.5 24.4 %collective-permute-start.11 = (bf16[256,512]{1,0:T(8,128)(2,1)S(1)}, bf16[256,512]{1,0:T(8,128)(2,1)S(1)}, u32[]{:S(2)}, u32[]{:S(2)}) collective-permute-start(bf16[256,512]{1,0:T(8,128)(2,1)S(1)} %get-tuple-element.102), channel_id=1, source_target_pairs={{0,16},{8,24},{16,0},{24,8},{1,17},{9,25},{17,1},{25,9},{2,18},{10... | collective-permute-start | bytes 786440 | tf_op jit(solution)/shard_map/ppermute | solution.py:717
  445.5 24.5 %collective-permute-start.12 = (bf16[256,512]{1,0:T(8,128)(2,1)S(1)}, bf16[256,512]{1,0:T(8,128)(2,1)S(1)}, u32[]{:S(2)}, u32[]{:S(2)}) collective-permute-start(bf16[256,512]{1,0:T(8,128)(2,1)S(1)} %get-tuple-element.103), channel_id=1, source_target_pairs={{0,24},{8,0},{16,8},{24,16},{1,25},{9,1},{17,9},{25,17},{2,26},{10... | collective-permute-start | bytes 786440 | tf_op jit(solution)/shard_map/ppermute | solution.py:717
  510.4 32.9 %collective-permute-start.15 = (bf16[64,2688]{1,0:T(8,128)(2,1)}, bf16[64,2688]{1,0:T(8,128)(2,1)S(1)}, u32[]{:S(2)}, u32[]{:S(2)}) collective-permute-start(bf16[64,2688]{1,0:T(8,128)(2,1)} %get-tuple-element.96), channel_id=1, source_target_pairs={{0,24},{8,0},{16,8},{24,16},{1,25},{9,1},{17,9},{25,17},{2,26},{10... | collective-permute-start | bytes 1032200 | tf_op jit(solution)/shard_map/ppermute | solution.py:717
  513.2 28.5 %collective-permute-start.14 = (bf16[64,2688]{1,0:T(8,128)(2,1)}, bf16[64,2688]{1,0:T(8,128)(2,1)S(1)}, u32[]{:S(2)}, u32[]{:S(2)}) collective-permute-start(bf16[64,2688]{1,0:T(8,128)(2,1)} %get-tuple-element.97), channel_id=1, source_target_pairs={{0,16},{8,24},{16,0},{24,8},{1,17},{9,25},{17,1},{25,9},{2,18},{10... | collective-permute-start | bytes 1032200 | tf_op jit(solution)/shard_map/ppermute | solution.py:717
  513.2 29.3 %collective-permute-start.13 = (bf16[64,2688]{1,0:T(8,128)(2,1)}, bf16[64,2688]{1,0:T(8,128)(2,1)S(1)}, u32[]{:S(2)}, u32[]{:S(2)}) collective-permute-start(bf16[64,2688]{1,0:T(8,128)(2,1)} %get-tuple-element.98), channel_id=1, source_target_pairs={{0,8},{8,16},{16,24},{24,0},{1,9},{9,17},{17,25},{25,1},{2,10},{10... | collective-permute-start | bytes 1032200 | tf_op jit(solution)/shard_map/ppermute | solution.py:717
  514.7 29.4 %all-to-all-start.6 = ((bf16[4,4,64,1152]{3,2,1,0:T(8,128)(2,1)}), bf16[4,4,64,1152]{3,2,1,0:T(8,128)(2,1)S(1)}, u32[]{:S(2)}, u32[]{:S(2)}) async-start(bf16[4,4,64,1152]{3,2,1,0:T(8,128)(2,1)} %tie.23), calls=%async_computation.6 | async-start | bytes 4718592 | tf_op jit(solution)/shard_map/all_to_all | solution.py:727
  553.7 12.2 %collective-permute-start.16 = (bf16[1024,1024]{1,0:T(8,128)(2,1)}, bf16[1024,1024]{1,0:T(8,128)(2,1)S(1)}, u32[]{:S(2)}, u32[]{:S(2)}) collective-permute-start(bf16[1024,1024]{1,0:T(8,128)(2,1)} %token_grad.2.refs_1_), channel_id=1, source_target_pairs={{0,1},{1,0},{2,3},{3,2},{4,5},{5,4},{6,7},{7,6},{8,9},{9,8},{10,11... | collective-permute-start | bytes 6291464 | tf_op jit(solution)/shard_map/ppermute | solution.py:712
  562.3 13.7 %collective-permute-start.17 = (bf16[4,64,512]{2,1,0:T(8,128)(2,1)S(1)}, bf16[4,64,512]{2,1,0:T(8,128)(2,1)S(1)}, u32[]{:S(2)}, u32[]{:S(2)}) collective-permute-start(bf16[4,64,512]{2,1,0:T(8,128)(2,1)S(1)} %get-tuple-element.101), channel_id=1, source_target_pairs={{0,2},{1,3},{2,0},{3,1},{4,6},{5,7},{6,4},{7,5},{8,10},{9,11},{10,... | collective-permute-start | bytes 786440 | tf_op jit(solution)/shard_map/ppermute | solution.py:712
  563.2 14.1 %collective-permute-start.18 = (bf16[4,64,512]{2,1,0:T(8,128)(2,1)S(1)}, bf16[4,64,512]{2,1,0:T(8,128)(2,1)S(1)}, u32[]{:S(2)}, u32[]{:S(2)}) collective-permute-start(bf16[4,64,512]{2,1,0:T(8,128)(2,1)S(1)} %get-tuple-element.100), channel_id=1, source_target_pairs={{0,4},{1,5},{2,6},{3,7},{4,0},{5,1},{6,2},{7,3},{8,12},{9,13},{10,... | collective-permute-start | bytes 786440 | tf_op jit(solution)/shard_map/ppermute | solution.py:712
  563.7 13.5 %collective-permute-start.19 = (bf16[4,64,512]{2,1,0:T(8,128)(2,1)S(1)}, bf16[4,64,512]{2,1,0:T(8,128)(2,1)S(1)}, u32[]{:S(2)}, u32[]{:S(2)}) collective-permute-start(bf16[4,64,512]{2,1,0:T(8,128)(2,1)S(1)} %get-tuple-element.99), channel_id=1, source_target_pairs={{0,6},{1,7},{2,4},{3,5},{4,2},{5,3},{6,0},{7,1},{8,14},{9,15},{10,... | collective-permute-start | bytes 786440 | tf_op jit(solution)/shard_map/ppermute | solution.py:712
  578.6 32.1 %all-to-all-start.7 = ((bf16[4,256,1024]{2,1,0:T(8,128)(2,1)}), bf16[4,256,1024]{2,1,0:T(8,128)(2,1)S(1)}, u32[]{:S(2)}, u32[]{:S(2)}) async-start(bf16[4,256,1024]{2,1,0:T(8,128)(2,1)} %bitcast.138), calls=%async_computation.7 | async-start | bytes 4194304 | tf_op jit(solution)/shard_map/all_to_all | solution.py:727
  584.5 29.0 %collective-permute-start.24 = (bf16[128,512]{1,0:T(8,128)(2,1)}, bf16[128,512]{1,0:T(8,128)(2,1)}, u32[]{:S(2)}, u32[]{:S(2)}) collective-permute-start(bf16[128,512]{1,0:T(8,128)(2,1)} %dynamic-slice_bitcast_fusion.9), channel_id=1, source_target_pairs={{0,1},{1,0},{2,3},{3,2},{4,5},{5,4},{6,7},{7,6},{8,9},{9,8},{10,11... | collective-permute-start | bytes 393224 | tf_op jit(solution)/shard_map/ppermute | solution.py:712
  588.0 16.4 %collective-permute-start.20 = (bf16[64,1664]{1,0:T(8,128)(2,1)S(1)}, bf16[64,1664]{1,0:T(8,128)(2,1)S(1)}, u32[]{:S(2)}, u32[]{:S(2)}) collective-permute-start(bf16[64,1664]{1,0:T(8,128)(2,1)S(1)} %get-tuple-element.106), channel_id=1, source_target_pairs={{0,8},{8,16},{16,24},{24,0},{1,9},{9,17},{17,25},{25,1},{2,10},{10... | collective-permute-start | bytes 638984 | tf_op jit(solution)/shard_map/ppermute | solution.py:717
  589.8 18.9 %collective-permute-start.21 = (bf16[64,1664]{1,0:T(8,128)(2,1)S(1)}, bf16[64,1664]{1,0:T(8,128)(2,1)S(1)}, u32[]{:S(2)}, u32[]{:S(2)}) collective-permute-start(bf16[64,1664]{1,0:T(8,128)(2,1)S(1)} %get-tuple-element.105), channel_id=1, source_target_pairs={{0,16},{8,24},{16,0},{24,8},{1,17},{9,25},{17,1},{25,9},{2,18},{10... | collective-permute-start | bytes 638984 | tf_op jit(solution)/shard_map/ppermute | solution.py:717
  591.4 19.4 %collective-permute-start.22 = (bf16[64,1664]{1,0:T(8,128)(2,1)S(1)}, bf16[64,1664]{1,0:T(8,128)(2,1)}, u32[]{:S(2)}, u32[]{:S(2)}) collective-permute-start(bf16[64,1664]{1,0:T(8,128)(2,1)S(1)} %get-tuple-element.107), channel_id=1, source_target_pairs={{0,24},{8,0},{16,8},{24,16},{1,25},{9,1},{17,9},{25,17},{2,26},{10... | collective-permute-start | bytes 638984 | tf_op jit(solution)/shard_map/ppermute | solution.py:717
  (59 other events, 294.8 us)
Sparse Core Ops, SparseCore 0:
  37.7 137.5 all-gather.1
